TPU v7x, 32 devices: a whole 2x2x4 slice. The times are simulated.
32 devices in a mesh: ctx: 16 (over z, y, core), tp: 2 (over x).
Axes of the slice: x: 2, y: 2, z: 4, core: 2. Of those that a mesh axis runs over, the one named last changes fastest.
Arguments:
- tokens: bfloat16 [4, 2048, 1536], P(None, 'ctx'), may hold values from -6 to 6
- output_cotangent: bfloat16 [4, 2048, 1536], P(None, 'ctx'), may hold values from -6 to 6
- segment_ids: int32 [4, 2048], replicated, may hold values from 0 to 255, as said below
- variant: int32 [4], replicated, may hold values from 0 to 7
- attn_gain: float32 [1536], replicated, may hold values from 0.1 to 1.9
- ffn_gain: float32 [1536], replicated, may hold values from 0.1 to 1.9
- q_gain: float32 [64], replicated, may hold values from 0.1 to 1.9
- k_gain: float32 [64], replicated, may hold values from 0.1 to 1.9
- query_matrix: bfloat16 [1536, 1536], P(None, 'tp'), may hold values from -0.15625 to 0.15625
- key_matrix: bfloat16 [1536, 512], P(None, 'tp'), may hold values from -0.15625 to 0.15625
- value_matrix: bfloat16 [1536, 512], P(None, 'tp'), may hold values from -0.15625 to 0.15625
- output_matrix: bfloat16 [1536, 1536], P('tp'), may hold values from -1.25 to 1.25
- gate_matrix: bfloat16 [1536, 6912], P(None, 'tp'), may hold values from -0.15625 to 0.15625
- up_matrix: bfloat16 [1536, 6912], P(None, 'tp'), may hold values from -0.15625 to 0.15625
- down_matrix: bfloat16 [6912, 1536], P('tp'), may hold values from -0.078125 to 0.078125
- query_input_factor: bfloat16 [128, 1536], replicated, may hold values from -0.15625 to 0.15625
- query_output_factor: bfloat16 [128, 1536], P(None, 'tp'), may hold values from -0.75 to 0.75
- key_input_factor: bfloat16 [128, 1536], replicated, may hold values from -0.15625 to 0.15625
- key_output_factor: bfloat16 [128, 512], P(None, 'tp'), may hold values from -0.75 to 0.75
- value_input_factor: bfloat16 [128, 1536], replicated, may hold values from -0.15625 to 0.15625
- value_output_factor: bfloat16 [128, 512], P(None, 'tp'), may hold values from -0.75 to 0.75
- output_input_factor: bfloat16 [128, 1536], P(None, 'tp'), may hold values from -0.15625 to 0.15625
- output_output_factor: bfloat16 [128, 1536], replicated, may hold values from -3 to 3
- gate_input_factor: bfloat16 [128, 1536], replicated, may hold values from -0.15625 to 0.15625
- gate_output_factor: bfloat16 [128, 6912], P(None, 'tp'), may hold values from -0.75 to 0.75
- up_input_factor: bfloat16 [128, 1536], replicated, may hold values from -0.15625 to 0.15625
- up_output_factor: bfloat16 [128, 6912], P(None, 'tp'), may hold values from -0.75 to 0.75
- down_input_factor: bfloat16 [128, 6912], P(None, 'tp'), may hold values from -0.078125 to 0.078125
- down_output_factor: bfloat16 [128, 1536], replicated, may hold values from -0.75 to 0.75
Outputs:
- block_result: bfloat16 [4, 2048, 1536], P(None, 'ctx')
- input_grad: bfloat16 [4, 2048, 1536], P(None, 'ctx')
- grad_a_query: float32 [128, 1536], P('ctx')
- grad_b_query: float32 [128, 1536], P('ctx', 'tp')
- grad_a_key: float32 [128, 1536], P('ctx')
- grad_b_key: float32 [128, 512], P('ctx', 'tp')
- grad_a_value: float32 [128, 1536], P('ctx')
- grad_b_value: float32 [128, 512], P('ctx', 'tp')
- grad_a_out: float32 [128, 1536], P('ctx', 'tp')
- grad_b_out: float32 [128, 1536], P('ctx')
- grad_a_gate: float32 [128, 1536], P('ctx')
- grad_b_gate: float32 [128, 6912], P('ctx', 'tp')
- grad_a_up: float32 [128, 1536], P('ctx')
- grad_b_up: float32 [128, 6912], P('ctx', 'tp')
- grad_a_down: float32 [128, 6912], P('ctx', 'tp')
- grad_b_down: float32 [128, 1536], P('ctx')
Inputs may be any that keep to these rules, and one draw needn't show every extreme that they name: `segment_ids`: in each sequence the ids start at 0, never fall, and rise by at most one from a position to the next; in every draw at least one sequence is a single document, and some sequence reaches the largest id 2048 // 8 - 1.
All inputs are finite; a program needn't handle non-finite values.
Results may differ from a plain program's by a relative error of at most 0.025.
Values may be sent and summed in bfloat16 or wider, within the bound.
A program may use at most 320 MiB of HBM per device.

v0:
```python
import jax
import jax.numpy as jnp
from jax import lax
from jax.sharding import PartitionSpec as P

HEAD_DIM = 64
RANK = 16


EPSILON = 1e-05
THETA_BASE = 1000000.0
ADAPTER_SCALE = 2.0
MASKED_SCORE = -1e30


def norm_rows(values, gains):
    return values * lax.rsqrt(jnp.mean(values * values, axis=-1, keepdims=True) + EPSILON) * gains


def rotate(values, positions):
    halfway = values.shape[-1] // 2
    frequencies = THETA_BASE ** (-jnp.arange(halfway, dtype=jnp.float32) * 2.0 / values.shape[-1])
    angles = positions.astype(jnp.float32)[:, None] * frequencies[None, :]
    cosine_table = jnp.cos(angles)[:, None, :]
    sine_table = jnp.sin(angles)[:, None, :]
    leading = values[..., :halfway]
    trailing = values[..., halfway:]
    return jnp.concatenate(
        [
            leading * cosine_table - trailing * sine_table,
            trailing * cosine_table + leading * sine_table,
        ],
        axis=-1,
    )


def head_prepare(values, gains, positions):
    sequences, row_count, columns = values.shape
    shaped = values.reshape(sequences, row_count, columns // HEAD_DIM, HEAD_DIM)
    return rotate(norm_rows(shaped, gains), positions)


def rounded(values):
    return lax.optimization_barrier(values.astype(jnp.bfloat16)).astype(jnp.float32)


def apply_projection(input_rows, weight_tuple):
    return jnp.einsum("cgt,tr->cgr", input_rows, weight_tuple, preferred_element_type=jnp.float32)


def projection_backward(gradient_tuple, weight_tuple):
    return jnp.einsum(
        "jwy,hy->jwh", gradient_tuple, weight_tuple, preferred_element_type=jnp.float32
    )


def lowrank_reduce(input_rows, lowrank_factor):
    return jnp.einsum("pou,hu->poh", input_rows, lowrank_factor, preferred_element_type=jnp.float32)


def lowrank_expand(hidden_rows, lowrank_factor):
    return ADAPTER_SCALE * jnp.einsum(
        "slr,re->sle", hidden_rows, lowrank_factor, preferred_element_type=jnp.float32
    )


def lowrank_hidden_gradient(gradient_tuple, lowrank_factor):
    return ADAPTER_SCALE * jnp.einsum(
        "sle,re->slr", gradient_tuple, lowrank_factor, preferred_element_type=jnp.float32
    )


def lowrank_input_gradient(hidden_gradient_list, lowrank_factor):
    return jnp.einsum(
        "cvg,gx->cvx", hidden_gradient_list, lowrank_factor, preferred_element_type=jnp.float32
    )


def factor_grad(hidden_rows, gradient_tuple):
    return jnp.einsum(
        "slr,sle->re", hidden_rows, gradient_tuple, preferred_element_type=jnp.float32
    )


def key_step(block_rows):
    return 4 * block_rows


def pair_scores(query_block, key_block, query_segs, key_segs, query_pos, key_pos):
    scaled = jnp.einsum(
        "sqkgd,snkd->skgqn", query_block, key_block, preferred_element_type=jnp.float32
    ) * query_block.shape[-1] ** (-0.5)
    allowed = (query_segs[:, :, None] == key_segs[:, None, :]) & (
        query_pos[None, :, None] >= key_pos[None, None, :]
    )
    return (scaled, allowed[:, None, None, :, :])


def local(
    tokens,
    output_cotangent,
    segment_ids,
    variant,
    attn_gain,
    ffn_gain,
    q_gain,
    k_gain,
    query_matrix,
    key_matrix,
    value_matrix,
    output_matrix,
    gate_matrix,
    up_matrix,
    down_matrix,
    query_input_factor,
    query_output_factor,
    key_input_factor,
    key_output_factor,
    value_input_factor,
    value_output_factor,
    output_input_factor,
    output_output_factor,
    gate_input_factor,
    gate_output_factor,
    up_input_factor,
    up_output_factor,
    down_input_factor,
    down_output_factor,
):
    sequences, rows_here, model_width = tokens.shape
    length = rows_here * lax.axis_size("ctx")
    heads_here = query_matrix.shape[1] // HEAD_DIM
    key_heads = key_matrix.shape[1] // HEAD_DIM
    group_size = heads_here // key_heads
    key_width = key_heads * HEAD_DIM
    stacked = query_input_factor.shape[0]
    first_row = lax.axis_index("ctx") * rows_here
    own_end = first_row + rows_here
    positions = first_row + jnp.arange(rows_here, dtype=jnp.int32)
    own_segs = lax.dynamic_slice_in_dim(segment_ids, first_row, rows_here, 1)
    pick_variant = (
        (jnp.arange(stacked, dtype=jnp.int32) // RANK)[None, :] == variant[:, None]
    ).astype(jnp.float32)[:, None, :]
    input_rows = tokens.astype(jnp.float32)
    first_normed = norm_rows(input_rows, attn_gain).astype(jnp.bfloat16)
    query_hidden = (lowrank_reduce(first_normed, query_input_factor) * pick_variant).astype(
        jnp.bfloat16
    )
    key_hidden = (lowrank_reduce(first_normed, key_input_factor) * pick_variant).astype(
        jnp.bfloat16
    )
    value_hidden = (lowrank_reduce(first_normed, value_input_factor) * pick_variant).astype(
        jnp.bfloat16
    )
    query_before = apply_projection(first_normed, query_matrix) + lowrank_expand(
        query_hidden, query_output_factor
    )
    key_before = apply_projection(first_normed, key_matrix) + lowrank_expand(
        key_hidden, key_output_factor
    )
    value_before = apply_projection(first_normed, value_matrix) + lowrank_expand(
        value_hidden, value_output_factor
    )
    query_block = (
        head_prepare(query_before, q_gain, positions)
        .astype(jnp.bfloat16)
        .reshape(sequences, rows_here, key_heads, group_size, HEAD_DIM)
    )
    keys_low = (
        head_prepare(key_before, k_gain, positions)
        .astype(jnp.bfloat16)
        .reshape(sequences, rows_here, key_width)
    )
    values_low = value_before.astype(jnp.bfloat16)
    stat_shape = (sequences, key_heads, group_size, rows_here)
    start_state = (
        jnp.full(stat_shape, MASKED_SCORE, jnp.float32),
        jnp.zeros(stat_shape, jnp.float32),
        jnp.zeros(stat_shape + (HEAD_DIM,), jnp.float32),
    )
    keys_part = lax.all_gather(keys_low, "ctx", axis=1, tiled=True)
    values_part = lax.all_gather(values_low, "ctx", axis=1, tiled=True)
    attend_block_keys = key_step(rows_here)
    block_total = keys_part.shape[1] // attend_block_keys
    needed = jnp.clip((own_end + attend_block_keys - 1) // attend_block_keys, 0, block_total)

    def one_step(step_index, state):
        highest, totals, accumulated = state
        offset = step_index * attend_block_keys
        key_block = lax.dynamic_slice_in_dim(keys_part, offset, attend_block_keys, 1).reshape(
            sequences, attend_block_keys, key_heads, HEAD_DIM
        )
        value_block = lax.dynamic_slice_in_dim(values_part, offset, attend_block_keys, 1).reshape(
            sequences, attend_block_keys, key_heads, HEAD_DIM
        )
        key_segs = lax.dynamic_slice_in_dim(segment_ids, offset, attend_block_keys, 1)
        key_pos = offset + jnp.arange(attend_block_keys, dtype=jnp.int32)
        scaled, allowed = pair_scores(
            query_block, key_block, own_segs, key_segs, positions, key_pos
        )
        masked = jnp.where(allowed, scaled, MASKED_SCORE)
        new_high = jnp.maximum(highest, jnp.max(masked, axis=-1))
        weights_now = jnp.where(allowed, jnp.exp(masked - new_high[..., None]), 0.0)
        fading = jnp.exp(highest - new_high)
        totals = totals * fading + jnp.sum(weights_now, axis=-1)
        accumulated = accumulated * fading[..., None] + jnp.einsum(
            "skgqn,snkd->skgqd",
            weights_now.astype(jnp.bfloat16),
            value_block,
            preferred_element_type=jnp.float32,
        )
        return (new_high, totals, accumulated)

    highest, totals, accumulated = lax.fori_loop(0, needed, one_step, start_state)
    attention = accumulated / totals[..., None]
    log_sums = highest + jnp.log(totals)
    attention_lowrank = (
        attention.transpose(0, 3, 1, 2, 4)
        .reshape(sequences, rows_here, heads_here * HEAD_DIM)
        .astype(jnp.bfloat16)
    )
    part_out = apply_projection(attention_lowrank, output_matrix)
    hidden_partial = lowrank_reduce(attention_lowrank, output_input_factor)
    output_total, sum_hidden = (
        lax.psum(part_out.astype(jnp.bfloat16), "tp").astype(jnp.float32),
        lax.psum(hidden_partial.astype(jnp.bfloat16), "tp").astype(jnp.float32),
    )
    output_hidden = (sum_hidden * pick_variant).astype(jnp.bfloat16)
    residual_middle = (
        input_rows + output_total + lowrank_expand(output_hidden, output_output_factor)
    )
    second_normed = norm_rows(residual_middle, ffn_gain).astype(jnp.bfloat16)
    gate_hidden = (lowrank_reduce(second_normed, gate_input_factor) * pick_variant).astype(
        jnp.bfloat16
    )
    up_hidden = (lowrank_reduce(second_normed, up_input_factor) * pick_variant).astype(jnp.bfloat16)
    gate_before = apply_projection(second_normed, gate_matrix) + lowrank_expand(
        gate_hidden, gate_output_factor
    )
    up_before = apply_projection(second_normed, up_matrix) + lowrank_expand(
        up_hidden, up_output_factor
    )
    sigmoid_gate = 1.0 / (1.0 + jnp.exp(-gate_before))
    gated_hidden = (gate_before / (1.0 + jnp.exp(-gate_before)) * up_before).astype(jnp.bfloat16)
    part_down = apply_projection(gated_hidden, down_matrix)
    lower_partial = lowrank_reduce(gated_hidden, down_input_factor)
    down_total, sum_lower = (
        lax.psum(part_down.astype(jnp.bfloat16), "tp").astype(jnp.float32),
        lax.psum(lower_partial.astype(jnp.bfloat16), "tp").astype(jnp.float32),
    )
    down_hidden = (sum_lower * pick_variant).astype(jnp.bfloat16)
    block_result = (
        residual_middle + down_total + lowrank_expand(down_hidden, down_output_factor)
    ).astype(jnp.bfloat16)
    down_hidden_cotangent = (
        lowrank_hidden_gradient(output_cotangent, down_output_factor) * pick_variant
    ).astype(jnp.bfloat16)
    grad_b_down = ADAPTER_SCALE * factor_grad(down_hidden, output_cotangent)
    grad_a_down = factor_grad(down_hidden_cotangent, gated_hidden)
    hidden_cotangent = projection_backward(output_cotangent, down_matrix) + lowrank_input_gradient(
        down_hidden_cotangent, down_input_factor
    )
    gate_cotangent = (
        hidden_cotangent * up_before * sigmoid_gate * (1.0 + gate_before * (1.0 - sigmoid_gate))
    ).astype(jnp.bfloat16)
    up_cotangent = (hidden_cotangent * gate_before * sigmoid_gate).astype(jnp.bfloat16)
    grad_b_gate = ADAPTER_SCALE * factor_grad(gate_hidden, gate_cotangent)
    grad_b_up = ADAPTER_SCALE * factor_grad(up_hidden, up_cotangent)
    feedforward_partial = projection_backward(gate_cotangent, gate_matrix) + projection_backward(
        up_cotangent, up_matrix
    )
    feedforward_total, sum_dh_gate, sum_dh_up = (
        lax.psum(feedforward_partial.astype(jnp.bfloat16), "tp").astype(jnp.float32),
        lax.psum(
            lowrank_hidden_gradient(gate_cotangent, gate_output_factor).astype(jnp.bfloat16), "tp"
        ).astype(jnp.float32),
        lax.psum(
            lowrank_hidden_gradient(up_cotangent, up_output_factor).astype(jnp.bfloat16), "tp"
        ).astype(jnp.float32),
    )
    gate_hidden_cotangent = (sum_dh_gate * pick_variant).astype(jnp.bfloat16)
    up_hidden_cotangent = (sum_dh_up * pick_variant).astype(jnp.bfloat16)
    grad_a_gate = factor_grad(gate_hidden_cotangent, second_normed)
    grad_a_up = factor_grad(up_hidden_cotangent, second_normed)
    second_normed_cotangent = (
        feedforward_total
        + lowrank_input_gradient(gate_hidden_cotangent, gate_input_factor)
        + lowrank_input_gradient(up_hidden_cotangent, up_input_factor)
    )
    norm_two_back = jax.vjp(lambda values: norm_rows(values, ffn_gain), residual_middle)[1]
    d_middle = output_cotangent.astype(jnp.float32) + norm_two_back(second_normed_cotangent)[0]
    branch_cotangent = d_middle.astype(jnp.bfloat16)
    output_hidden_cotangent = (
        lowrank_hidden_gradient(branch_cotangent, output_output_factor) * pick_variant
    ).astype(jnp.bfloat16)
    grad_b_out = ADAPTER_SCALE * factor_grad(output_hidden, branch_cotangent)
    grad_a_out = factor_grad(output_hidden_cotangent, attention_lowrank)
    attention_cotangent = (
        projection_backward(branch_cotangent, output_matrix)
        + lowrank_input_gradient(output_hidden_cotangent, output_input_factor)
    ).astype(jnp.bfloat16)
    grad_block = attention_cotangent.reshape(sequences, rows_here, key_heads, group_size, HEAD_DIM)
    deltas = jnp.sum(grad_block.astype(jnp.float32).transpose(0, 2, 3, 1, 4) * attention, axis=-1)
    keys_whole, values_whole = (
        lax.all_gather(keys_low, "ctx", axis=1, tiled=True),
        lax.all_gather(values_low, "ctx", axis=1, tiled=True),
    )
    block_keys = key_step(rows_here)
    needed_blocks = (own_end + block_keys - 1) // block_keys
    scale_factor = HEAD_DIM ** (-0.5)
    dq_start = jnp.zeros((sequences, rows_here, key_heads, group_size, HEAD_DIM), jnp.float32)

    def block_terms(step_index):
        offset = step_index * block_keys
        key_block = lax.dynamic_slice_in_dim(keys_whole, offset, block_keys, 1).reshape(
            sequences, block_keys, key_heads, HEAD_DIM
        )
        value_block = lax.dynamic_slice_in_dim(values_whole, offset, block_keys, 1).reshape(
            sequences, block_keys, key_heads, HEAD_DIM
        )
        key_segs = lax.dynamic_slice_in_dim(segment_ids, offset, block_keys, 1)
        key_pos = offset + jnp.arange(block_keys, dtype=jnp.int32)
        scaled, allowed = pair_scores(
            query_block, key_block, own_segs, key_segs, positions, key_pos
        )
        probs_full = jnp.where(
            allowed, jnp.exp(jnp.where(allowed, scaled - log_sums[..., None], MASKED_SCORE)), 0.0
        )
        d_probs = jnp.einsum(
            "sqkgd,snkd->skgqn", grad_block, value_block, preferred_element_type=jnp.float32
        )
        d_scores = (probs_full * (d_probs - deltas[..., None])).astype(jnp.bfloat16)
        dq_part = (
            jnp.einsum("skgqn,snkd->sqkgd", d_scores, key_block, preferred_element_type=jnp.float32)
            * scale_factor
        )
        return (dq_part, d_scores, probs_full)

    def dense_step(step_index, state):
        dq_sum, key_terms = state
        dq_part, d_scores, probs_full = block_terms(step_index)
        d_keys = (
            jnp.einsum(
                "skgqn,sqkgd->nskd", d_scores, query_block, preferred_element_type=jnp.float32
            )
            * scale_factor
        )
        d_values = jnp.einsum(
            "skgqn,sqkgd->nskd",
            probs_full.astype(jnp.bfloat16),
            grad_block,
            preferred_element_type=jnp.float32,
        )
        joined = jnp.concatenate(
            [
                d_keys.reshape(block_keys, sequences, key_width),
                d_values.reshape(block_keys, sequences, key_width),
            ],
            axis=-1,
        )
        key_terms = lax.dynamic_update_slice_in_dim(key_terms, joined, step_index * block_keys, 0)
        return (dq_sum + dq_part, key_terms)

    terms_start = jnp.zeros((length, sequences, 2 * key_width), jnp.float32)
    dq_sum, key_terms = lax.fori_loop(0, needed_blocks, dense_step, (dq_start, terms_start))
    own_grads = lax.psum_scatter(key_terms, "ctx", scatter_dimension=0, tiled=True).transpose(
        1, 0, 2
    )
    d_keys_own = rounded(own_grads[..., :key_width]).reshape(
        sequences, rows_here, key_heads, HEAD_DIM
    )
    value_prior_cotangent = own_grads[..., key_width:].astype(jnp.bfloat16)
    d_queries = rounded(dq_sum).reshape(sequences, rows_here, heads_here, HEAD_DIM)
    query_back = jax.vjp(lambda values: head_prepare(values, q_gain, positions), query_before)[1]
    key_back = jax.vjp(lambda values: head_prepare(values, k_gain, positions), key_before)[1]
    query_prior_cotangent = query_back(d_queries)[0].astype(jnp.bfloat16)
    key_prior_cotangent = key_back(d_keys_own)[0].astype(jnp.bfloat16)
    grad_b_query = ADAPTER_SCALE * factor_grad(query_hidden, query_prior_cotangent)
    grad_b_key = ADAPTER_SCALE * factor_grad(key_hidden, key_prior_cotangent)
    grad_b_value = ADAPTER_SCALE * factor_grad(value_hidden, value_prior_cotangent)
    part_attn = (
        projection_backward(query_prior_cotangent, query_matrix)
        + projection_backward(key_prior_cotangent, key_matrix)
        + projection_backward(value_prior_cotangent, value_matrix)
    )
    sum_attn, sum_dh_query, sum_dh_key, sum_dh_value = (
        lax.psum(part_attn.astype(jnp.bfloat16), "tp").astype(jnp.float32),
        lax.psum(
            lowrank_hidden_gradient(query_prior_cotangent, query_output_factor).astype(
                jnp.bfloat16
            ),
            "tp",
        ).astype(jnp.float32),
        lax.psum(
            lowrank_hidden_gradient(key_prior_cotangent, key_output_factor).astype(jnp.bfloat16),
            "tp",
        ).astype(jnp.float32),
        lax.psum(
            lowrank_hidden_gradient(value_prior_cotangent, value_output_factor).astype(
                jnp.bfloat16
            ),
            "tp",
        ).astype(jnp.float32),
    )
    query_hidden_cotangent = (sum_dh_query * pick_variant).astype(jnp.bfloat16)
    key_hidden_cotangent = (sum_dh_key * pick_variant).astype(jnp.bfloat16)
    value_hidden_cotangent = (sum_dh_value * pick_variant).astype(jnp.bfloat16)
    grad_a_query = factor_grad(query_hidden_cotangent, first_normed)
    grad_a_key = factor_grad(key_hidden_cotangent, first_normed)
    grad_a_value = factor_grad(value_hidden_cotangent, first_normed)
    d_normed_one = (
        sum_attn
        + lowrank_input_gradient(query_hidden_cotangent, query_input_factor)
        + lowrank_input_gradient(key_hidden_cotangent, key_input_factor)
        + lowrank_input_gradient(value_hidden_cotangent, value_input_factor)
    )
    norm_one_back = jax.vjp(lambda values: norm_rows(values, attn_gain), input_rows)[1]
    input_grad = (d_middle + norm_one_back(d_normed_one)[0]).astype(jnp.bfloat16)
    reduced = (
        lax.psum_scatter(grad_a_query, "ctx", scatter_dimension=0, tiled=True),
        lax.psum_scatter(grad_b_query, "ctx", scatter_dimension=0, tiled=True),
        lax.psum_scatter(grad_a_key, "ctx", scatter_dimension=0, tiled=True),
        lax.psum_scatter(grad_b_key, "ctx", scatter_dimension=0, tiled=True),
        lax.psum_scatter(grad_a_value, "ctx", scatter_dimension=0, tiled=True),
        lax.psum_scatter(grad_b_value, "ctx", scatter_dimension=0, tiled=True),
        lax.psum_scatter(grad_a_out, "ctx", scatter_dimension=0, tiled=True),
        lax.psum_scatter(grad_b_out, "ctx", scatter_dimension=0, tiled=True),
        lax.psum_scatter(grad_a_gate, "ctx", scatter_dimension=0, tiled=True),
        lax.psum_scatter(grad_b_gate, "ctx", scatter_dimension=0, tiled=True),
        lax.psum_scatter(grad_a_up, "ctx", scatter_dimension=0, tiled=True),
        lax.psum_scatter(grad_b_up, "ctx", scatter_dimension=0, tiled=True),
        lax.psum_scatter(grad_a_down, "ctx", scatter_dimension=0, tiled=True),
        lax.psum_scatter(grad_b_down, "ctx", scatter_dimension=0, tiled=True),
    )
    return (
        block_result,
        input_grad,
        reduced[0],
        reduced[1],
        reduced[2],
        reduced[3],
        reduced[4],
        reduced[5],
        reduced[6],
        reduced[7],
        reduced[8],
        reduced[9],
        reduced[10],
        reduced[11],
        reduced[12],
        reduced[13],
    )


def solution(mesh):
    return jax.shard_map(
        local,
        mesh=mesh,
        in_specs=(
            P(None, "ctx", None),
            P(None, "ctx", None),
            P(),
            P(),
            P(),
            P(),
            P(),
            P(),
            P(None, "tp"),
            P(None, "tp"),
            P(None, "tp"),
            P("tp", None),
            P(None, "tp"),
            P(None, "tp"),
            P("tp", None),
            P(),
            P(None, "tp"),
            P(),
            P(None, "tp"),
            P(),
            P(None, "tp"),
            P(None, "tp"),
            P(),
            P(),
            P(None, "tp"),
            P(),
            P(None, "tp"),
            P(None, "tp"),
            P(),
        ),
        out_specs=(
            P(None, "ctx", None),
            P(None, "ctx", None),
            P("ctx", None),
            P("ctx", "tp"),
            P("ctx", None),
            P("ctx", "tp"),
            P("ctx", None),
            P("ctx", "tp"),
            P("ctx", "tp"),
            P("ctx", None),
            P("ctx", None),
            P("ctx", "tp"),
            P("ctx", None),
            P("ctx", "tp"),
            P("ctx", "tp"),
            P("ctx", None),
        ),
        check_vma=False,
    )
```

profile of v0, /device:TPU:0, one launch (start us, length us, event | category | flops | bytes accessed | tf_op | source)
XLA Modules:
  0.0 1603.0 jit_solution(5591606998434879347)
XLA Ops:
  23.7 3.3 fusion.71
  28.5 3.0 copy.115
  36.9 30.7 %all-gather.5.cloned.1.call-done = bf16[4,2048,256]{2,1,0:T(8,128)(2,1)} async-done(((bf16[4,128,256]{2,1,0:T(8,128)(2,1)}), bf16[4,2048,256]{2,1,0:T(8,128)(2,1)}) %all-gather.5.cloned.1.call-update) | async-done | bytes 4194320 | tf_op jit(solution)/shard_map/all_gather | solution.py:182
  67.6 6.3 copy.116
  73.9 47.6 %all-gather.3.cloned.1.call-done = bf16[4,2048,256]{1,2,0:T(8,128)(2,1)} async-done(((bf16[4,128,256]{1,2,0:T(8,128)(2,1)}), bf16[4,2048,256]{1,2,0:T(8,128)(2,1)}) %all-gather.3.cloned.1.call-update) | async-done | bytes 4194320 | tf_op jit(solution)/shard_map/all_gather | solution.py:181
  122.8 13.4 while.28
  128.1 3.1 fusion.222
  131.3 3.8 multiply_add_fusion.16
  142.2 9.4 fusion.27
  151.7 4.0 convolution_add_fusion
  155.7 78.0 %all-reduce.22.cloned.1.call-done = (bf16[4,128,1536]{2,1,0:T(8,128)(2,1)}, bf16[4,128,128]{2,1,0:T(8,128)(2,1)}) async-done(((bf16[4,128,1536]{2,1,0:T(8,128)(2,1)}, bf16[4,128,128]{2,1,0:T(8,128)(2,1)}), (bf16[4,128,1536]{2,1,0:T(8,128)(2,1)}, bf16[4,128,128]{2,1,0:T(8,128)(2,1)})) %all-reduce.22.cloned.1.call-update) | async-done | bytes 1703952 | tf_op jit(solution)/shard_map/psum | solution.py:225
  233.7 3.0 multiply_reduce_fusion.1
  239.2 9.6 fusion.33
  248.9 7.8 fusion.37
  256.7 4.0 multiply_add_fusion.2
  260.8 9.3 multiply_convert_fusion.1
  272.3 8.8 fusion.31
  282.8 9.5 fusion.61
  293.0 57.0 %all-reduce.20.cloned.1.call-done = (bf16[4,128,1536]{2,1,0:T(8,128)(2,1)}, bf16[4,128,128]{2,1,0:T(8,128)(2,1)}, bf16[4,128,128]{2,1,0:T(8,128)(2,1)}) async-done(((bf16[4,128,1536]{2,1,0:T(8,128)(2,1)}, bf16[4,128,128]{2,1,0:T(8,128)(2,1)}, bf16[4,128,128]{2,1,0:T(8,128)(2,1)}), (bf16[4,128,1536]{2,1,0:T(8,128)(2,1)}, bf16[4,128,128]{2,1,0:T(8,128)(2,1)}, ...) | async-done | bytes 1835024 | tf_op jit(solution)/shard_map/psum | solution.py:273
  361.7 8.0 broadcast_in_dim.69.clone
  369.7 39.6 %while.29 = (s32[]{:T(128)}, f32[4,128,4,3,64]{1,4,3,2,0:T(8,128)}, f32[2048,4,512]{2,0,1:T(8,128)}, s32[]{:T(128)}, bf16[4,2048,256]{1,2,0:T(8,128)(2,1)}, /*in...) while((s32[]{:T(128)}, f32[4,128,4,3,64]{1,4,3,2,0:T(8,128)}, ...), condition=%wide.region_18.19_spmd.clone, body=%wide.region_17.18_spmd.clone.sunk | while | flops 2053964416 | bytes 119512392 | solution.py:365
  372.8 6.4 fusion.233
  379.2 6.4 fusion.235
  385.6 7.5 fusion.234
  399.0 5.3 copy.193
  404.3 4.6 constant_dynamic-update-slice_fusion.2
  410.5 3.9 convolution_convert_fusion.1
  414.4 9.6 fusion.56
  428.0 3.1 fusion.69
  431.2 274.9 %reduce-scatter.13.cloned.1.call-done = f32[128,4,512]{2,0,1:T(8,128)} async-done(((f32[2048,4,512]{2,0,1:T(8,128)}), f32[128,4,512]{2,0,1:T(8,128)}) %reduce-scatter.13.cloned.1.call-update) | async-done | bytes 1048592 | tf_op jit(solution)/shard_map/reduce_scatter | solution.py:366
  714.9 4.1 convolution_bitcast_fusion
  730.4 2.9 convolution_bitcast_fusion.5
  738.9 72.3 %all-reduce.18.cloned.1.call-done = (bf16[4,128,1536]{2,1,0:T(8,128)(2,1)}, bf16[4,128,128]{2,1,0:T(8,128)(2,1)}, bf16[4,128,1536]{2,1,0:T(8,128)(2,1)}, bf16[4,...) async-done(((bf16[4,128,1536]{2,1,0:T(8,128)(2,1)}, bf16[4,128,128]{2,1,0:T(8,128)(2,1)}, bf16[4,128,1536]{2,1,0:T(8,128)(2,1)}, ...) | async-done | bytes 3670032 | tf_op jit(solution)/shard_map/psum | solution.py:248
  817.1 124.5 %all-reduce.16.cloned.1.call-done = (f32[128,3456]{1,0:T(8,128)}, f32[128,3456]{1,0:T(8,128)}, f32[128,3456]{1,0:T(8,128)}) async-done(((f32[128,3456]{1,0:T(8,128)}, f32[128,3456]{1,0:T(8,128)}, f32[128,3456]{1,0:T(8,128)}), (f32[128,3456]{1,0:T(8,128)}, f32[128,3456]{1,0:T(8,128)}, f32[128,3456]{1,0:T(8,128)})) %all-reduce.16.cloned.1.call-update) | async-done | bytes 5308432
  952.0 3.0 fusion.55
  955.8 3.4 fusion.59
  959.2 4.0 fusion.51
  963.1 38.3 %reduce-scatter.27.cloned.1.call-done = f32[8,768]{1,0:T(8,128)} async-done(((f32[128,768]{1,0:T(8,128)}), f32[8,768]{1,0:T(8,128)}) %reduce-scatter.27.cloned.1.call-update) | async-done | bytes 24592 | tf_op jit(solution)/shard_map/reduce_scatter | solution.py:426
  1001.4 59.1 %reduce-scatter.17.cloned.1.call-done = f32[8,768]{1,0:T(8,128)} async-done(((f32[128,768]{1,0:T(8,128)}), f32[8,768]{1,0:T(8,128)}) %reduce-scatter.17.cloned.1.call-update) | async-done | bytes 24592 | tf_op jit(solution)/shard_map/reduce_scatter | solution.py:421
  1060.5 59.5 %reduce-scatter.33.cloned.1.call-done = f32[8,1536]{1,0:T(8,128)} async-done(((f32[128,1536]{1,0:T(8,128)}), f32[8,1536]{1,0:T(8,128)}) %reduce-scatter.33.cloned.1.call-update) | async-done | bytes 49168 | tf_op jit(solution)/shard_map/reduce_scatter | solution.py:430
  1120.0 60.2 %reduce-scatter.31.cloned.1.call-done = f32[8,1536]{1,0:T(8,128)} async-done(((f32[128,1536]{1,0:T(8,128)}), f32[8,1536]{1,0:T(8,128)}) %reduce-scatter.31.cloned.1.call-update) | async-done | bytes 49168 | tf_op jit(solution)/shard_map/reduce_scatter | solution.py:428
  1180.2 59.6 %reduce-scatter.29.cloned.1.call-done = f32[8,1536]{1,0:T(8,128)} async-done(((f32[128,1536]{1,0:T(8,128)}), f32[8,1536]{1,0:T(8,128)}) %reduce-scatter.29.cloned.1.call-update) | async-done | bytes 49168 | tf_op jit(solution)/shard_map/reduce_scatter | solution.py:427
  1239.8 58.6 %reduce-scatter.25.cloned.1.call-done = f32[8,256]{1,0:T(8,128)} async-done(((f32[128,256]{1,0:T(8,128)}), f32[8,256]{1,0:T(8,128)}) %reduce-scatter.25.cloned.1.call-update) | async-done | bytes 8208 | tf_op jit(solution)/shard_map/reduce_scatter | solution.py:425
  1298.4 58.4 %reduce-scatter.21.cloned.1.call-done = f32[8,256]{1,0:T(8,128)} async-done(((f32[128,256]{1,0:T(8,128)}), f32[8,256]{1,0:T(8,128)}) %reduce-scatter.21.cloned.1.call-update) | async-done | bytes 8208 | tf_op jit(solution)/shard_map/reduce_scatter | solution.py:423
  1356.8 60.0 %reduce-scatter.35.cloned.1.call-done = f32[8,1536]{1,0:T(8,128)} async-done(((f32[128,1536]{1,0:T(8,128)}), f32[8,1536]{1,0:T(8,128)}) %reduce-scatter.35.cloned.1.call-update) | async-done | bytes 49168 | tf_op jit(solution)/shard_map/reduce_scatter | solution.py:433
  1416.8 59.6 %reduce-scatter.15.cloned.1.call-done = f32[8,1536]{1,0:T(8,128)} async-done(((f32[128,1536]{1,0:T(8,128)}), f32[8,1536]{1,0:T(8,128)}) %reduce-scatter.15.cloned.1.call-update) | async-done | bytes 49168 | tf_op jit(solution)/shard_map/reduce_scatter | solution.py:420
  1476.4 60.0 %reduce-scatter.19.cloned.1.call-done = f32[8,1536]{1,0:T(8,128)} async-done(((f32[128,1536]{1,0:T(8,128)}), f32[8,1536]{1,0:T(8,128)}) %reduce-scatter.19.cloned.1.call-update) | async-done | bytes 49168 | tf_op jit(solution)/shard_map/reduce_scatter | solution.py:422
  1536.3 59.6 %reduce-scatter.23.cloned.1.call-done = f32[8,1536]{1,0:T(8,128)} async-done(((f32[128,1536]{1,0:T(8,128)}), f32[8,1536]{1,0:T(8,128)}) %reduce-scatter.23.cloned.1.call-update) | async-done | bytes 49168 | tf_op jit(solution)/shard_map/reduce_scatter | solution.py:424
  (395 shorter events, 110.6 us)
Async XLA Ops:
  7.2 131.8 %copy-start = (bf16[768,1536]{1,0:T(8,128)(2,1)S(1)}, bf16[768,1536]{1,0:T(8,128)(2,1)}, u32[]{:S(2)}) copy-start(bf16[768,1536]{1,0:T(8,128)(2,1)} %param.44) | copy-start | bytes 7077892
  7.2 60.4 %all-gather.5.cloned.1.call-start = ((), (), s32[]{:S(2)}) async-start(), calls=%async_computation.13 | async-start | bytes 4456448 | tf_op jit(solution)/shard_map/all_gather | solution.py:182
  9.3 14.4 copy-start.107
  10.0 342.4 %copy-start.74 = (f32[4,128]{1,0:T(4,128)}, f32[4,128]{1,0:T(4,128)S(1)}, u32[]{:S(2)}) copy-start(f32[4,128]{1,0:T(4,128)S(1)} %compare_convert_fusion) | copy-start | bytes 6148
  14.1 107.4 %all-gather.3.cloned.1.call-start = ((), (), s32[]{:S(2)}) async-start(), calls=%async_computation.12 | async-start | bytes 4456448 | tf_op jit(solution)/shard_map/all_gather | solution.py:181
  20.0 15.8 copy-start.70
  20.0 15.8 copy-start.72
  21.4 212.3 %all-reduce.22.cloned.1.call-start = ((), (), s32[]{:S(2)}) async-start(), calls=%async_computation.29 | async-start | bytes 3407872 | tf_op jit(solution)/shard_map/psum | solution.py:225
  36.3 37.6 %copy-start.97 = (f32[4,128]{1,0:T(4,128)}, f32[4,128]{1,0:T(4,128)S(1)}, u32[]{:S(2)}) copy-start(f32[4,128]{1,0:T(4,128)S(1)} %compare_select_fusion) | copy-start | bytes 6148
  36.9 114.8 %copy-start.40 = (bf16[4,128,128]{2,1,0:T(8,128)(2,1)}, bf16[4,128,128]{2,1,0:T(8,128)(2,1)S(1)}, u32[]{:S(2)}) copy-start(bf16[4,128,128]{2,1,0:T(8,128)(2,1)S(1)} %fusion.86) | copy-start | bytes 393220
  122.8 15.1 copy-start.60
  141.6 208.5 %all-reduce.20.cloned.1.call-start = ((), (), s32[]{:S(2)}) async-start(), calls=%async_computation.28 | async-start | bytes 3670016 | tf_op jit(solution)/shard_map/psum | solution.py:273
  236.8 12.1 slice-start.2
  238.0 10.8 copy-start.12
  238.6 18.1 %copy-start.42 = (bf16[4,128,128]{2,1,0:T(8,128)(2,1)}, bf16[4,128,128]{2,1,0:T(8,128)(2,1)S(1)}, u32[]{:S(2)}) copy-start(bf16[4,128,128]{2,1,0:T(8,128)(2,1)S(1)} %fusion.85) | copy-start | bytes 393220
  239.2 21.5 %copy-start.55 = (bf16[4,128,128]{2,1,0:T(8,128)(2,1)}, bf16[4,128,128]{2,1,0:T(8,128)(2,1)S(1)}, u32[]{:S(2)}) copy-start(bf16[4,128,128]{2,1,0:T(8,128)(2,1)S(1)} %fusion.84) | copy-start | bytes 393220
  239.2 9.6 slice-start.3
  239.2 9.6 slice-start.4
  239.2 21.5 %slice-start = ((s8[7077888]{0:T(1024)(128)(4,1)}), s8[4194304]{0:T(1024)(128)(4,1)S(1)}, s32[]{:S(2)}) async-start(s8[7077888]{0:T(1024)(128)(4,1)} %bitcast.371), calls=%async_computation.30 | async-start | bytes 8388608
  248.9 11.9 slice-start.1
  270.1 12.8 copy-start.30
  292.4 413.7 %reduce-scatter.13.cloned.1.call-start = ((), (), s32[]{:S(2)}) async-start(), calls=%async_computation.14 | async-start | bytes 17825792 | tf_op jit(solution)/shard_map/reduce_scatter | solution.py:366
  409.4 401.9 %all-reduce.18.cloned.1.call-start = ((), (), s32[]{:S(2)}) async-start(), calls=%async_computation.27 | async-start | bytes 7340032 | tf_op jit(solution)/shard_map/psum | solution.py:248
  428.0 279.3 %copy-start.94 = (bf16[128,256]{1,0:T(8,128)(2,1)S(1)}, bf16[128,256]{1,0:T(8,128)(2,1)}, u32[]{:S(2)}) copy-start(bf16[128,256]{1,0:T(8,128)(2,1)} %param.53) | copy-start | bytes 196612
  431.1 277.3 %copy-start.25 = (f32[4,128,256]{1,2,0:T(8,128)S(1)}, f32[4,128,256]{1,2,0:T(8,128)}, u32[]{:S(2)}) copy-start(f32[4,128,256]{1,2,0:T(8,128)} %copy-done.24) | copy-start | bytes 1572868
  431.1 277.3 %copy-start.111 = (f32[64]{0:T(128)S(1)}, f32[64]{0:T(128)}, u32[]{:S(2)}) copy-start(f32[64]{0:T(128)} %param.40) | copy-start | bytes 772
  431.1 277.5 %copy-start.92 = (f32[4,128,4]{1,2,0:T(4,128)S(1)}, f32[4,128,4]{1,2,0:T(4,128)}, u32[]{:S(2)}) copy-start(f32[4,128,4]{1,2,0:T(4,128)} %copy-done.91) | copy-start | bytes 24580
  431.2 277.5 %copy-start.90 = (f32[4,128,4]{1,2,0:T(4,128)S(1)}, f32[4,128,4]{1,2,0:T(4,128)}, u32[]{:S(2)}) copy-start(f32[4,128,4]{1,2,0:T(4,128)} %copy-done.89) | copy-start | bytes 24580
  431.2 277.7 %copy-start.84 = (bf16[128,256]{1,0:T(8,128)(2,1)S(1)}, bf16[128,256]{1,0:T(8,128)(2,1)}, u32[]{:S(2)}) copy-start(bf16[128,256]{1,0:T(8,128)(2,1)} %param.51) | copy-start | bytes 196612
  714.0 227.6 %all-reduce.16.cloned.1.call-start = ((), (), s32[]{:S(2)}) async-start(), calls=%async_computation.26 | async-start | bytes 10616832
  724.0 277.4 %reduce-scatter.27.cloned.1.call-start = ((), (), s32[]{:S(2)}) async-start(), calls=%async_computation.21 | async-start | bytes 417792 | tf_op jit(solution)/shard_map/reduce_scatter | solution.py:426
  726.2 334.3 %reduce-scatter.17.cloned.1.call-start = ((), (), s32[]{:S(2)}) async-start(), calls=%async_computation.16 | async-start | bytes 417792 | tf_op jit(solution)/shard_map/reduce_scatter | solution.py:421
  727.5 392.6 %reduce-scatter.33.cloned.1.call-start = ((), (), s32[]{:S(2)}) async-start(), calls=%async_computation.24 | async-start | bytes 835584 | tf_op jit(solution)/shard_map/reduce_scatter | solution.py:430
  730.4 449.8 %reduce-scatter.31.cloned.1.call-start = ((), (), s32[]{:S(2)}) async-start(), calls=%async_computation.23 | async-start | bytes 835584 | tf_op jit(solution)/shard_map/reduce_scatter | solution.py:428
  733.3 506.5 %reduce-scatter.29.cloned.1.call-start = ((), (), s32[]{:S(2)}) async-start(), calls=%async_computation.22 | async-start | bytes 835584 | tf_op jit(solution)/shard_map/reduce_scatter | solution.py:427
  734.7 79.4 %copy-start.119 = (u32[32]{0:T(128)S(1)}, u32[32]{0:T(128)}, u32[]{:S(2)}) copy-start(u32[32]{0:T(128)} %constant.141) | copy-start | bytes 388
  734.7 80.7 %copy-start.16 = (bf16[4,128,1536]{2,1,0:T(8,128)(2,1)S(1)}, bf16[4,128,1536]{2,1,0:T(8,128)(2,1)}, u32[]{:S(2)}) copy-start(bf16[4,128,1536]{2,1,0:T(8,128)(2,1)} %param.33) | copy-start | bytes 4718596
  734.7 80.7 %copy-start.106 = (f32[1536]{0:T(1024)S(1)}, f32[1536]{0:T(1024)}, u32[]{:S(2)}) copy-start(f32[1536]{0:T(1024)} %param.37) | copy-start | bytes 18436
  734.7 80.7 %copy-start.108 = (f32[4,128]{1,0:T(4,128)S(1)}, f32[4,128]{1,0:T(4,128)}, u32[]{:S(2)}) copy-start(f32[4,128]{1,0:T(4,128)} %copy-done.107) | copy-start | bytes 6148
  734.8 563.6 %reduce-scatter.25.cloned.1.call-start = ((), (), s32[]{:S(2)}) async-start(), calls=%async_computation.20 | async-start | bytes 139264 | tf_op jit(solution)/shard_map/reduce_scatter | solution.py:425
  736.8 619.9 %reduce-scatter.21.cloned.1.call-start = ((), (), s32[]{:S(2)}) async-start(), calls=%async_computation.18 | async-start | bytes 139264 | tf_op jit(solution)/shard_map/reduce_scatter | solution.py:423
  738.9 677.9 %reduce-scatter.35.cloned.1.call-start = ((), (), s32[]{:S(2)}) async-start(), calls=%async_computation.25 | async-start | bytes 835584 | tf_op jit(solution)/shard_map/reduce_scatter | solution.py:433
  814.1 130.7 %copy-start.87 = (bf16[4,128,128]{2,1,0:T(8,128)(2,1)S(1)}, bf16[4,128,128]{2,1,0:T(8,128)(2,1)}, u32[]{:S(2)}) copy-start(bf16[4,128,128]{2,1,0:T(8,128)(2,1)} %get-tuple-element.333) | copy-start | bytes 393220
  814.1 662.3 %reduce-scatter.15.cloned.1.call-start = ((), (), s32[]{:S(2)}) async-start(), calls=%async_computation.15 | async-start | bytes 835584 | tf_op jit(solution)/shard_map/reduce_scatter | solution.py:420
  815.4 131.0 %copy-start.85 = (bf16[4,128,128]{2,1,0:T(8,128)(2,1)S(1)}, bf16[4,128,128]{2,1,0:T(8,128)(2,1)}, u32[]{:S(2)}) copy-start(bf16[4,128,128]{2,1,0:T(8,128)(2,1)} %get-tuple-element.334) | copy-start | bytes 393220
  817.1 719.3 %reduce-scatter.19.cloned.1.call-start = ((), (), s32[]{:S(2)}) async-start(), calls=%async_computation.17 | async-start | bytes 835584 | tf_op jit(solution)/shard_map/reduce_scatter | solution.py:422
  948.0 647.9 %reduce-scatter.23.cloned.1.call-start = ((), (), s32[]{:S(2)}) async-start(), calls=%async_computation.19 | async-start | bytes 835584 | tf_op jit(solution)/shard_map/reduce_scatter | solution.py:424
  959.2 636.8 %copy-start.1 = (bf16[768,1536]{1,0:T(8,128)(2,1)S(1)}, bf16[768,1536]{1,0:T(8,128)(2,1)}, u32[]{:S(2)}) copy-start(bf16[768,1536]{1,0:T(8,128)(2,1)} %param.44) | copy-start | bytes 7077892
  (95 other events, 275.1 us)
Sparse Core Ops, SparseCore 0:
  14.3 53.3 all-gather.4
  69.8 51.6 all-gather.2
  141.7 91.9 all-reduce.21
  292.5 57.5 all-reduce.19
  409.5 296.5 reduce-scatter.12
  714.1 97.0 all-reduce.17
  815.8 125.7 all-reduce.15
  945.7 55.6 reduce-scatter.26
  1005.9 54.5 reduce-scatter.16
  1064.5 55.5 reduce-scatter.32
  1124.6 55.5 reduce-scatter.30
  1184.2 55.5 reduce-scatter.28
  1244.2 54.0 reduce-scatter.24
  1302.6 54.0 reduce-scatter.20
  1361.2 55.5 reduce-scatter.34
  1420.7 55.5 reduce-scatter.14
  1480.7 55.5 reduce-scatter.18
  1540.3 55.5 reduce-scatter.22
where the time goes:
time: 1610 us; the launch traced here: 1600 us
  waiting for transfers between devices  1320 us (82%)
  matrix products  187 us (12%)
  local copies, waits for them, and re-layouts  53.1 us (3%)
  other arithmetic  25.9 us (2%)
  between operations  16.7 us (1%)
    reduce_scatter x1, waiting for transfers between devices, local(): lax.psum_scatter(key_terms, 'ctx', scatter_dimension=0, tiled=True)  275 us
    unnamed x19, waiting for transfers between devices  125 us
    psum x1, waiting for transfers between devices, local(): lax.psum(part_out.astype(jnp.bfloat16), 'tp').astype(jnp.float32)  78 us
    psum x1, waiting for transfers between devices, local(): lax.psum(part_down.astype(jnp.bfloat16), 'tp').astype(jnp.float32)  72.3 us
    reduce_scatter x1, waiting for transfers between devices, local(): lax.psum_scatter(grad_a_gate, 'ctx', scatter_dimension=0, tiled=True)  60.2 us
    reduce_scatter x1, waiting for transfers between devices, local(): lax.psum_scatter(grad_b_down, 'ctx', scatter_dimension=0, tiled=True)  60 us
    reduce_scatter x1, waiting for transfers between devices, local(): lax.psum_scatter(grad_a_key, 'ctx', scatter_dimension=0, tiled=True)  60 us
    reduce_scatter x1, waiting for transfers between devices, local(): lax.psum_scatter(grad_b_out, 'ctx', scatter_dimension=0, tiled=True)  59.6 us
  transfers between devices with their start and end apart: 18, of which 18 were waited for; matrix products, arithmetic and copies ran while one was open for 7% of the time, Pallas kernels for 0%

commit v1 on v0

v1 whole, which is shorter than its diff:
```python
import functools, jax, jax.numpy as jnp
from jax import lax
from jax.experimental import pallas as pl
from jax.experimental.pallas import tpu as pltpu
from jax.sharding import PartitionSpec as P

HEAD_DIM = 64
LOG2E = 1.4426950408889634
KEY_TILE = 256


def tile_bounds(tile, stride, part):
    first = (2 * tile) * stride + part
    last = (2 * tile + 1) * stride + part
    return first, last


def allowed_pairs(seg_rows, seq, first, last, key_tile, group):
    lanes = lax.broadcasted_iota(jnp.int32, (1, 128), 1)
    q_pos = jnp.concatenate([first * 128 + lanes, last * 128 + lanes], axis=1)
    q_seg = jnp.concatenate(
        [seg_rows[seq, block] for block in (first, last)], axis=1
    )
    k_seg = jnp.concatenate(
        [jnp.transpose(jnp.broadcast_to(seg_rows[seq, 2 * key_tile + b], (128, 128))) for b in (0, 1)], axis=0
    )
    k_seg = jnp.concatenate([k_seg, k_seg], axis=1)
    k_pos = key_tile * 256 + lax.broadcasted_iota(jnp.int32, (256, 256), 0)
    allowed = (k_seg == jnp.broadcast_to(q_seg, (256, 256))) & (k_pos <= jnp.broadcast_to(q_pos, (256, 256)))
    return jnp.concatenate([allowed] * group, axis=1)


def tile_kind(seg_smem, seq, first, last, key_tile):
    key_low = seg_smem[seq, key_tile * 256]
    key_high = seg_smem[seq, key_tile * 256 + 255]
    q_low = seg_smem[seq, first * 128]
    q_high = seg_smem[seq, last * 128 + 127]
    needed = key_high >= q_low
    plain = (key_low == q_high) & (2 * key_tile + 1 < first)
    return needed, plain


def heads_side_by_side(ref, tile, group, offset=0):
    return jnp.concatenate(
        [ref[2 * tile + b, offset + h * HEAD_DIM : offset + (h + 1) * HEAD_DIM, :] for h in range(group) for b in (0, 1)], axis=1
    )


def attn_fwd_kernel(stride, group, units_per_seq, unit_ref, seg_smem, seg_rows, q_ref, kv_ref, o_ref, of_ref, lse_ref, kb, vt, acc):
    unit, part = unit_ref[0], unit_ref[1]
    seq = unit // units_per_seq
    key_tiles = kv_ref.shape[0] // 2
    q_tiles = q_ref.shape[0] // 2
    width = group * 256

    def load(j, _):
        for b in (0, 1):
            kb[j, b * 128 : (b + 1) * 128, :] = jnp.transpose(kv_ref[2 * j + b, :HEAD_DIM, :])
            vt[j, :HEAD_DIM, b * 128 : (b + 1) * 128] = kv_ref[2 * j + b, HEAD_DIM:, :]
        vt[j, HEAD_DIM:, :] = jnp.ones((16, 256), jnp.bfloat16)
        return 0

    lax.fori_loop(0, key_tiles, load, 0)

    def q_step(i, _):
        first, last = tile_bounds(i, stride, part)
        qt = heads_side_by_side(q_ref, i, group)
        acc[...] = jnp.zeros_like(acc)

        def k_step(j, _):
            needed, plain = tile_kind(seg_smem, seq, first, last, j)

            def weigh(masked):
                s = jnp.dot(kb[j], qt, preferred_element_type=jnp.float32)
                p = jnp.exp2(s * (LOG2E * HEAD_DIM**-0.5))
                if masked:
                    p = jnp.where(allowed_pairs(seg_rows, seq, first, last, j, group), p, 0.0)
                acc[...] += jnp.dot(vt[j], p.astype(jnp.bfloat16), preferred_element_type=jnp.float32)

            @pl.when(needed & plain)
            def _():
                weigh(False)

            @pl.when(needed & jnp.logical_not(plain))
            def _():
                weigh(True)

            return 0

        lax.fori_loop(0, last // 2 + 1, k_step, 0)
        total = acc[HEAD_DIM : HEAD_DIM + 1, :]
        lse_ref[i] = jnp.broadcast_to(jnp.log2(total), (8, width))
        out = acc[:HEAD_DIM, :] / total
        for h in range(group):
            for b in (0, 1):
                piece = out[:, h * 256 + b * 128 : h * 256 + (b + 1) * 128]
                of_ref[2 * i + b, h * HEAD_DIM : (h + 1) * HEAD_DIM, :] = piece
                o_ref[2 * i + b, h * HEAD_DIM : (h + 1) * HEAD_DIM, :] = piece.astype(jnp.bfloat16)
        return 0

    lax.fori_loop(0, q_tiles, q_step, 0)


def attn_bwd_kernel(
    stride, group, units_per_seq, unit_ref, seg_smem, seg_rows, q_ref, kv_ref, do_ref, of_ref, lse_ref,
    dq_ref, dkv_ref, qt, q3, dot_t, do3, delta, dqt,
):
    unit, part = unit_ref[0], unit_ref[1]
    seq = unit // units_per_seq
    key_tiles = kv_ref.shape[0] // 2
    q_tiles = q_ref.shape[0] // 2
    width = group * 256

    def load(i, _):
        for h in range(group):
            for b in (0, 1):
                rows = slice(h * HEAD_DIM, (h + 1) * HEAD_DIM)
                lanes = slice(h * 256 + b * 128, h * 256 + (b + 1) * 128)
                q = q_ref[2 * i + b, rows, :]
                g = do_ref[2 * i + b, rows, :]
                qt[i, :, lanes] = q
                q3[i, lanes, :] = jnp.transpose(q)
                dot_t[i, :, lanes] = g
                do3[i, lanes, :] = jnp.transpose(g)
                d = jnp.sum(g.astype(jnp.float32) * of_ref[2 * i + b, rows, :], axis=0, keepdims=True)
                delta[i, :, lanes] = jnp.broadcast_to(d, (8, 128))
        dqt[i] = jnp.zeros((HEAD_DIM, width), jnp.float32)
        return 0

    lax.fori_loop(0, q_tiles, load, 0)

    def k_step(j, _):
        kt = jnp.concatenate([kv_ref[2 * j + b, :HEAD_DIM, :] for b in (0, 1)], axis=1)
        vt = jnp.concatenate([kv_ref[2 * j + b, HEAD_DIM:, :] for b in (0, 1)], axis=1)
        kb = jnp.transpose(kt)
        vb = jnp.transpose(vt)

        def q_step(i, state):
            first, last = tile_bounds(i, stride, part)
            needed, plain = tile_kind(seg_smem, seq, first, last, j)

            def terms(masked, dk, dv):
                s = jnp.dot(kb, qt[i], preferred_element_type=jnp.float32)
                p = jnp.exp2(s * (LOG2E * HEAD_DIM**-0.5) - lse_ref[i, 0:1, :])
                if masked:
                    p = jnp.where(allowed_pairs(seg_rows, seq, first, last, j, group), p, 0.0)
                dp = jnp.dot(vb, dot_t[i], preferred_element_type=jnp.float32)
                ds = (p * (dp - delta[i, 0:1, :])).astype(jnp.bfloat16)
                dv = dv + jnp.dot(p.astype(jnp.bfloat16), do3[i], preferred_element_type=jnp.float32)
                dk = dk + jnp.dot(ds, q3[i], preferred_element_type=jnp.float32)
                dqt[i] += jnp.dot(kt, ds, preferred_element_type=jnp.float32)
                return dk, dv

            kind = jnp.where(needed, jnp.where(plain, 1, 2), 0)
            return lax.switch(
                kind, [lambda a, b: (a, b), functools.partial(terms, False), functools.partial(terms, True)], *state
            )

        zero = jnp.zeros((256, HEAD_DIM), jnp.float32)
        start = jnp.maximum((2 * j - part + stride - 1) // stride, 0) // 2
        dk, dv = lax.fori_loop(start, q_tiles, q_step, (zero, zero))
        for b in (0, 1):
            rows = slice(b * 128, (b + 1) * 128)
            dkv_ref[2 * j + b, :HEAD_DIM, :] = jnp.transpose(dk[rows] * HEAD_DIM**-0.5).astype(jnp.bfloat16)
            dkv_ref[2 * j + b, HEAD_DIM:, :] = jnp.transpose(dv[rows]).astype(jnp.bfloat16)
        return 0

    lax.fori_loop(0, key_tiles, k_step, 0)

    def store(i, _):
        for h in range(group):
            for b in (0, 1):
                piece = dqt[i, :, h * 256 + b * 128 : h * 256 + (b + 1) * 128]
                dq_ref[2 * i + b, h * HEAD_DIM : (h + 1) * HEAD_DIM, :] = (piece * HEAD_DIM**-0.5).astype(jnp.bfloat16)
        return 0

    lax.fori_loop(0, q_tiles, store, 0)


SMEM = pl.BlockSpec(memory_space=pltpu.SMEM)
VM = pl.BlockSpec(memory_space=pltpu.VMEM)


def attn_fwd(unit, segs, q, kv, stride, units_per_seq):
    blocks, qrows, _ = q.shape
    group = qrows // HEAD_DIM
    tiles, ktiles, width = blocks // 2, kv.shape[0] // 2, group * 256
    return pl.pallas_call(
        functools.partial(attn_fwd_kernel, stride, group, units_per_seq),
        out_shape=(
            jax.ShapeDtypeStruct(q.shape, jnp.bfloat16),
            jax.ShapeDtypeStruct(q.shape, jnp.float32),
            jax.ShapeDtypeStruct((tiles, 8, width), jnp.float32),
        ),
        in_specs=[SMEM, SMEM, VM, VM, VM],
        out_specs=(VM, VM, VM),
        scratch_shapes=[
            pltpu.VMEM((ktiles, 256, HEAD_DIM), jnp.bfloat16),
            pltpu.VMEM((ktiles, HEAD_DIM + 16, 256), jnp.bfloat16),
            pltpu.VMEM((HEAD_DIM + 16, width), jnp.float32),
        ],
        compiler_params=pltpu.CompilerParams(vmem_limit_bytes=56 * 2**20),
        name="attention_forward",
    )(unit, segs, segs.reshape(segs.shape[0], -1, 1, 128), q, kv)


def attn_bwd(unit, segs, q, kv, do, of, lse, stride, units_per_seq):
    blocks, qrows, _ = q.shape
    group = qrows // HEAD_DIM
    tiles, ktiles, width = blocks // 2, kv.shape[0] // 2, group * 256
    return pl.pallas_call(
        functools.partial(attn_bwd_kernel, stride, group, units_per_seq),
        out_shape=(jax.ShapeDtypeStruct(q.shape, jnp.bfloat16), jax.ShapeDtypeStruct(kv.shape, jnp.bfloat16)),
        in_specs=[SMEM, SMEM, VM, VM, VM, VM, VM, VM],
        out_specs=(VM, VM),
        scratch_shapes=[
            pltpu.VMEM((tiles, HEAD_DIM, width), jnp.bfloat16),
            pltpu.VMEM((tiles, width, HEAD_DIM), jnp.bfloat16),
            pltpu.VMEM((tiles, HEAD_DIM, width), jnp.bfloat16),
            pltpu.VMEM((tiles, width, HEAD_DIM), jnp.bfloat16),
            pltpu.VMEM((tiles, 8, width), jnp.float32),
            pltpu.VMEM((tiles, HEAD_DIM, width), jnp.float32),
        ],
        compiler_params=pltpu.CompilerParams(vmem_limit_bytes=56 * 2**20),
        name="attention_backward",
    )(unit, segs, segs.reshape(segs.shape[0], -1, 1, 128), q, kv, do, of, lse)


NT = (((1,), (1,)), ((), ()))


def mm(a, b):
    return jnp.dot(a, b, preferred_element_type=jnp.float32)


def mm_nt(a, b):
    return lax.dot_general(a, b, NT, preferred_element_type=jnp.float32)


def ffn_kernel(
    chunk, n2_ref, cot_ref, mask_ref, ag_ref, au_ref, bd_ref, wg_ref, wu_ref, wd_ref, bg_ref, bu_ref, ad_ref,
    down_ref, dn2_ref, gbg_ref, gbu_ref, gad_ref,
    hg, hu, dhd, hgt, hut, dhdt, down_acc, hdown_acc, dn2_acc, dhg_acc, dhu_acc, d_gate, d_up, hidden,
):
    step = pl.program_id(0)
    rows = n2_ref.shape[0]

    @pl.when(step == 0)
    def _():
        mask = mask_ref[...]
        hg[...] = (mm_nt(n2_ref[...], ag_ref[...]) * mask).astype(jnp.bfloat16)
        hu[...] = (mm_nt(n2_ref[...], au_ref[...]) * mask).astype(jnp.bfloat16)
        dhd[...] = (mm_nt(cot_ref[...], bd_ref[...]) * (2.0 * mask)).astype(jnp.bfloat16)
        hgt[...] = jnp.transpose(hg[...]) * 2
        hut[...] = jnp.transpose(hu[...]) * 2
        dhdt[...] = jnp.transpose(dhd[...])
        down_acc[...] = jnp.zeros_like(down_acc)
        hdown_acc[...] = jnp.zeros_like(hdown_acc)
        dn2_acc[...] = jnp.zeros_like(dn2_acc)
        dhg_acc[...] = jnp.zeros_like(dhg_acc)
        dhu_acc[...] = jnp.zeros_like(dhu_acc)

    def one(r, _):
        rs = pl.ds(pl.multiple_of(r * chunk, chunk), chunk)
        n2 = n2_ref[rs, :]
        cot = cot_ref[rs, :]
        gate = mm(n2, wg_ref[...]) + mm(hg[rs, :] * 2, bg_ref[...])
        up = mm(n2, wu_ref[...]) + mm(hu[rs, :] * 2, bu_ref[...])
        sg = 1.0 / (1.0 + jnp.exp(-gate))
        silu = gate * sg
        hid = (silu * up).astype(jnp.bfloat16)
        hidden[rs, :] = hid
        dh = mm_nt(cot, wd_ref[...]) + mm(dhd[rs, :], ad_ref[...])
        dg = (dh * up * sg * (1.0 + gate * (1.0 - sg))).astype(jnp.bfloat16)
        du = (dh * silu).astype(jnp.bfloat16)
        d_gate[rs, :] = dg
        d_up[rs, :] = du
        down_acc[rs, :] += mm(hid, wd_ref[...])
        hdown_acc[rs, :] += mm_nt(hid, ad_ref[...])
        dn2_acc[rs, :] += mm_nt(dg, wg_ref[...]) + mm_nt(du, wu_ref[...])
        dhg_acc[rs, :] += mm_nt(dg, bg_ref[...])
        dhu_acc[rs, :] += mm_nt(du, bu_ref[...])
        return 0

    lax.fori_loop(0, rows // chunk, one, 0)
    gbg_ref[...] = mm(hgt[...], d_gate[...]).astype(gbg_ref.dtype)
    gbu_ref[...] = mm(hut[...], d_up[...]).astype(gbu_ref.dtype)
    gad_ref[...] = mm(dhdt[...], hidden[...]).astype(gad_ref.dtype)

    @pl.when(step == pl.num_programs(0) - 1)
    def _():
        width, rank = n2_ref.shape[1], ag_ref.shape[0]
        down_ref[:, :width] = down_acc[...].astype(jnp.bfloat16)
        down_ref[:, width:] = hdown_acc[...].astype(jnp.bfloat16)
        dn2_ref[:, :width] = dn2_acc[...].astype(jnp.bfloat16)
        dn2_ref[:, width : width + rank] = (dhg_acc[...] * 2).astype(jnp.bfloat16)
        dn2_ref[:, width + rank :] = (dhu_acc[...] * 2).astype(jnp.bfloat16)


def ffn(n2, cot, mask, ag, au, bd, wg, wu, wd, bg, bu, ad, tile=1152, chunk=256):
    rows, width = n2.shape
    rank = ag.shape[0]
    units = wg.shape[1]
    tile = min(tile, units)
    fixed = lambda shape: pl.BlockSpec(shape, lambda f: (0, 0))
    cols = lambda height: pl.BlockSpec((height, tile), lambda f: (0, f))
    bf = jnp.bfloat16
    out = lambda shape: jax.ShapeDtypeStruct(shape, bf)
    f32 = jnp.float32
    return pl.pallas_call(
        functools.partial(ffn_kernel, chunk),
        grid=(units // tile,),
        out_shape=(
            out((rows, width + rank)), out((rows, width + 2 * rank)),
            out((rank, units)), out((rank, units)), out((rank, units)),
        ),
        in_specs=[
            fixed((rows, width)), fixed((rows, width)), fixed((rows, rank)),
            fixed((rank, width)), fixed((rank, width)), fixed((rank, width)),
            cols(width), cols(width), pl.BlockSpec((tile, width), lambda f: (f, 0)),
            cols(rank), cols(rank), cols(rank),
        ],
        out_specs=(
            fixed((rows, width + rank)), fixed((rows, width + 2 * rank)),
            cols(rank), cols(rank), cols(rank),
        ),
        scratch_shapes=[
            pltpu.VMEM((rows, rank), bf), pltpu.VMEM((rows, rank), bf), pltpu.VMEM((rows, rank), bf),
            pltpu.VMEM((rank, rows), bf), pltpu.VMEM((rank, rows), bf), pltpu.VMEM((rank, rows), bf),
            pltpu.VMEM((rows, width), f32), pltpu.VMEM((rows, rank), f32), pltpu.VMEM((rows, width), f32),
            pltpu.VMEM((rows, rank), f32), pltpu.VMEM((rows, rank), f32),
            pltpu.VMEM((rows, tile), bf), pltpu.VMEM((rows, tile), bf), pltpu.VMEM((rows, tile), bf),
        ],
        compiler_params=pltpu.CompilerParams(vmem_limit_bytes=60 * 2**20),
        name="feed_forward",
    )(n2, cot, mask, ag, au, bd, wg, wu, wd, bg, bu, ad)


MESH = pl.DeviceIdType.MESH


def exchange_kernel(count, parts, kinds, *refs):
    n = len(kinds)
    xs, outs = refs[:n], refs[n : 2 * n]
    sends, recvs, locals_ = refs[2 * n : 3 * n], refs[3 * n : 4 * n], refs[4 * n]
    me = lax.axis_index("ctx")
    barrier = pltpu.get_barrier_semaphore()
    step = 1 if "full" in kinds else parts
    peers = count // step - 1

    def greet(k, _):
        other = lax.rem(me + k * step, count)
        pl.semaphore_signal(barrier, inc=1, device_id={"ctx": other}, device_id_type=MESH)
        return 0

    lax.fori_loop(1, peers + 1, greet, 0)

    def block(kind, x, device):
        if kind == "class" or x.shape[0] != count:
            return device // parts
        return device

    def slot(kind, device):
        return device // parts if kind == "class" else device

    def copy(i, target, place):
        kind = kinds[i]
        return pltpu.make_async_remote_copy(
            src_ref=xs[i].at[block(kind, xs[i], target)],
            dst_ref=outs[i].at[slot(kind, place)],
            send_sem=sends[i].at[slot(kind, target)],
            recv_sem=recvs[i].at[slot(kind, place)],
            device_id={"ctx": target},
            device_id_type=MESH,
        )

    own = [
        pltpu.make_async_copy(xs[i].at[block(kinds[i], xs[i], me)], outs[i].at[slot(kinds[i], me)], locals_.at[i])
        for i in range(n)
    ]
    for c in own:
        c.start()
    pl.semaphore_wait(barrier, peers)
    for i in range(n):
        hop = 1 if kinds[i] == "full" else parts

        def send(k, _, i=i, hop=hop):
            copy(i, lax.rem(me + k * hop, count), me).start()
            return 0

        lax.fori_loop(1, count // hop, send, 0)
    for i in range(n):
        hop = 1 if kinds[i] == "full" else parts

        def finish(k, _, i=i, hop=hop):
            other = lax.rem(me + k * hop, count)
            copy(i, other, me).wait_send()
            copy(i, other, other).wait_recv()
            return 0

        lax.fori_loop(1, count // hop, finish, 0)
    for c in own:
        c.wait()


def exchange(arrays, kinds, count, parts, collective_id, name):
    n = len(arrays)
    members = [count // parts if kind == "class" else count for kind in kinds]
    anywhere = pl.BlockSpec(memory_space=pl.ANY)
    return pl.pallas_call(
        functools.partial(exchange_kernel, count, parts, kinds),
        out_shape=tuple(jax.ShapeDtypeStruct((k,) + a.shape[1:], a.dtype) for k, a in zip(members, arrays)),
        in_specs=[anywhere] * n,
        out_specs=(anywhere,) * n,
        scratch_shapes=[pltpu.SemaphoreType.DMA((k,)) for k in members] * 2 + [pltpu.SemaphoreType.DMA((n,))],
        compiler_params=pltpu.CompilerParams(collective_id=collective_id, has_side_effects=True),
        name=name,
    )(*arrays)


RANK = 16
EPSILON = 1e-05
THETA_BASE = 1000000.0
BF = jnp.bfloat16
F32 = jnp.float32


def norm_rows(values, gains):
    return values * lax.rsqrt(jnp.mean(values * values, axis=-1, keepdims=True) + EPSILON) * gains


def norm_rows_back(values, gains, cotangent):
    scale = lax.rsqrt(jnp.mean(values * values, axis=-1, keepdims=True) + EPSILON)
    unit = values * scale
    weighted = cotangent * gains
    return scale * (weighted - unit * jnp.mean(weighted * unit, axis=-1, keepdims=True))


def rotary_tables(positions):
    half = HEAD_DIM // 2
    frequencies = THETA_BASE ** (-jnp.arange(half, dtype=F32) * 2.0 / HEAD_DIM)
    angles = frequencies[:, None] * positions.astype(F32)[None, :]
    return jnp.cos(angles), jnp.sin(angles)


def turn(values, cosine, sine):
    a, b = jnp.split(values, 2, axis=-2)
    return jnp.concatenate([a * cosine - b * sine, b * cosine + a * sine], axis=-2)


def head_prepare(values, gains, tables):
    sequences, width, rows = values.shape
    heads = values.reshape(sequences, width // HEAD_DIM, HEAD_DIM, rows)
    scale = lax.rsqrt(jnp.mean(heads * heads, axis=2, keepdims=True) + EPSILON)
    return turn(heads * scale * gains[:, None], *tables).astype(BF)


def head_prepare_back(values, gains, tables, cotangent):
    sequences, width, rows = values.shape
    heads = values.reshape(sequences, width // HEAD_DIM, HEAD_DIM, rows)
    scale = lax.rsqrt(jnp.mean(heads * heads, axis=2, keepdims=True) + EPSILON)
    unit = heads * scale
    cosine, sine = tables
    weighted = turn(cotangent.reshape(heads.shape).astype(F32), cosine, -sine) * gains[:, None]
    back = scale * (weighted - unit * jnp.mean(weighted * unit, axis=2, keepdims=True))
    return back.reshape(values.shape).astype(BF)


def ein(spec, a, b):
    return jnp.einsum(spec, a, b, preferred_element_type=F32)


def swap(values):
    return lax.ppermute(values, "tp", [(0, 1), (1, 0)])


def reduce_scatter_rows(grads, count):
    rows, columns = grads.shape
    index = lax.axis_index("ctx")
    held = grads.reshape(count, rows // count, columns)
    bit = 1
    while bit < count:
        mine = (index // bit) % 2
        pairs = held.reshape(held.shape[0] // 2, 2, held.shape[1], columns)
        kept = lax.dynamic_index_in_dim(pairs, mine, 1, keepdims=False)
        sent = lax.dynamic_index_in_dim(pairs, 1 - mine, 1, keepdims=False).astype(BF)
        held = kept.astype(F32) + lax.ppermute(sent, "ctx", [(i, i ^ bit) for i in range(count)]).astype(F32)
        bit *= 2
    return held[0]


def local(
    tokens, output_cotangent, segment_ids, variant, attn_gain, ffn_gain, q_gain, k_gain,
    query_matrix, key_matrix, value_matrix, output_matrix, gate_matrix, up_matrix, down_matrix,
    query_input_factor, query_output_factor, key_input_factor, key_output_factor,
    value_input_factor, value_output_factor, output_input_factor, output_output_factor,
    gate_input_factor, gate_output_factor, up_input_factor, up_output_factor,
    down_input_factor, down_output_factor,
):
    sequences, rows_here, model_width = tokens.shape
    count = lax.axis_size("ctx")
    index = lax.axis_index("ctx")
    half = lax.axis_index("tp")
    key_heads = key_matrix.shape[1] // HEAD_DIM
    group = query_matrix.shape[1] // key_matrix.shape[1]
    units = sequences * key_heads
    parts = count // units
    unit = jnp.stack([index // parts, index % parts]).astype(jnp.int32)
    stacked = query_input_factor.shape[0]
    pick = ((jnp.arange(stacked, dtype=jnp.int32) // RANK)[None, :] == variant[:, None]).astype(F32)[:, None, :]
    tables = rotary_tables(index * rows_here + jnp.arange(rows_here, dtype=jnp.int32))

    output_matrix_other = swap(output_matrix)
    output_input_other = swap(output_input_factor)

    x = tokens.astype(F32)
    n1 = norm_rows(x, attn_gain).astype(BF)

    def low(rows, factor):
        return (ein("spd,rd->spr", rows, factor) * pick).astype(BF)

    h_query, h_key, h_value = (low(n1, f) for f in (query_input_factor, key_input_factor, value_input_factor))

    def project(hidden, matrix, factor):
        return ein("spd,de->sep", n1, matrix) + 2.0 * ein("spr,re->sep", hidden, factor)

    q_pre = project(h_query, query_matrix, query_output_factor)
    k_pre = project(h_key, key_matrix, key_output_factor)
    v_pre = project(h_value, value_matrix, value_output_factor)
    queries = head_prepare(q_pre, q_gain, tables).reshape(units, group * HEAD_DIM, rows_here)
    keys = head_prepare(k_pre, k_gain, tables).reshape(units, HEAD_DIM, rows_here)
    values = v_pre.astype(BF).reshape(units, HEAD_DIM, rows_here)
    q_all, kv_all = exchange(
        (queries, jnp.concatenate([keys, values], axis=1)), ("class", "full"), count, parts, 0, "send_qkv"
    )
    o_all, o_wide, lse = attn_fwd(unit, segment_ids, q_all, kv_all, parts, key_heads)
    (attn,) = exchange((o_all,), ("class",), count, parts, 1, "send_attn")
    attn = attn.reshape(sequences, key_heads * group * HEAD_DIM, rows_here)
    attn_other = swap(attn)

    out_sum = ein("sep,ed->spd", attn, output_matrix) + ein("sep,ed->spd", attn_other, output_matrix_other)
    h_out = ein("sep,re->spr", attn, output_input_factor) + ein("sep,re->spr", attn_other, output_input_other)
    h_out = (h_out * pick).astype(BF)
    mid = x + (out_sum + 2.0 * ein("spr,rd->spd", h_out, output_output_factor))
    n2 = norm_rows(mid, ffn_gain).astype(BF)

    halves = []
    cut = sequences // 2
    for part in (slice(0, cut), slice(cut, sequences)):
        flat = lambda a: a[part].reshape(-1, a.shape[-1])
        mask = jnp.broadcast_to(pick[part], (cut, rows_here, stacked)).reshape(-1, stacked)
        down, back, gb_gate, gb_up, ga_down = ffn(
            flat(n2), flat(output_cotangent), mask, gate_input_factor, up_input_factor, down_output_factor,
            gate_matrix, up_matrix, down_matrix, gate_output_factor, up_output_factor, down_input_factor,
        )
        shape = lambda a: a.reshape(cut, rows_here, -1).astype(F32)
        halves.append((shape(down), shape(swap(down)), shape(back), shape(swap(back)), gb_gate, gb_up, ga_down))
    gb_gate, gb_up, ga_down = (halves[0][i].astype(F32) + halves[1][i].astype(F32) for i in (4, 5, 6))

    def mine(a):
        return lax.dynamic_slice_in_dim(a, half * (model_width // 2), model_width // 2, a.ndim - 1)

    def grad(hidden, rows):
        return ein("spr,spe->re", hidden, rows)

    back = jnp.concatenate([h[2] + h[3] for h in halves], axis=0)
    dh_gate = (back[..., model_width : model_width + stacked] * pick).astype(BF)
    dh_up = (back[..., model_width + stacked :] * pick).astype(BF)
    d_n2 = back[..., :model_width] + ein("spr,rd->spd", dh_gate, gate_input_factor)
    d_n2 = d_n2 + ein("spr,rd->spd", dh_up, up_input_factor)
    d_mid = output_cotangent.astype(F32) + norm_rows_back(mid, ffn_gain, d_n2)
    d_branch = d_mid.astype(BF)
    dh_out = (2.0 * ein("spd,rd->spr", d_branch, output_output_factor) * pick).astype(BF)
    d_attn = ein("spd,ed->sep", d_branch, output_matrix) + ein("spr,re->sep", dh_out, output_input_factor)
    d_attn = d_attn.astype(BF).reshape(units, group * HEAD_DIM, rows_here)
    (do_all,) = exchange((d_attn,), ("class",), count, parts, 2, "send_d_attn")
    dq_all, dkv_all = attn_bwd(unit, segment_ids, q_all, kv_all, do_all, o_wide, lse, parts, key_heads)
    dq, dkv = exchange((dq_all, dkv_all), ("class", "full"), count, parts, 3, "send_dqkv")

    down = jnp.concatenate([h[0] + h[1] for h in halves], axis=0)
    h_down = (down[..., model_width:] * pick).astype(BF)
    block_result = mid + (down[..., :model_width] + 2.0 * ein("spr,rd->spd", h_down, down_output_factor))
    n2_mine, cot_mine, branch_mine = mine(n2), mine(output_cotangent), mine(d_branch)
    first = [
        2.0 * grad(h_down, cot_mine),
        grad(dh_gate, n2_mine),
        grad(dh_up, n2_mine),
        2.0 * grad(h_out, branch_mine),
        ein("spr,sep->re", dh_out, attn),
        gb_gate, gb_up, ga_down,
    ]
    first = reduce_scatter_rows(jnp.concatenate(first, axis=1), count)

    dq = dq.reshape(sequences, -1, rows_here)
    dkv = dkv.reshape(sequences, key_heads, parts, 2, HEAD_DIM, rows_here)
    dkv = jnp.sum(dkv.astype(F32), axis=2).astype(BF)
    d_v_pre = dkv[:, :, 1].reshape(sequences, -1, rows_here)
    d_q_pre = head_prepare_back(q_pre, q_gain, tables, dq)
    d_k_pre = head_prepare_back(k_pre, k_gain, tables, dkv[:, :, 0].reshape(sequences, -1, rows_here))
    partial = (
        ein("sep,de->spd", d_q_pre, query_matrix)
        + ein("sep,de->spd", d_k_pre, key_matrix)
        + ein("sep,de->spd", d_v_pre, value_matrix)
    )
    partial = jnp.concatenate(
        [
            partial,
            2.0 * ein("sep,re->spr", d_q_pre, query_output_factor),
            2.0 * ein("sep,re->spr", d_k_pre, key_output_factor),
            2.0 * ein("sep,re->spr", d_v_pre, value_output_factor),
        ],
        axis=-1,
    ).astype(BF)
    whole = partial.astype(F32) + swap(partial).astype(F32)
    dh_query, dh_key, dh_value = (
        (whole[..., model_width + i * stacked : model_width + (i + 1) * stacked] * pick).astype(BF) for i in range(3)
    )
    d_n1 = whole[..., :model_width] + ein("spr,rd->spd", dh_query, query_input_factor)
    d_n1 = d_n1 + ein("spr,rd->spd", dh_key, key_input_factor)
    d_n1 = d_n1 + ein("spr,rd->spd", dh_value, value_input_factor)
    input_grad = (d_mid + norm_rows_back(x, attn_gain, d_n1)).astype(BF)
    n1_mine = mine(n1)
    second = [
        grad(dh_query, n1_mine),
        grad(dh_key, n1_mine),
        grad(dh_value, n1_mine),
        2.0 * ein("spr,sep->re", h_query, d_q_pre),
        2.0 * ein("spr,sep->re", h_key, d_k_pre),
        2.0 * ein("spr,sep->re", h_value, d_v_pre),
    ]
    second = reduce_scatter_rows(jnp.concatenate(second, axis=1), count)

    w = model_width // 2
    shared = jnp.concatenate([first[:, : 4 * w], second[:, : 3 * w]], axis=1)
    other = swap(shared)
    both = jnp.where(half == 0, jnp.stack([shared, other], 1), jnp.stack([other, shared], 1))
    gb_down, ga_gate, ga_up, gb_out, ga_query, ga_key, ga_value = (
        both[:, :, i * w : (i + 1) * w].reshape(-1, model_width) for i in range(7)
    )
    units_here = gate_matrix.shape[1]
    qw, kw = query_matrix.shape[1], key_matrix.shape[1]
    ga_out, gb_gate, gb_up, ga_down = jnp.split(first[:, 4 * w :], [qw, qw + units_here, qw + 2 * units_here], axis=1)
    gb_query, gb_key, gb_value = jnp.split(second[:, 3 * w :], [qw, qw + kw], axis=1)
    return (
        block_result.astype(BF), input_grad, ga_query, gb_query, ga_key, gb_key, ga_value, gb_value,
        ga_out, gb_out, ga_gate, gb_gate, ga_up, gb_up, ga_down, gb_down,
    )


def solution(mesh):
    rows, whole, columns = P(None, "ctx", None), P(), P(None, "tp")
    owned, owned_half = P("ctx", None), P("ctx", "tp")
    return jax.shard_map(
        local,
        mesh=mesh,
        in_specs=(rows, rows) + (whole,) * 6
        + (columns, columns, columns, P("tp", None), columns, columns, P("tp", None))
        + (whole, columns) * 3 + (columns, whole) + (whole, columns) * 2 + (columns, whole),
        out_specs=(
            rows, rows, owned, owned_half, owned, owned_half, owned, owned_half,
            owned_half, owned, owned, owned_half, owned, owned_half, owned_half, owned,
        ),
        check_vma=False,
    )
```

time: 1610 us -> 510 us (0.32)
  waiting for transfers between devices: 1320 us -> 120 us
  Pallas kernels: 0 us -> 225 us
  matrix products: 187 us -> 35 us
  starting transfers between devices: 1.51 us -> 26.2 us
    reduce_scatter x12 -> x0, waiting for transfers between devices: 908 us -> none  [the longest x1 275 us: local(): lax.psum_scatter(key_terms, 'ctx', scatter_dimension=0, tiled=True)]
    pallas_call x0 -> x8, Pallas kernels: none -> 225 us  [the longest x4 127 us: exchange(): pl.pallas_call(functools.partial(exchange_kernel, count, parts, kinds), o...]
    psum x3 -> x0, waiting for transfers between devices: 207 us -> none  [the longest x1 78 us: local(): lax.psum(part_out.astype(jnp.bfloat16), 'tp').astype(jnp.float32)]
    dot_general x63 -> x40, matrix products: 187 us -> 35 us  [ein(): return jnp.einsum(spec, a, b, preferred_element_type=F32)]
    unnamed x19 -> x0, waiting for transfers between devices: 125 us -> none
    ppermute x0 -> x17, waiting for transfers between devices: none -> 120 us  [the longest x9 95.9 us: swap(): return lax.ppermute(values, 'tp', [(0, 1), (1, 0)])]
    all_gather x2 -> x0, waiting for transfers between devices: 78.3 us -> none  [the longest x1 47.6 us: local(): keys_part = lax.all_gather(keys_low, 'ctx', axis=1, tiled=True)]
    ppermute x0 -> x17, starting transfers between devices: none -> 26.2 us  [the longest x8 13.9 us: reduce_scatter_rows(): lax.ppermute(sent, 'ctx', [(i, i ^ bit) for i in range(count)]).astype(F32)]
  transfers between devices with their start and end apart: 18 -> 17, of which waited for: 18 -> 10; matrix products, arithmetic and copies ran while one was open for 7% -> 14% of each run, Pallas kernels for 0% -> 21%
where the time goes in v1:
time: 510 us; the launch traced here: 501 us
  Pallas kernels  225 us (44%)
  waiting for transfers between devices  120 us (24%)
  local copies, waits for them, and re-layouts  58.7 us (12%)
  matrix products  35 us (7%)
  other arithmetic  33.8 us (7%)
  starting transfers between devices  26.2 us (5%)
    pallas_call x4, Pallas kernels, exchange(): pl.pallas_call(functools.partial(exchange_kernel, count, parts, kinds), o...  127 us
    ppermute x9, waiting for transfers between devices, swap(): return lax.ppermute(values, 'tp', [(0, 1), (1, 0)])  95.9 us
    pallas_call x2, Pallas kernels, ffn(): pl.pallas_call(functools.partial(ffn_kernel, chunk), grid=(units // tile,...  65.2 us
    dot_general x40, matrix products, ein(): return jnp.einsum(spec, a, b, preferred_element_type=F32)  35 us
    ppermute x8, waiting for transfers between devices, reduce_scatter_rows(): lax.ppermute(sent, 'ctx', [(i, i ^ bit) for i in range(count)]).astype(F32)  24 us
    pallas_call x1, Pallas kernels, attn_bwd(): pl.pallas_call(functools.partial(attn_bwd_kernel, stride, group, units_pe...  20.1 us
    unnamed x202, local copies, waits for them, and re-layouts  15.8 us
    ppermute x8, starting transfers between devices, reduce_scatter_rows(): lax.ppermute(sent, 'ctx', [(i, i ^ bit) for i in range(count)]).astype(F32)  13.9 us
  transfers between devices with their start and end apart: 17, of which 10 were waited for; matrix products, arithmetic and copies ran while one was open for 14% of the time, Pallas kernels for 21%

profile of v1, /device:TPU:0, one launch (start us, length us, event | category | flops | bytes accessed | tf_op | source)
XLA Modules:
  0.0 500.6 jit_solution(4801135405482812618)
XLA Ops:
  0.7 3.0 collective-permute-start.1
  3.7 1.9 fusion.17
  11.2 3.1 copy.116
  14.3 1.6 multiply_reduce_fusion.3
  17.1 2.7 fusion.53
  19.8 1.6 fusion.52
  24.7 3.1 multiply_multiply_fusion
  31.4 1.6 subtract_convert_fusion
  34.0 30.4 %send_qkv.1 = (bf16[16,192,128]{2,1,0:T(8,128)(2,1)}, bf16[16,128,128]{2,1,0:T(8,128)(2,1)}) custom-call(bf16[16,192,128]{2,1,0:T(8,128)(2,1)} %bitcast.309, bf16[16,128,128]{2,1,0:T(8,128)(2,1)} %pad_maximum_fusion.3.refs_1_), custom_call_target="tpu_custom_call" | custom-call | tf_op jit(solution)/shard_map/send_qkv/pallas_call | solution.py:410
  65.0 12.0 %attention_forward.1 = (bf16[16,192,128]{2,1,0:T(8,128)(2,1)}, f32[16,192,128]{2,1,0:T(8,128)}, f32[8,8,768]{2,1,0:T(8,128)}) custom-call(s32[2]{0:T(128)} %pad_add_fusion.unit_ref, s32[4,2048]{1,0:T(4,128)} %seg_smem.3, s32[4,16,1,128]{3,2,1,0:T(1,128)} %reshape.362.seg_rows, bf16[16,192,128]{2,1,0:T(8,128)(2,1)} %get-tuple-element.35.q_ref, ...), custom_call_target="tpu_custom_call" | custom-call | tf_op jit(solution)/shard_map/attention_forward/pallas_call | solution.py:188
  77.0 28.7 %send_attn.1 = bf16[16,192,128]{2,1,0:T(8,128)(2,1)} custom-call(bf16[16,192,128]{2,1,0:T(8,128)(2,1)} %get-tuple-element.37.refs_0_), custom_call_target="tpu_custom_call" | custom-call | tf_op jit(solution)/shard_map/send_attn/pallas_call | solution.py:410
  105.7 2.4 copy.120
  110.1 3.2 fusion.25
  115.0 16.6 %collective-permute-done.2 = bf16[128,768]{1,0:T(8,128)(2,1)S(1)} collective-permute-done((bf16[128,768]{1,0:T(8,128)(2,1)S(1)}, bf16[128,768]{1,0:T(8,128)(2,1)S(1)}, u32[]{:S(2)}, u32[]{:S(2)}) %collective-permute-start.2) | collective-permute-done | bytes 196640 | tf_op jit(solution)/shard_map/ppermute | solution.py:474
  132.0 3.2 convolution_add_fusion.3
  140.2 32.3 %feed_forward.2 = (bf16[256,1664]{1,0:T(8,128)(2,1)}, bf16[256,1792]{1,0:T(8,128)(2,1)}, bf16[128,3456]{1,0:T(8,128)(2,1)}, bf16[128,3456]{1,0:T(8,128)(2,1)}, bf16[128,3456]{1,0:T(8,128)(2,1)}) custom-call(bf16[256,1536]{1,0:T(8,128)(2,1)} %bitcast.314, bf16[256,1536]{1,0:T(8,128)(2,1)} %bitcast.312, f32[256,128]{1,0:T(8,128)} %bitcast.326, ...), custom_call_target="tpu_custom_call" | custom-call | tf_op jit(solution)/shard_map/feed_forward/pallas_call | solution.py:310
  173.8 32.9 %feed_forward.3 = (bf16[256,1664]{1,0:T(8,128)(2,1)}, bf16[256,1792]{1,0:T(8,128)(2,1)}, bf16[128,3456]{1,0:T(8,128)(2,1)}, bf16[128,3456]{1,0:T(8,128)(2,1)}, bf16[128,3456]{1,0:T(8,128)(2,1)}) custom-call(bf16[256,1536]{1,0:T(8,128)(2,1)} %bitcast.313, bf16[256,1536]{1,0:T(8,128)(2,1)} %bitcast.311, f32[256,128]{1,0:T(8,128)} %bitcast.327, ...), custom_call_target="tpu_custom_call" | custom-call | tf_op jit(solution)/shard_map/feed_forward/pallas_call | solution.py:310
  206.7 1.5 collective-permute-start.4
  209.1 2.0 copy.131
  213.7 2.0 mul.497
  215.7 3.0 copy.126
  224.2 1.6 convert_add_fusion.5
  225.8 3.2 collective-permute-done.4
  230.3 18.2 %collective-permute-done.6 = bf16[256,1792]{1,0:T(8,128)(2,1)S(1)} collective-permute-done((bf16[256,1792]{1,0:T(8,128)(2,1)}, bf16[256,1792]{1,0:T(8,128)(2,1)S(1)}, u32[]{:S(2)}, u32[]{:S(2)}) %collective-permute-start.6) | collective-permute-done | bytes 917536 | tf_op jit(solution)/shard_map/ppermute | solution.py:474
  248.7 16.9 %collective-permute-done.5 = bf16[256,1792]{1,0:T(8,128)(2,1)S(1)} collective-permute-done((bf16[256,1792]{1,0:T(8,128)(2,1)}, bf16[256,1792]{1,0:T(8,128)(2,1)S(1)}, u32[]{:S(2)}, u32[]{:S(2)}) %collective-permute-start.5) | collective-permute-done | bytes 917536 | tf_op jit(solution)/shard_map/ppermute | solution.py:474
  276.5 2.3 copy.122
  278.7 23.4 %send_d_attn.1.do_ref = bf16[16,192,128]{2,1,0:T(8,128)(2,1)} custom-call(bf16[16,192,128]{2,1,0:T(8,128)(2,1)} %bitcast.310), custom_call_target="tpu_custom_call" | custom-call | tf_op jit(solution)/shard_map/send_d_attn/pallas_call | solution.py:410
  302.2 20.1 %attention_backward.1 = (bf16[16,192,128]{2,1,0:T(8,128)(2,1)}, bf16[16,128,128]{2,1,0:T(8,128)(2,1)}) custom-call(s32[2]{0:T(128)} %pad_add_fusion.unit_ref, s32[4,2048]{1,0:T(4,128)} %seg_smem.3, s32[4,16,1,128]{3,2,1,0:T(1,128)} %reshape.362.seg_rows, bf16[16,192,128]{2,1,0:T(8,128)(2,1)} %get-tuple-element.35.q_ref, ...), custom_call_target="tpu_custom_call" | custom-call | tf_op jit(solution)/shard_map/attention_backward/pallas_call | solution.py:211
  322.3 44.8 %send_dqkv.1 = (bf16[16,192,128]{2,1,0:T(8,128)(2,1)}, bf16[16,128,128]{2,1,0:T(8,128)(2,1)}) custom-call(bf16[16,192,128]{2,1,0:T(8,128)(2,1)} %get-tuple-element.44.refs_0_, bf16[16,128,128]{2,1,0:T(8,128)(2,1)} %get-tuple-element.45.refs_1_), custom_call_target="tpu_custom_call" | custom-call | tf_op jit(solution)/shard_map/send_dqkv/pallas_call | solution.py:410
  372.0 2.1 copy.130
  374.1 2.0 copy.128
  381.6 3.0 copy.125
  384.7 3.0 copy.123
  387.7 3.4 multiply_convert_fusion.1
  402.9 1.5 collective-permute-start.7
  405.1 1.8 fusion.8
  407.3 2.9 collective-permute-start.9
  410.3 37.9 %collective-permute-done.7 = bf16[4,128,1920]{2,1,0:T(8,128)(2,1)S(1)} collective-permute-done((bf16[4,128,1920]{2,1,0:T(8,128)(2,1)S(1)}, bf16[4,128,1920]{2,1,0:T(8,128)(2,1)S(1)}, u32[]{:S(2)}, u32[]{:S(2)}) %collective-permute-start.7) | collective-permute-done | bytes 1966112 | tf_op jit(solution)/shard_map/ppermute | solution.py:474
  455.0 3.0 collective-permute-start.13
  458.0 2.4 fusion.14
  460.4 3.4 collective-permute-done.13
  463.9 3.3 collective-permute-start.14
  467.5 3.3 collective-permute-done.14
  470.8 2.3 collective-permute-start.15
  473.1 7.9 %collective-permute-done.10 = bf16[2,8,14208]{2,1,0:T(8,128)(2,1)S(1)} collective-permute-done((bf16[2,8,14208]{2,1,0:T(8,128)(2,1)S(1)}, bf16[2,8,14208]{2,1,0:T(8,128)(2,1)S(1)}, u32[]{:S(2)}, u32[]{:S(2)}) %collective-permute-start.10) | collective-permute-done | bytes 454688 | tf_op jit(solution)/shard_map/ppermute | solution.py:487
  481.1 1.7 collective-permute-start.11
  484.1 9.4 %collective-permute-done.11 = bf16[1,8,14208]{2,1,0:T(8,128)(2,1)S(1)} collective-permute-done((bf16[1,8,14208]{2,1,0:T(8,128)(2,1)S(1)}, bf16[1,8,14208]{2,1,0:T(8,128)(2,1)S(1)}, u32[]{:S(2)}, u32[]{:S(2)}) %collective-permute-start.11) | collective-permute-done | bytes 227360 | tf_op jit(solution)/shard_map/ppermute | solution.py:487
  496.4 3.1 collective-permute-done.16
  (332 shorter events, 81.3 us)
Async XLA Ops:
  0.6 6.7 %copy-start = (bf16[1536,768]{1,0:T(8,128)(2,1)S(1)}, bf16[1536,768]{1,0:T(8,128)(2,1)}, u32[]{:S(2)}) copy-start(bf16[1536,768]{1,0:T(8,128)(2,1)} %param.37) | copy-start | bytes 7077892
  0.7 131.3 %collective-permute-start.1 = (bf16[768,1536]{1,0:T(8,128)(2,1)}, bf16[768,1536]{1,0:T(8,128)(2,1)}, u32[]{:S(2)}, u32[]{:S(2)}) collective-permute-start(bf16[768,1536]{1,0:T(8,128)(2,1)} %param.40), channel_id=1, source_target_pairs={{0,1},{1,0},{2,3},{3,2},{4,5},{5,4},{6,7},{7,6},{8,9},{9,8},{10,11... | collective-permute-start | bytes 7077896 | tf_op jit(solution)/shard_map/ppermute | solution.py:474
  3.7 5.1 %copy-start.99 = (s32[128]{0:T(128)}, s32[128]{0:T(128)S(1)}, u32[]{:S(2)}) copy-start(s32[128]{0:T(128)S(1)} %and_select_fusion) | copy-start | bytes 1540
  9.7 4.6 copy-start.59
  11.2 5.9 %copy-start.45 = (bf16[128,1536]{1,0:T(8,128)(2,1)S(1)}, bf16[128,1536]{1,0:T(8,128)(2,1)}, u32[]{:S(2)}) copy-start(bf16[128,1536]{1,0:T(8,128)(2,1)} %param.48) | copy-start | bytes 1179652
  17.1 4.3 copy-start.82
  17.1 4.9 copy-start.36
  24.6 4.9 copy-start.30
  24.6 3.3 copy-start.100
  24.6 4.0 copy-start.55
  24.6 4.0 copy-start.81
  24.7 4.1 copy-start.6
  24.7 4.1 copy-start.38
  65.0 43.7 %copy-start.72 = (bf16[128,768]{1,0:T(8,128)(2,1)S(1)}, bf16[128,768]{1,0:T(8,128)(2,1)}, u32[]{:S(2)}) copy-start(bf16[128,768]{1,0:T(8,128)(2,1)} %param.50) | copy-start | bytes 589828
  105.7 4.4 copy-start.18
  108.1 23.5 %collective-permute-start = (bf16[4,768,128]{1,2,0:T(8,128)(2,1)}, bf16[4,768,128]{1,2,0:T(8,128)(2,1)S(1)}, u32[]{:S(2)}, u32[]{:S(2)}) collective-permute-start(bf16[4,768,128]{1,2,0:T(8,128)(2,1)} %copy.120), channel_id=1, source_target_pairs={{0,1},{1,0},{2,3},{3,2},{4,5},{5,4},{6,7},{7,6},{8,9},{9,8},{10,11... | collective-permute-start | bytes 2359304 | tf_op jit(solution)/shard_map/ppermute | solution.py:474
  108.6 23.0 %collective-permute-start.2 = (bf16[128,768]{1,0:T(8,128)(2,1)S(1)}, bf16[128,768]{1,0:T(8,128)(2,1)S(1)}, u32[]{:S(2)}, u32[]{:S(2)}) collective-permute-start(bf16[128,768]{1,0:T(8,128)(2,1)S(1)} %copy-done.72), channel_id=1, source_target_pairs={{0,1},{1,0},{2,3},{3,2},{4,5},{5,4},{6,7},{7,6},{8,9},{9,8},{10,11... | collective-permute-start | bytes 589832 | tf_op jit(solution)/shard_map/ppermute | solution.py:474
  110.1 3.6 copy-start.19
  132.0 3.2 copy-start.53
  132.0 3.2 copy-start.13
  172.6 51.6 %collective-permute-start.3 = (bf16[256,1664]{1,0:T(8,128)(2,1)}, bf16[256,1664]{1,0:T(8,128)(2,1)}, u32[]{:S(2)}, u32[]{:S(2)}) collective-permute-start(bf16[256,1664]{1,0:T(8,128)(2,1)} %get-tuple-element.38), channel_id=1, source_target_pairs={{0,1},{1,0},{2,3},{3,2},{4,5},{5,4},{6,7},{7,6},{8,9},{9,8},{10,11... | collective-permute-start | bytes 2555912 | tf_op jit(solution)/shard_map/ppermute | solution.py:474
  206.7 22.3 %collective-permute-start.4 = (bf16[256,1664]{1,0:T(8,128)(2,1)}, bf16[256,1664]{1,0:T(8,128)(2,1)}, u32[]{:S(2)}, u32[]{:S(2)}) collective-permute-start(bf16[256,1664]{1,0:T(8,128)(2,1)} %get-tuple-element.39), channel_id=1, source_target_pairs={{0,1},{1,0},{2,3},{3,2},{4,5},{5,4},{6,7},{7,6},{8,9},{9,8},{10,11... | collective-permute-start | bytes 2555912 | tf_op jit(solution)/shard_map/ppermute | solution.py:474
  221.4 7.6 %copy-start.71 = (bf16[256,1664]{1,0:T(8,128)(2,1)S(1)}, bf16[256,1664]{1,0:T(8,128)(2,1)}, u32[]{:S(2)}) copy-start(bf16[256,1664]{1,0:T(8,128)(2,1)} %get-tuple-element.39) | copy-start | bytes 2555908
  222.2 26.4 %collective-permute-start.6 = (bf16[256,1792]{1,0:T(8,128)(2,1)}, bf16[256,1792]{1,0:T(8,128)(2,1)S(1)}, u32[]{:S(2)}, u32[]{:S(2)}) collective-permute-start(bf16[256,1792]{1,0:T(8,128)(2,1)} %get-tuple-element.41), channel_id=1, source_target_pairs={{0,1},{1,0},{2,3},{3,2},{4,5},{5,4},{6,7},{7,6},{8,9},{9,8},{10,11... | collective-permute-start | bytes 2752520 | tf_op jit(solution)/shard_map/ppermute | solution.py:474
  222.7 42.9 %collective-permute-start.5 = (bf16[256,1792]{1,0:T(8,128)(2,1)}, bf16[256,1792]{1,0:T(8,128)(2,1)S(1)}, u32[]{:S(2)}, u32[]{:S(2)}) collective-permute-start(bf16[256,1792]{1,0:T(8,128)(2,1)} %get-tuple-element.40), channel_id=1, source_target_pairs={{0,1},{1,0},{2,3},{3,2},{4,5},{5,4},{6,7},{7,6},{8,9},{9,8},{10,11... | collective-permute-start | bytes 2752520 | tf_op jit(solution)/shard_map/ppermute | solution.py:474
  225.8 40.6 %copy-start.22 = (f32[256,1664]{1,0:T(8,128)}, f32[256,1664]{1,0:T(8,128)S(1)}, u32[]{:S(2)}) copy-start(f32[256,1664]{1,0:T(8,128)S(1)} %convert_add_fusion.5) | copy-start | bytes 5111812
  225.8 22.7 %copy-start.64 = (bf16[256,1792]{1,0:T(8,128)(2,1)S(1)}, bf16[256,1792]{1,0:T(8,128)(2,1)}, u32[]{:S(2)}) copy-start(bf16[256,1792]{1,0:T(8,128)(2,1)} %get-tuple-element.41) | copy-start | bytes 2752516
  230.3 36.1 %copy-start.24 = (f32[256,1664]{1,0:T(8,128)}, f32[256,1664]{1,0:T(8,128)S(1)}, u32[]{:S(2)}) copy-start(f32[256,1664]{1,0:T(8,128)S(1)} %convert_add_fusion.4) | copy-start | bytes 5111812
  230.3 35.3 %copy-start.63 = (bf16[256,1792]{1,0:T(8,128)(2,1)S(1)}, bf16[256,1792]{1,0:T(8,128)(2,1)}, u32[]{:S(2)}) copy-start(bf16[256,1792]{1,0:T(8,128)(2,1)} %get-tuple-element.40) | copy-start | bytes 2752516
  248.7 18.4 %copy-start.8 = (f32[256,1792]{1,0:T(8,128)}, f32[256,1792]{1,0:T(8,128)S(1)}, u32[]{:S(2)}) copy-start(f32[256,1792]{1,0:T(8,128)S(1)} %convert_add_fusion.2) | copy-start | bytes 5505028
  248.7 17.1 %copy-start.35 = (bf16[128,1536]{1,0:T(8,128)(2,1)S(1)}, bf16[128,1536]{1,0:T(8,128)(2,1)}, u32[]{:S(2)}) copy-start(bf16[128,1536]{1,0:T(8,128)(2,1)} %ag_ref.3) | copy-start | bytes 1179652
  387.7 3.4 copy-start.75
  387.7 3.8 copy-start.21
  387.7 3.8 copy-start.50
  387.7 4.2 copy-start.11
  387.7 4.4 copy-start.27
  397.8 9.1 %collective-permute-start.8 = (bf16[8,8,14208]{2,1,0:T(8,128)(2,1)S(1)}, bf16[8,8,14208]{2,1,0:T(8,128)(2,1)S(1)}, u32[]{:S(2)}, u32[]{:S(2)}) collective-permute-start(bf16[8,8,14208]{2,1,0:T(8,128)(2,1)S(1)} %fusion.31), channel_id=1, source_target_pairs={{0,2},{2,0},{4,6},{6,4},{8,10},{10,8},{12,14},{14,12},{16,18},{18,... | collective-permute-start | bytes 5455880 | tf_op jit(solution)/shard_map/ppermute | solution.py:487
  402.9 45.3 %collective-permute-start.7 = (bf16[4,128,1920]{2,1,0:T(8,128)(2,1)S(1)}, bf16[4,128,1920]{2,1,0:T(8,128)(2,1)S(1)}, u32[]{:S(2)}, u32[]{:S(2)}) collective-permute-start(bf16[4,128,1920]{2,1,0:T(8,128)(2,1)S(1)} %pad_maximum_fusion), channel_id=1, source_target_pairs={{0,1},{1,0},{2,3},{3,2},{4,5},{5,4},{6,7},{7,6},{8,9},{9,8},{10,11... | collective-permute-start | bytes 5898248 | tf_op jit(solution)/shard_map/ppermute | solution.py:474
  407.3 41.3 %copy-start.47 = (bf16[128,1536]{1,0:T(8,128)(2,1)S(1)}, bf16[128,1536]{1,0:T(8,128)(2,1)}, u32[]{:S(2)}) copy-start(bf16[128,1536]{1,0:T(8,128)(2,1)} %param.46) | copy-start | bytes 1179652
  407.3 59.8 %collective-permute-start.9 = (bf16[4,8,14208]{2,1,0:T(8,128)(2,1)S(1)}, bf16[4,8,14208]{2,1,0:T(8,128)(2,1)S(1)}, u32[]{:S(2)}, u32[]{:S(2)}) collective-permute-start(bf16[4,8,14208]{2,1,0:T(8,128)(2,1)S(1)} %fusion.61), channel_id=1, source_target_pairs={{0,4},{2,6},{4,0},{6,2},{8,12},{10,14},{12,8},{14,10},{16,20},{18,... | collective-permute-start | bytes 2727944 | tf_op jit(solution)/shard_map/ppermute | solution.py:487
  452.9 1.9 collective-permute-start.12
  453.5 4.5 copy-start.16
  455.0 8.8 %collective-permute-start.13 = (bf16[4,8,3584]{2,1,0:T(8,128)(2,1)S(1)}, bf16[4,8,3584]{2,1,0:T(8,128)(2,1)S(1)}, u32[]{:S(2)}, u32[]{:S(2)}) collective-permute-start(bf16[4,8,3584]{2,1,0:T(8,128)(2,1)S(1)} %fusion.103), channel_id=1, source_target_pairs={{0,4},{2,6},{4,0},{6,2},{8,12},{10,14},{12,8},{14,10},{16,20},{18,... | collective-permute-start | bytes 688136 | tf_op jit(solution)/shard_map/ppermute | solution.py:487
  463.9 6.9 %collective-permute-start.14 = (bf16[2,8,3584]{2,1,0:T(8,128)(2,1)S(1)}, bf16[2,8,3584]{2,1,0:T(8,128)(2,1)S(1)}, u32[]{:S(2)}, u32[]{:S(2)}) collective-permute-start(bf16[2,8,3584]{2,1,0:T(8,128)(2,1)S(1)} %fusion.110), channel_id=1, source_target_pairs={{0,8},{2,10},{4,12},{6,14},{8,0},{10,2},{12,4},{14,6},{16,24},{18,... | collective-permute-start | bytes 344072 | tf_op jit(solution)/shard_map/ppermute | solution.py:487
  467.4 13.6 %collective-permute-start.10 = (bf16[2,8,14208]{2,1,0:T(8,128)(2,1)S(1)}, bf16[2,8,14208]{2,1,0:T(8,128)(2,1)S(1)}, u32[]{:S(2)}, u32[]{:S(2)}) collective-permute-start(bf16[2,8,14208]{2,1,0:T(8,128)(2,1)S(1)} %fusion.74), channel_id=1, source_target_pairs={{0,8},{2,10},{4,12},{6,14},{8,0},{10,2},{12,4},{14,6},{16,24},{18,... | collective-permute-start | bytes 1363976 | tf_op jit(solution)/shard_map/ppermute | solution.py:487
  470.8 12.0 %collective-permute-start.15 = (bf16[1,8,3584]{2,1,0:T(8,128)(2,1)S(1)}, bf16[1,8,3584]{2,1,0:T(8,128)(2,1)S(1)}, u32[]{:S(2)}, u32[]{:S(2)}) collective-permute-start(bf16[1,8,3584]{2,1,0:T(8,128)(2,1)S(1)} %dynamic-slice_convert_fusion.4), channel_id=1, source_target_pairs={{0,16},{2,18},{4,20},{6,22},{8,24},{10,26},{12,28},{14,30},{16,0},... | collective-permute-start | bytes 172040 | tf_op jit(solution)/shard_map/ppermute | solution.py:487
  481.1 12.4 %collective-permute-start.11 = (bf16[1,8,14208]{2,1,0:T(8,128)(2,1)S(1)}, bf16[1,8,14208]{2,1,0:T(8,128)(2,1)S(1)}, u32[]{:S(2)}, u32[]{:S(2)}) collective-permute-start(bf16[1,8,14208]{2,1,0:T(8,128)(2,1)S(1)} %dynamic-slice_convert_fusion.3), channel_id=1, source_target_pairs={{0,16},{2,18},{4,20},{6,22},{8,24},{10,26},{12,28},{14,30},{16,0},... | collective-permute-start | bytes 681992 | tf_op jit(solution)/shard_map/ppermute | solution.py:487
  493.6 6.0 %collective-permute-start.16 = (f32[8,5376]{1,0:T(8,128)S(1)}, f32[8,5376]{1,0:T(8,128)S(1)}, u32[]{:S(2)}, u32[]{:S(2)}) collective-permute-start(f32[8,5376]{1,0:T(8,128)S(1)} %get-tuple-element.83), channel_id=1, source_target_pairs={{0,1},{1,0},{2,3},{3,2},{4,5},{5,4},{6,7},{7,6},{8,9},{9,8},{10,11... | collective-permute-start | bytes 516104 | tf_op jit(solution)/shard_map/ppermute | solution.py:474
  (70 other events, 117.5 us)

commit v2 on v1

v2 whole, which is shorter than its diff:
```python
import functools, jax, jax.numpy as jnp
from jax import lax
from jax.experimental import pallas as pl
from jax.experimental.pallas import tpu as pltpu
from jax.sharding import PartitionSpec as P

HEAD_DIM = 64
LOG2E = 1.4426950408889634
KEY_TILE = 256


def tile_bounds(tile, stride, part):
    first = (2 * tile) * stride + part
    last = (2 * tile + 1) * stride + part
    return first, last


def allowed_pairs(seg_rows, seq, first, last, key_tile, group):
    lanes = lax.broadcasted_iota(jnp.int32, (1, 128), 1)
    q_pos = jnp.concatenate([first * 128 + lanes, last * 128 + lanes], axis=1)
    q_seg = jnp.concatenate(
        [seg_rows[block] for block in (first, last)], axis=1
    )
    k_seg = jnp.concatenate(
        [jnp.transpose(jnp.broadcast_to(seg_rows[2 * key_tile + b], (128, 128))) for b in (0, 1)], axis=0
    )
    k_seg = jnp.concatenate([k_seg, k_seg], axis=1)
    k_pos = key_tile * 256 + lax.broadcasted_iota(jnp.int32, (256, 256), 0)
    allowed = (k_seg == jnp.broadcast_to(q_seg, (256, 256))) & (k_pos <= jnp.broadcast_to(q_pos, (256, 256)))
    return jnp.concatenate([allowed] * group, axis=1)


def load_segments(seg_ref, seq, seg_rows):
    sequences, length = seg_ref.shape
    number = lax.broadcasted_iota(jnp.int32, (sequences, length), 0)
    row = jnp.sum(jnp.where(number == seq, seg_ref[...], 0), axis=0, keepdims=True)
    for b in range(length // 128):
        seg_rows[b] = row[:, b * 128 : (b + 1) * 128]


def tile_kind(seg_smem, seq, first, last, key_tile):
    key_low = seg_smem[seq, key_tile * 256]
    key_high = seg_smem[seq, key_tile * 256 + 255]
    q_low = seg_smem[seq, first * 128]
    q_high = seg_smem[seq, last * 128 + 127]
    needed = key_high >= q_low
    plain = (key_low == q_high) & (2 * key_tile + 1 < first)
    return needed, plain


def heads_side_by_side(ref, tile, group, offset=0):
    return jnp.concatenate(
        [ref[2 * tile + b, offset + h * HEAD_DIM : offset + (h + 1) * HEAD_DIM, :] for h in range(group) for b in (0, 1)], axis=1
    )


def attn_fwd_kernel(stride, group, units_per_seq, seg_smem, seg_ref, q_ref, kv_ref, o_ref, of_ref, lse_ref, kb, vt, acc, seg_rows):
    unit, part = lax.axis_index("ctx") // stride, lax.rem(lax.axis_index("ctx"), stride)
    seq = unit // units_per_seq
    load_segments(seg_ref, seq, seg_rows)
    key_tiles = kv_ref.shape[0] // 2
    q_tiles = q_ref.shape[0] // 2
    width = group * 256

    def load(j, _):
        for b in (0, 1):
            kb[j, b * 128 : (b + 1) * 128, :] = jnp.transpose(kv_ref[2 * j + b, :HEAD_DIM, :])
            vt[j, :HEAD_DIM, b * 128 : (b + 1) * 128] = kv_ref[2 * j + b, HEAD_DIM:, :]
        vt[j, HEAD_DIM:, :] = jnp.ones((16, 256), jnp.bfloat16)
        return 0

    lax.fori_loop(0, key_tiles, load, 0)

    def q_step(i, _):
        first, last = tile_bounds(i, stride, part)
        qt = heads_side_by_side(q_ref, i, group)
        acc[...] = jnp.zeros_like(acc)

        def k_step(j, _):
            needed, plain = tile_kind(seg_smem, seq, first, last, j)

            def weigh(masked):
                s = jnp.dot(kb[j], qt, preferred_element_type=jnp.float32)
                p = jnp.exp2(s * (LOG2E * HEAD_DIM**-0.5))
                if masked:
                    p = jnp.where(allowed_pairs(seg_rows, seq, first, last, j, group), p, 0.0)
                acc[...] += jnp.dot(vt[j], p.astype(jnp.bfloat16), preferred_element_type=jnp.float32)

            @pl.when(needed & plain)
            def _():
                weigh(False)

            @pl.when(needed & jnp.logical_not(plain))
            def _():
                weigh(True)

            return 0

        lax.fori_loop(0, last // 2 + 1, k_step, 0)
        total = acc[HEAD_DIM : HEAD_DIM + 1, :]
        lse_ref[i] = jnp.broadcast_to(jnp.log2(total), (8, width))
        out = acc[:HEAD_DIM, :] / total
        for h in range(group):
            for b in (0, 1):
                piece = out[:, h * 256 + b * 128 : h * 256 + (b + 1) * 128]
                of_ref[2 * i + b, h * HEAD_DIM : (h + 1) * HEAD_DIM, :] = piece
                o_ref[2 * i + b, h * HEAD_DIM : (h + 1) * HEAD_DIM, :] = piece.astype(jnp.bfloat16)
        return 0

    lax.fori_loop(0, q_tiles, q_step, 0)


def attn_bwd_kernel(
    stride, group, units_per_seq, seg_smem, seg_ref, q_ref, kv_ref, do_ref, of_ref, lse_ref,
    dq_ref, dkv_ref, qt, q3, dot_t, do3, delta, dqt, seg_rows,
):
    unit, part = lax.axis_index("ctx") // stride, lax.rem(lax.axis_index("ctx"), stride)
    seq = unit // units_per_seq
    load_segments(seg_ref, seq, seg_rows)
    key_tiles = kv_ref.shape[0] // 2
    q_tiles = q_ref.shape[0] // 2
    width = group * 256

    def load(i, _):
        for h in range(group):
            for b in (0, 1):
                rows = slice(h * HEAD_DIM, (h + 1) * HEAD_DIM)
                lanes = slice(h * 256 + b * 128, h * 256 + (b + 1) * 128)
                q = q_ref[2 * i + b, rows, :]
                g = do_ref[2 * i + b, rows, :]
                qt[i, :, lanes] = q
                q3[i, lanes, :] = jnp.transpose(q)
                dot_t[i, :, lanes] = g
                do3[i, lanes, :] = jnp.transpose(g)
                d = jnp.sum(g.astype(jnp.float32) * of_ref[2 * i + b, rows, :], axis=0, keepdims=True)
                delta[i, :, lanes] = jnp.broadcast_to(d, (8, 128))
        dqt[i] = jnp.zeros((HEAD_DIM, width), jnp.float32)
        return 0

    lax.fori_loop(0, q_tiles, load, 0)

    def k_step(j, _):
        kt = jnp.concatenate([kv_ref[2 * j + b, :HEAD_DIM, :] for b in (0, 1)], axis=1)
        vt = jnp.concatenate([kv_ref[2 * j + b, HEAD_DIM:, :] for b in (0, 1)], axis=1)
        kb = jnp.transpose(kt)
        vb = jnp.transpose(vt)

        def q_step(i, state):
            first, last = tile_bounds(i, stride, part)
            needed, plain = tile_kind(seg_smem, seq, first, last, j)

            def terms(masked, dk, dv):
                s = jnp.dot(kb, qt[i], preferred_element_type=jnp.float32)
                p = jnp.exp2(s * (LOG2E * HEAD_DIM**-0.5) - lse_ref[i, 0:1, :])
                if masked:
                    p = jnp.where(allowed_pairs(seg_rows, seq, first, last, j, group), p, 0.0)
                dp = jnp.dot(vb, dot_t[i], preferred_element_type=jnp.float32)
                ds = (p * (dp - delta[i, 0:1, :])).astype(jnp.bfloat16)
                dv = dv + jnp.dot(p.astype(jnp.bfloat16), do3[i], preferred_element_type=jnp.float32)
                dk = dk + jnp.dot(ds, q3[i], preferred_element_type=jnp.float32)
                dqt[i] += jnp.dot(kt, ds, preferred_element_type=jnp.float32)
                return dk, dv

            kind = jnp.where(needed, jnp.where(plain, 1, 2), 0)
            return lax.switch(
                kind, [lambda a, b: (a, b), functools.partial(terms, False), functools.partial(terms, True)], *state
            )

        zero = jnp.zeros((256, HEAD_DIM), jnp.float32)
        start = jnp.maximum((2 * j - part + stride - 1) // stride, 0) // 2
        dk, dv = lax.fori_loop(start, q_tiles, q_step, (zero, zero))
        for b in (0, 1):
            rows = slice(b * 128, (b + 1) * 128)
            dkv_ref[2 * j + b, :HEAD_DIM, :] = jnp.transpose(dk[rows] * HEAD_DIM**-0.5).astype(jnp.bfloat16)
            dkv_ref[2 * j + b, HEAD_DIM:, :] = jnp.transpose(dv[rows]).astype(jnp.bfloat16)
        return 0

    lax.fori_loop(0, key_tiles, k_step, 0)

    def store(i, _):
        for h in range(group):
            for b in (0, 1):
                piece = dqt[i, :, h * 256 + b * 128 : h * 256 + (b + 1) * 128]
                dq_ref[2 * i + b, h * HEAD_DIM : (h + 1) * HEAD_DIM, :] = (piece * HEAD_DIM**-0.5).astype(jnp.bfloat16)
        return 0

    lax.fori_loop(0, q_tiles, store, 0)


SMEM = pl.BlockSpec(memory_space=pltpu.SMEM)
VM = pl.BlockSpec(memory_space=pltpu.VMEM)


def attn_fwd(segs, q, kv, stride, units_per_seq):
    blocks, qrows, _ = q.shape
    group = qrows // HEAD_DIM
    tiles, ktiles, width = blocks // 2, kv.shape[0] // 2, group * 256
    return pl.pallas_call(
        functools.partial(attn_fwd_kernel, stride, group, units_per_seq),
        out_shape=(
            jax.ShapeDtypeStruct(q.shape, jnp.bfloat16),
            jax.ShapeDtypeStruct(q.shape, jnp.float32),
            jax.ShapeDtypeStruct((tiles, 8, width), jnp.float32),
        ),
        in_specs=[SMEM, VM, VM, VM],
        out_specs=(VM, VM, VM),
        scratch_shapes=[
            pltpu.VMEM((ktiles, 256, HEAD_DIM), jnp.bfloat16),
            pltpu.VMEM((ktiles, HEAD_DIM + 16, 256), jnp.bfloat16),
            pltpu.VMEM((HEAD_DIM + 16, width), jnp.float32),
            pltpu.VMEM((kv.shape[0], 1, 128), jnp.int32),
        ],
        compiler_params=pltpu.CompilerParams(vmem_limit_bytes=56 * 2**20),
        cost_estimate=pl.CostEstimate(flops=2 * 128 * blocks * qrows * kv.shape[0] * 128, bytes_accessed=4 * q.size, transcendentals=0),
        name="attention_forward",
    )(segs, segs, q, kv)


def attn_bwd(segs, q, kv, do, of, lse, stride, units_per_seq):
    blocks, qrows, _ = q.shape
    group = qrows // HEAD_DIM
    tiles, ktiles, width = blocks // 2, kv.shape[0] // 2, group * 256
    return pl.pallas_call(
        functools.partial(attn_bwd_kernel, stride, group, units_per_seq),
        out_shape=(jax.ShapeDtypeStruct(q.shape, jnp.bfloat16), jax.ShapeDtypeStruct(kv.shape, jnp.bfloat16)),
        in_specs=[SMEM, VM, VM, VM, VM, VM, VM],
        out_specs=(VM, VM),
        scratch_shapes=[
            pltpu.VMEM((tiles, HEAD_DIM, width), jnp.bfloat16),
            pltpu.VMEM((tiles, width, HEAD_DIM), jnp.bfloat16),
            pltpu.VMEM((tiles, HEAD_DIM, width), jnp.bfloat16),
            pltpu.VMEM((tiles, width, HEAD_DIM), jnp.bfloat16),
            pltpu.VMEM((tiles, 8, width), jnp.float32),
            pltpu.VMEM((tiles, HEAD_DIM, width), jnp.float32),
            pltpu.VMEM((kv.shape[0], 1, 128), jnp.int32),
        ],
        compiler_params=pltpu.CompilerParams(vmem_limit_bytes=56 * 2**20),
        cost_estimate=pl.CostEstimate(flops=5 * 128 * blocks * qrows * kv.shape[0] * 128, bytes_accessed=4 * q.size, transcendentals=0),
        name="attention_backward",
    )(segs, segs, q, kv, do, of, lse)

RANK = 16
EPSILON = 1e-05
THETA_BASE = 1000000.0
BF = jnp.bfloat16
F32 = jnp.float32
NT = (((1,), (1,)), ((), ()))
BIG = pltpu.CompilerParams(vmem_limit_bytes=60 * 2**20)


def cost(rows, width, columns, products, moved):
    return pl.CostEstimate(flops=2 * products * rows * width * columns, bytes_accessed=moved, transcendentals=0)

ANYWHERE = pl.BlockSpec(memory_space=pl.ANY)


def mm(a, b):
    return jnp.dot(a, b, preferred_element_type=F32)


def mm_nt(a, b):
    return lax.dot_general(a, b, NT, preferred_element_type=F32)


def shape(dims, kind):
    return jax.ShapeDtypeStruct(dims, kind)


def own_rows(ref, variant):
    return ref[pl.ds(pl.multiple_of(variant * RANK, RANK), RANK), :]


def norm_back(u, gain, c):
    scale = lax.rsqrt(jnp.mean(u * u, axis=-1, keepdims=True) + EPSILON)
    y = u * scale
    w = c * gain
    return scale * (w - y * jnp.mean(w * y, axis=-1, keepdims=True))


def turn(values, cosine, sine):
    half = HEAD_DIM // 2
    a, b = values[:, :half], values[:, half:]
    return jnp.concatenate([a * cosine - b * sine, b * cosine + a * sine], axis=1)


def rank_halves(blocks):
    return jnp.concatenate([b[: RANK // 2] for b in blocks] + [b[RANK // 2 :] for b in blocks], axis=0)


def spread(blocks):
    wide = []
    for i, b in enumerate(blocks):
        zero = jnp.zeros_like(b)
        wide.append(jnp.concatenate([b if i == j else zero for j in range(len(blocks))], axis=1))
    return rank_halves(wide)


def column(ref):
    return jnp.transpose(jnp.broadcast_to(ref[...][None, :], (128, ref.shape[0])))


def project_kernel(
    variant, x_ref, gain_ref, wq, wk, wv, aq, ak, av, bq, bk, bv, qg_ref, kg_ref, cos_ref, sin_ref,
    n1_ref, h_ref, pre_ref, q_ref, kv_ref, ac_ref, bc_ref, gains_ref, pick_ref, n1_s,
):
    sequences, rows, width = x_ref.shape
    qw, kw = wq.shape[1], wk.shape[1]
    heads_q, heads_k = qw // HEAD_DIM, kw // HEAD_DIM
    cosine, sine = cos_ref[...], sin_ref[...]
    qg, kg = column(qg_ref), column(kg_ref)
    gains_ref[0], gains_ref[1] = qg, kg
    gain = gain_ref[...][None, :]
    for v in range(pick_ref.shape[0]):
        for s in range(sequences):
            pick_ref[v, s] = jnp.full((8, 128), jnp.where(variant[s] == v, 1.0, 0.0), F32)

    def prepare(t, gains):
        heads = t.reshape(t.shape[0] // HEAD_DIM, HEAD_DIM, rows)
        scale = lax.rsqrt(jnp.mean(heads * heads, axis=1, keepdims=True) + EPSILON)
        return turn(heads * scale * gains, cosine, sine).astype(BF)

    def pair(p, _):
        for i in (0, 1):
            x = x_ref[2 * p + i].astype(F32)
            scale = lax.rsqrt(jnp.mean(x * x, axis=-1, keepdims=True) + EPSILON)
            n1 = (x * scale * gain).astype(BF)
            n1_ref[2 * p + i] = n1
            n1_s[i * rows : (i + 1) * rows, :] = n1
        n1 = n1_s[...]
        base = [mm(n1, w[...]) for w in (wq, wk, wv)]
        for i in (0, 1):
            s = 2 * p + i
            v = variant[s]
            half = slice(i * rows, (i + 1) * rows)
            a = jnp.concatenate([own_rows(f, v) for f in (aq, ak, av)], axis=0)
            b = [own_rows(f, v) for f in (bq, bk, bv)]
            ac_ref[s] = a
            bc_ref[s] = jnp.concatenate(b, axis=1)
            h = mm_nt(n1_s[half, :], a).astype(BF)
            h_ref[s] = jnp.concatenate([h, jnp.zeros((rows, 128 - 3 * RANK), BF)], axis=1)
            h2 = h * 2
            q, k, val = (
                jnp.transpose(base[n][half] + mm(h2[:, n * RANK : (n + 1) * RANK], b[n])) for n in range(3)
            )
            pre_ref[s, :qw, :] = q
            pre_ref[s, qw:, :] = k
            group = heads_q // heads_k
            q = prepare(q, qg).reshape(heads_k, group * HEAD_DIM, rows)
            k = prepare(k, kg)
            val = val.astype(BF).reshape(heads_k, HEAD_DIM, rows)
            q_ref[pl.ds(s * heads_k, heads_k)] = q
            kv_ref[pl.ds(s * heads_k, heads_k), :HEAD_DIM, :] = k
            kv_ref[pl.ds(s * heads_k, heads_k), HEAD_DIM:, :] = val
        return 0

    lax.fori_loop(0, sequences // 2, pair, 0)


def project(variant, x, gain, weights, ins, outs, qg, kg, tables):
    sequences, rows, width = x.shape
    qw, kw = weights[0].shape[1], weights[1].shape[1]
    units = sequences * kw // HEAD_DIM
    return pl.pallas_call(
        project_kernel,
        out_shape=(
            shape(x.shape, BF), shape((sequences, rows, 128), BF), shape((sequences, qw + kw, rows), F32),
            shape((units, qw // kw * HEAD_DIM, rows), BF), shape((units, 2 * HEAD_DIM, rows), BF),
            shape((sequences, 3 * RANK, width), BF), shape((sequences, RANK, qw + 2 * kw), BF),
            shape((2, HEAD_DIM, rows), F32), shape((ins[0].shape[0] // RANK, sequences, 8, 128), F32),
        ),
        in_specs=[SMEM] + [VM] * 15,
        out_specs=(VM,) * 9,
        scratch_shapes=[pltpu.VMEM((2 * rows, width), BF)],
        compiler_params=BIG,
        cost_estimate=cost(sequences * rows, width, qw + 2 * kw, 1, 12 * sequences * rows * width),
        name="project",
    )(variant, x, gain, *weights, *ins, *outs, qg, kg, *tables)


def middle_kernel(variant, x_ref, gain_ref, attn, attn_x, wo, wo_x, ao, ao_x, bo, mid_ref, n2_ref, h_ref, lhs, lhs_x):
    sequences, rows, width = x_ref.shape

    def pair(p, _):
        for i in (0, 1):
            half = slice(i * rows, (i + 1) * rows)
            lhs[half, :] = jnp.transpose(attn[2 * p + i])
            lhs_x[half, :] = jnp.transpose(attn_x[2 * p + i])
        out = mm(lhs[...], wo[...]) + mm(lhs_x[...], wo_x[...])
        for i in (0, 1):
            s = 2 * p + i
            v = variant[s]
            half = slice(i * rows, (i + 1) * rows)
            h = (mm_nt(lhs[half, :], own_rows(ao, v)) + mm_nt(lhs_x[half, :], own_rows(ao_x, v))).astype(BF)
            h_ref[s] = jnp.concatenate([h, jnp.zeros((rows, 128 - RANK), BF)], axis=1)
            mid = x_ref[s].astype(F32) + (out[half] + mm(h * 2, own_rows(bo, v)))
            mid_ref[s] = mid
            scale = lax.rsqrt(jnp.mean(mid * mid, axis=-1, keepdims=True) + EPSILON)
            n2_ref[s] = (mid * scale * gain_ref[...][None, :]).astype(BF)
        return 0

    lax.fori_loop(0, sequences // 2, pair, 0)


def middle(variant, x, gain, attn, attn_x, wo, wo_x, ao, ao_x, bo):
    sequences, rows, width = x.shape
    inner = attn.shape[1]
    return pl.pallas_call(
        middle_kernel,
        out_shape=(shape(x.shape, F32), shape(x.shape, BF), shape((sequences, rows, 128), BF)),
        in_specs=[SMEM] + [VM] * 9,
        out_specs=(VM,) * 3,
        scratch_shapes=[pltpu.VMEM((2 * rows, inner), BF), pltpu.VMEM((2 * rows, inner), BF)],
        compiler_params=BIG,
        cost_estimate=cost(sequences * rows, width, inner, 2, 12 * sequences * rows * width),
        name="middle",
    )(variant, x, gain, attn, attn_x, wo, wo_x, ao, ao_x, bo)


def feed_kernel(
    first, variant, n2_ref, cot_ref, ag, au, bd, wg_ref, wu_ref, wd_ref, bg_ref, bu_ref, ad_ref,
    back_ref, h_ref, hidden_ref, dgate_ref, dup_ref, hg, hu, dhd, dn2_acc, dhg_acc, dhu_acc,
):
    step = pl.program_id(0)
    rows, width = n2_ref.shape
    seqs = rows // 128
    ranks = seqs * RANK
    keep = lax.broadcasted_iota(jnp.int32, (rows, ranks), 0) // 128 == (
        lax.broadcasted_iota(jnp.int32, (rows, ranks), 1) // RANK
    )

    def gather(ref):
        return jnp.concatenate([own_rows(ref, variant[first + i]) for i in range(seqs)], axis=0)

    def compact(a):
        a = jnp.where(keep, a, 0.0)
        return sum(a[:, i * RANK : (i + 1) * RANK] for i in range(seqs))

    @pl.when(step == 0)
    def _():
        g = jnp.where(keep, mm_nt(n2_ref[...], gather(ag)), 0.0)
        u = jnp.where(keep, mm_nt(n2_ref[...], gather(au)), 0.0)
        d = jnp.where(keep, mm_nt(cot_ref[...], gather(bd)) * 2.0, 0.0)
        hg[...] = (g * 2.0).astype(BF)
        hu[...] = (u * 2.0).astype(BF)
        dhd[...] = d.astype(BF)
        h_ref[...] = jnp.concatenate(
            [compact(g), compact(u), compact(d), jnp.zeros((rows, 128 - 3 * RANK), F32)], axis=1
        ).astype(BF)
        dn2_acc[...] = jnp.zeros_like(dn2_acc)
        dhg_acc[...] = jnp.zeros_like(dhg_acc)
        dhu_acc[...] = jnp.zeros_like(dhu_acc)

    n2 = n2_ref[...]
    bg, bu, ad = gather(bg_ref), gather(bu_ref), gather(ad_ref)
    gate = mm(n2, wg_ref[...]) + mm(hg[...], bg)
    up = mm(n2, wu_ref[...]) + mm(hu[...], bu)
    sg = 1.0 / (1.0 + jnp.exp(-gate))
    silu = gate * sg
    hidden_ref[...] = (silu * up).astype(BF)
    dh = mm_nt(cot_ref[...], wd_ref[...]) + mm(dhd[...], ad)
    dg = (dh * up * sg * (1.0 + gate * (1.0 - sg))).astype(BF)
    du = (dh * silu).astype(BF)
    dgate_ref[...] = dg
    dup_ref[...] = du
    dn2_acc[...] += mm_nt(dg, wg_ref[...]) + mm_nt(du, wu_ref[...])
    dhg_acc[...] += mm_nt(dg, bg)
    dhu_acc[...] += mm_nt(du, bu)

    @pl.when(step == pl.num_programs(0) - 1)
    def _():
        back_ref[:, :width] = dn2_acc[...].astype(BF)
        back_ref[:, width:] = jnp.concatenate(
            [compact(dhg_acc[...]) * 2, compact(dhu_acc[...]) * 2, jnp.zeros((rows, 128 - 2 * RANK), F32)], axis=1
        ).astype(BF)


def feed_tile(units):
    return 1152 if units % 1152 == 0 else units


def feed(index, parts, variant, n2, cot, ag, au, bd, wg, wu, wd, bg, bu, ad):
    rows, width = n2.shape[0] // parts, n2.shape[1]
    stacked, units = bg.shape
    tile = feed_tile(units)
    ranks = rows // 128 * RANK
    part = pl.BlockSpec((rows, width), lambda f: (index, 0))
    fixed = lambda dims: pl.BlockSpec(dims, lambda f: (0, 0))
    cols = lambda height: pl.BlockSpec((height, tile), lambda f: (0, f))
    return pl.pallas_call(
        functools.partial(feed_kernel, index * rows // 128),
        grid=(units // tile,),
        out_shape=(shape((rows, width + 128), BF), shape((rows, 128), BF)) + (shape((rows, units), BF),) * 3,
        in_specs=[SMEM, part, part] + [fixed((stacked, width))] * 3
        + [cols(width), cols(width), pl.BlockSpec((tile, width), lambda f: (f, 0))] + [cols(stacked)] * 3,
        out_specs=(fixed((rows, width + 128)), fixed((rows, 128))) + (cols(rows),) * 3,
        scratch_shapes=[pltpu.VMEM((rows, ranks), BF)] * 3
        + [pltpu.VMEM((rows, width), F32), pltpu.VMEM((rows, ranks), F32), pltpu.VMEM((rows, ranks), F32)],
        compiler_params=BIG,
        cost_estimate=cost(rows, width, units, 5, 6 * width * units),
        name="feed_forward",
    )(variant, n2, cot, ag, au, bd, wg, wu, wd, bg, bu, ad)


def down_kernel(variant, *refs):
    (h_a, hidden_a, dgate_a, dup_a), (h_b, hidden_b, dgate_b, dup_b) = refs[:4], refs[4:8]
    wd_ref, ad_ref, down_ref, grads_ref, hs, acc, hacc = refs[8:]
    step = pl.program_id(0)
    part = hidden_a.shape[0]
    width, tile = wd_ref.shape[1], wd_ref.shape[0]
    seqs = 2 * part // 128

    @pl.when(step == 0)
    def _():
        turned = [jnp.transpose(r[i * 128 : (i + 1) * 128, :].astype(F32)) for r in (h_a, h_b) for i in range(seqs // 2)]
        for n, factor in enumerate((2.0, 2.0, 1.0)):
            hs[n] = (spread([t[n * RANK : (n + 1) * RANK] for t in turned]) * factor).astype(BF)
        acc[...] = jnp.zeros_like(acc)
        hacc[...] = jnp.zeros_like(hacc)

    for c, hidden in enumerate((hidden_a, hidden_b)):
        acc[c * part : (c + 1) * part] += mm(hidden[...], wd_ref[...])
        for i in range(seqs // 2):
            rows = slice(i * 128, (i + 1) * 128)
            own = own_rows(ad_ref, variant[c * (seqs // 2) + i])
            hacc[c * part + i * 128 : c * part + (i + 1) * 128, :RANK] += mm_nt(hidden[rows], own)
    for n, (a, b) in enumerate(((dgate_a, dgate_b), (dup_a, dup_b), (hidden_a, hidden_b))):
        grad = mm(hs[n, :, :part], a[...]) + mm(hs[n, :, part:], b[...])
        grads_ref[:, n * tile : (n + 1) * tile] = grad.astype(BF)

    @pl.when(step == pl.num_programs(0) - 1)
    def _():
        down_ref[:, :width] = acc[...].astype(BF)
        down_ref[:, width:] = hacc[...].astype(BF)


def down_part(variant, fed_a, fed_b, wd, ad):
    part, units = fed_a[1].shape
    rows = 2 * part
    stacked, width = ad.shape[0], wd.shape[1]
    tile = feed_tile(units)
    ranks = rows // 128 * RANK
    fixed = lambda dims: pl.BlockSpec(dims, lambda f: (0, 0))
    cols = lambda height, n=1: pl.BlockSpec((height, n * tile), lambda f: (0, f))
    return pl.pallas_call(
        down_kernel,
        grid=(units // tile,),
        out_shape=(shape((rows, width + 128), BF), shape((ranks, 3 * units), BF)),
        in_specs=[SMEM] + [fixed((part, 128)), cols(part), cols(part), cols(part)] * 2
        + [pl.BlockSpec((tile, width), lambda f: (f, 0)), cols(stacked)],
        out_specs=(fixed((rows, width + 128)), cols(ranks, 3)),
        scratch_shapes=[pltpu.VMEM((3, ranks, rows), BF), pltpu.VMEM((rows, width), F32), pltpu.VMEM((rows, 128), F32)],
        compiler_params=BIG,
        cost_estimate=cost(rows, width, units, 1, 2 * width * units),
        name="feed_down",
    )(variant, *fed_a, *fed_b, wd, ad)


def turn_back_kernel(
    variant, mid_ref, n2_ref, cot_ref, back_a, back_ax, back_b, back_bx, hout_ref, attn_ref, gain_ref, ag, au, bo, ao, wo,
    dmid_ref, dattn_ref, grads_ref, branch_s, hidden_s,
):
    sequences, rows, width = mid_ref.shape
    half = pl.multiple_of(lax.axis_index("tp") * (width // 2), width // 2)
    mine = pl.ds(half, width // 2)
    gain = gain_ref[...][None, :]
    cut = sequences // 2
    sums = ((back_a, back_ax), (back_b, back_bx))
    blocks = []
    for s in range(sequences):
        v = variant[s]
        own, other = (r[s % cut * rows : (s % cut + 1) * rows, :].astype(F32) for r in sums[s // cut])
        whole = own + other
        dh = whole[:, width : width + 2 * RANK].astype(BF)
        c = whole[:, :width] + mm(dh, jnp.concatenate([own_rows(ag, v), own_rows(au, v)], axis=0))
        d_mid = cot_ref[s].astype(F32) + norm_back(mid_ref[s], gain, c)
        dmid_ref[s] = d_mid
        here = slice(s * rows, (s + 1) * rows)
        branch_s[here, :] = d_mid.astype(BF)
        dho = (mm_nt(branch_s[here, :], own_rows(bo, v)) * 2.0).astype(BF)
        hidden_s[here, :] = mm(dho, own_rows(ao, v))
        wide = jnp.concatenate([dh, dho, hout_ref[s][:, :RANK] * 2, jnp.zeros((rows, 128 - 4 * RANK), BF)], axis=1)
        t = jnp.transpose(wide.astype(F32)).astype(BF)
        blocks.append(
            jnp.concatenate(
                [
                    mm_nt(t[2 * RANK : 3 * RANK], attn_ref[s]),
                    mm(t[:RANK], n2_ref[s, :, mine]),
                    mm(t[RANK : 2 * RANK], n2_ref[s, :, mine]),
                    mm(t[3 * RANK : 4 * RANK], branch_s[here, mine]),
                ],
                axis=1,
            )
        )
    grads_ref[...] = rank_halves(blocks).astype(BF)
    for p in range(sequences // 2):
        d_attn = mm_nt(branch_s[2 * p * rows : 2 * (p + 1) * rows, :], wo[...]) + hidden_s[2 * p * rows : 2 * (p + 1) * rows, :]
        for i in (0, 1):
            dattn_ref[2 * p + i] = jnp.transpose(d_attn[i * rows : (i + 1) * rows]).astype(BF)


def turn_back(variant, mid, n2, cot, backs, hout, attn, gain, ag, au, bo, ao, wo):
    sequences, rows, width = mid.shape
    inner = wo.shape[0]
    return pl.pallas_call(
        turn_back_kernel,
        out_shape=(
            shape(mid.shape, F32), shape((sequences, inner, rows), BF),
            shape((sequences * RANK, inner + 3 * (width // 2)), BF),
        ),
        in_specs=[SMEM] + [VM] * 15,
        out_specs=(VM,) * 3,
        scratch_shapes=[pltpu.VMEM((sequences * rows, width), BF), pltpu.VMEM((sequences * rows, inner), F32)],
        compiler_params=BIG,
        cost_estimate=cost(sequences * rows, width, inner, 1, 20 * sequences * rows * width),
        name="turn_back",
    )(variant, mid, n2, cot, *backs, hout, attn, gain, ag, au, bo, ao, wo)


def result_kernel(variant, mid_ref, down_ref, down_x_ref, cot_ref, bd, out_ref, grads_ref):
    sequences, rows, width = mid_ref.shape
    mine = pl.ds(pl.multiple_of(lax.axis_index("tp") * (width // 2), width // 2), width // 2)
    blocks = []
    for s in range(sequences):
        v = variant[s]
        whole = down_ref[s].astype(F32) + down_x_ref[s].astype(F32)
        h = whole[:, width : width + RANK].astype(BF) * 2
        out_ref[s] = (mid_ref[s] + (whole[:, :width] + mm(h, own_rows(bd, v)))).astype(BF)
        t = jnp.transpose(jnp.concatenate([h, jnp.zeros((rows, 128 - RANK), BF)], axis=1).astype(F32)).astype(BF)
        blocks.append(mm(t[:RANK], cot_ref[s, :, mine]))
    grads_ref[...] = rank_halves(blocks).astype(BF)


def result(variant, mid, down, down_x, cot, bd):
    sequences, rows, width = mid.shape
    return pl.pallas_call(
        result_kernel,
        out_shape=(shape(mid.shape, BF), shape((sequences * RANK, width // 2), BF)),
        in_specs=[SMEM] + [VM] * 5,
        out_specs=(VM,) * 2,
        compiler_params=BIG,
        cost_estimate=cost(sequences * rows, width, 16, 2, 12 * sequences * rows * width),
        name="block_result",
    )(variant, mid, down, down_x, cot, bd)


MESH = pl.DeviceIdType.MESH


def exchange_kernel(count, parts, kinds, *refs):
    n = len(kinds)
    xs, outs = refs[:n], refs[n : 2 * n]
    sends, recvs, locals_ = refs[2 * n : 3 * n], refs[3 * n : 4 * n], refs[4 * n]
    me = lax.axis_index("ctx")
    barrier = pltpu.get_barrier_semaphore()
    step = 1 if "full" in kinds else parts
    peers = count // step - 1

    def greet(k, _):
        other = lax.rem(me + k * step, count)
        pl.semaphore_signal(barrier, inc=1, device_id={"ctx": other}, device_id_type=MESH)
        return 0

    lax.fori_loop(1, peers + 1, greet, 0)

    def block(kind, x, device):
        if kind == "class" or x.shape[0] != count:
            return device // parts
        return device

    def slot(kind, device):
        return device // parts if kind == "class" else device

    def copy(i, target, place):
        kind = kinds[i]
        return pltpu.make_async_remote_copy(
            src_ref=xs[i].at[block(kind, xs[i], target)],
            dst_ref=outs[i].at[slot(kind, place)],
            send_sem=sends[i].at[slot(kind, target)],
            recv_sem=recvs[i].at[slot(kind, place)],
            device_id={"ctx": target},
            device_id_type=MESH,
        )

    own = [
        pltpu.make_async_copy(xs[i].at[block(kinds[i], xs[i], me)], outs[i].at[slot(kinds[i], me)], locals_.at[i])
        for i in range(n)
    ]
    for c in own:
        c.start()
    pl.semaphore_wait(barrier, peers)
    for i in range(n):
        hop = 1 if kinds[i] == "full" else parts

        def send(k, _, i=i, hop=hop):
            copy(i, lax.rem(me + k * hop, count), me).start()
            return 0

        lax.fori_loop(1, count // hop, send, 0)
    for i in range(n):
        hop = 1 if kinds[i] == "full" else parts

        def finish(k, _, i=i, hop=hop):
            other = lax.rem(me + k * hop, count)
            copy(i, other, me).wait_send()
            copy(i, other, other).wait_recv()
            return 0

        lax.fori_loop(1, count // hop, finish, 0)
    for c in own:
        c.wait()


def exchange(arrays, kinds, count, parts, collective_id, name):
    n = len(arrays)
    members = [count // parts if kind == "class" else count for kind in kinds]
    anywhere = pl.BlockSpec(memory_space=pl.ANY)
    return pl.pallas_call(
        functools.partial(exchange_kernel, count, parts, kinds),
        out_shape=tuple(jax.ShapeDtypeStruct((k,) + a.shape[1:], a.dtype) for k, a in zip(members, arrays)),
        in_specs=[anywhere] * n,
        out_specs=(anywhere,) * n,
        scratch_shapes=[pltpu.SemaphoreType.DMA((k,)) for k in members] * 2 + [pltpu.SemaphoreType.DMA((n,))],
        compiler_params=pltpu.CompilerParams(collective_id=collective_id, has_side_effects=True),
        name=name,
    )(*arrays)


def home_kernel(count, parts, x, o, ox, send, recv, xsend, xrecv, own):
    me = lax.axis_index("ctx")
    unit = me // parts
    units = count // parts
    across = {"tp": 1 - lax.axis_index("tp")}
    barrier = pltpu.get_barrier_semaphore()

    def greet(k, _):
        pl.semaphore_signal(barrier, inc=1, device_id={"ctx": lax.rem(me + k * parts, count)}, device_id_type=MESH)
        return 0

    lax.fori_loop(1, units, greet, 0)
    pl.semaphore_signal(barrier, inc=1, device_id=across, device_id_type=MESH)
    kept = pltpu.make_async_copy(x.at[unit], o.at[unit], own)
    kept.start()
    pl.semaphore_wait(barrier, units)

    def copy(target, place):
        return pltpu.make_async_remote_copy(
            src_ref=x.at[target // parts], dst_ref=o.at[place // parts], send_sem=send.at[target // parts],
            recv_sem=recv.at[place // parts], device_id={"ctx": target}, device_id_type=MESH,
        )

    def pass_on(source, slot):
        return pltpu.make_async_remote_copy(
            src_ref=source.at[slot], dst_ref=ox.at[slot], send_sem=xsend.at[slot], recv_sem=xrecv.at[slot],
            device_id=across, device_id_type=MESH,
        )

    def start(k, _):
        copy(lax.rem(me + k * parts, count), me).start()
        return 0

    lax.fori_loop(1, units, start, 0)
    pass_on(x, unit).start()

    def relay(k, _):
        other = lax.rem(me + count - k * parts, count)
        copy(other, other).wait_recv()
        pass_on(o, other // parts).start()
        return 0

    lax.fori_loop(1, units, relay, 0)

    def finish(k, _):
        other = lax.rem(me + k * parts, count)
        copy(other, me).wait_send()
        return 0

    lax.fori_loop(1, units, finish, 0)

    def finish_across(k, _):
        pass_on(o, k).wait_send()
        pass_on(o, k).wait_recv()
        return 0

    lax.fori_loop(0, units, finish_across, 0)
    kept.wait()


def send_home(x, count, parts, collective_id):
    units = count // parts
    dma = pltpu.SemaphoreType.DMA
    return pl.pallas_call(
        functools.partial(home_kernel, count, parts),
        out_shape=(shape(x.shape, x.dtype),) * 2,
        in_specs=[ANYWHERE],
        out_specs=(ANYWHERE,) * 2,
        scratch_shapes=[dma((units,))] * 4 + [dma],
        compiler_params=pltpu.CompilerParams(collective_id=collective_id, has_side_effects=True),
        name="send_attn",
    )(x)


def finish_kernel(reduce, count, widths, shared, *refs):
    refs = list(refs)
    take = lambda n: [refs.pop(0) for _ in range(n)]
    dq_ref, dkv_ref, pre_ref, h_ref, gains, cos_ref, sin_ref, gain_ref, bc_ref, pick_ref = take(10)
    far = take(7)
    grads = take(3) if reduce else []
    (out_ref,) = take(1)
    gout = take(4) if reduce else take(1)
    x, d_mid, n1, wq, wk, wv, ac = near = take(7)
    d_n, gb, dh_own, dh_other, dh_sum, sbuf, rbuf, gq = take(8)
    near_sems, dh_send, dh_recv, xsend, xrecv = take(5)
    sequences, inner, rows = dq_ref.shape
    width = out_ref.shape[2]
    kw = wk.shape[1]
    half_rows = sequences * RANK // 2
    me = lax.axis_index("ctx")
    across = {"tp": 1 - lax.axis_index("tp")}
    mine = pl.ds(pl.multiple_of(lax.axis_index("tp") * (width // 2), width // 2), width // 2)

    def remote(source, target, send, recv, device):
        return pltpu.make_async_remote_copy(
            src_ref=source, dst_ref=target, send_sem=send, recv_sem=recv, device_id=device, device_id_type=MESH
        )

    loads = [pltpu.make_async_copy(f, n, near_sems.at[i]) for i, (f, n) in enumerate(zip(far, near))]
    barrier = pltpu.get_barrier_semaphore()
    pl.semaphore_signal(barrier, inc=1, device_id=across, device_id_type=MESH)
    peers = 1
    if reduce:
        planes, plane_ins, fin_outs, fin_ins = take(2), take(2), take(2), take(2)
        own, core_in = take(2)
        own_sems, core_send, core_recv = take(3)
        plane_send, plane_recv, fin_send, fin_recv = take(4)
        (last_sems,) = take(1)
        chips = count // 2
        chip, core = me // 2, lax.rem(me, 2)
        twin = {"ctx": 2 * chip + 1 - core}
        pl.semaphore_signal(barrier, inc=1, device_id=twin, device_id_type=MESH)

        def at_chip(k):
            return lax.rem(chip + k, chips)

        def greet(k, _):
            pl.semaphore_signal(barrier, inc=1, device_id={"ctx": 2 * at_chip(k) + core}, device_id_type=MESH)
            return 0

        lax.fori_loop(1, chips, greet, 0)
        peers += chips

        def part_of(ref, who):
            size = ref.shape[0] // 2
            return ref.at[pl.ds(pl.multiple_of(who * size, 16), size), :]

        known, w_qkv = sum(widths[:3]), widths[3]
        own_loads, to_twin, at = [], [], 0
        for i, ref in enumerate(grads):
            place = slice(at, at + widths[i])
            at += widths[i]
            own_loads.append(pltpu.make_async_copy(part_of(ref, core), own.at[:, place], own_sems.at[i]))
            to_twin.append(
                remote(part_of(ref, 1 - core), core_in.at[:, place], core_send.at[i], core_recv.at[i], twin)
            )
        to_twin.append(remote(gq.at[1 - core], core_in.at[:, known : known + w_qkv], core_send.at[3], core_recv.at[3], twin))
        for c in own_loads:
            c.start()
    for i in (3, 4, 5, 2, 6, 0, 1):
        loads[i].start()
    pl.semaphore_wait(barrier, peers)
    if reduce:
        for c in to_twin[:3]:
            c.start()

    cosine, sine = cos_ref[...], sin_ref[...]
    heads_k = kw // HEAD_DIM
    cuts = (slice(0, inner), slice(inner, inner + kw), slice(inner + kw, inner + 2 * kw))

    def prepare_back(pre, gains, c):
        u = pre.reshape(pre.shape[0] // HEAD_DIM, HEAD_DIM, rows)
        scale = lax.rsqrt(jnp.mean(u * u, axis=1, keepdims=True) + EPSILON)
        y = u * scale
        w = turn(c.reshape(u.shape).astype(F32), cosine, -sine) * gains
        return (scale * (w - y * jnp.mean(w * y, axis=1, keepdims=True))).reshape(pre.shape)

    def first_step(s):
        dkv = dkv_ref[s * heads_k : (s + 1) * heads_k].astype(F32)
        dkv = jnp.sum(dkv, axis=1).astype(BF) if dkv.shape[1] > 1 else dkv[:, 0].astype(BF)
        d_q = prepare_back(pre_ref[s, :inner, :], gains[0], dq_ref[s])
        d_k = prepare_back(pre_ref[s, inner:, :], gains[1], dkv[:, :HEAD_DIM, :].reshape(kw, rows))
        d_v = dkv[:, HEAD_DIM:, :].reshape(kw, rows).astype(F32)
        d = jnp.transpose(jnp.concatenate([d_q, d_k, d_v], axis=0)).astype(BF)
        d_n[s] = d
        dh = [mm_nt(d[:, c], bc_ref[s, :, c]) * 2.0 for c in cuts]
        dh_own[s] = jnp.concatenate(dh + [jnp.zeros((rows, 128 - 3 * RANK), F32)], axis=1).astype(BF)
        t = (jnp.transpose(h_ref[s].astype(F32)) * 2.0).astype(BF)
        gb[s] = jnp.concatenate([mm(t[i * RANK : (i + 1) * RANK], d[:, c]) for i, c in enumerate(cuts)], axis=1)

    def part_copy(s):
        return remote(sbuf.at[s], rbuf.at[s], xsend.at[s], xrecv.at[s], across)

    dh_copies = []

    def send_pair(p):
        pair = pl.ds(2 * p, 2)
        first_step(2 * p)
        first_step(2 * p + 1)
        dh_copies.append(remote(dh_own.at[pair], dh_other.at[pair], dh_send.at[p], dh_recv.at[p], across))
        dh_copies[-1].start()
        if p == 0:
            for i in (3, 4, 5):
                loads[i].wait()
        d = jnp.concatenate([d_n[2 * p], d_n[2 * p + 1]], axis=0)
        part = mm_nt(d[:, cuts[0]], wq[...]) + mm_nt(d[:, cuts[1]], wk[...]) + mm_nt(d[:, cuts[2]], wv[...])
        for i in (0, 1):
            sbuf[2 * p + i] = part[i * rows : (i + 1) * rows].astype(BF)
            part_copy(2 * p + i).start()

    def plane_copy(g, k, slot):
        chunk = planes[g].shape[1] // chips
        return remote(
            planes[g].at[:, pl.ds(pl.multiple_of(k * chunk, 128), chunk)], plane_ins[g].at[slot],
            plane_send.at[g, k], plane_recv.at[g, slot], {"ctx": 2 * k + core},
        )

    def fin_copy(g, k, slot):
        return remote(
            fin_outs[g].at[k], fin_ins[g].at[slot], fin_send.at[g, k], fin_recv.at[g, slot], {"ctx": 2 * k + core}
        )

    def each_chip(step):
        def body(k, _):
            step(at_chip(k))
            return 0

        lax.fori_loop(1, chips, body, 0)

    def to_plane(g):
        chunk = planes[g].shape[1] // chips
        each_chip(lambda k: plane_copy(g, k, chip).start())
        plane_ins[g][chip] = planes[g][:, pl.ds(pl.multiple_of(chip * chunk, 128), chunk)]

    def to_owners(g):
        each_chip(lambda k: plane_copy(g, k, k).wait_recv())
        total = plane_ins[g][0].astype(F32)
        for k in range(1, chips):
            total = total + plane_ins[g][k].astype(F32)
        chunk, per = total.shape[1], RANK // 2
        for k in range(chips):
            row = jnp.zeros((per, chunk), F32)
            for s in range(sequences):
                row = row + total[s * per : (s + 1) * per] * pick_ref[k, s][:, :1]
            fin_outs[g][k] = jnp.concatenate([row[:, : chunk // 2], row[:, chunk // 2 :]], axis=0).astype(BF)
        each_chip(lambda k: fin_copy(g, k, chip).start())
        fin_ins[g][chip] = fin_outs[g][chip]

    def rows_in(g):
        each_chip(lambda k: fin_copy(g, k, k).wait_recv())
        rows_ref, per = gout[g], RANK // 2
        chunk = rows_ref.shape[1] // chips
        for k in range(chips):
            block = fin_ins[g][k].astype(F32)
            rows_ref[:, k * chunk : k * chunk + chunk // 2] = block[:per]
            rows_ref[:, k * chunk + chunk // 2 : (k + 1) * chunk] = block[per:]
        copy = remote(
            rows_ref.at[:, shared[g][0] : shared[g][1]], gout[2 + g], last_sems.at[g], last_sems.at[2 + g], across
        )
        copy.start()
        return copy

    def last_step(s):
        part_copy(s).wait_recv()
        c = sbuf[s].astype(F32) + rbuf[s].astype(F32) + mm(dh_sum[s][:, : 3 * RANK], ac[s])
        out_ref[s] = (d_mid[s] + norm_back(x[s].astype(F32), gain_ref[...][None, :], c)).astype(BF)

    pairs = sequences // 2
    send_pair(0)
    if reduce:
        for c in own_loads:
            c.wait()
        for c in to_twin[:3]:
            c.wait_recv()
        planes[0][:, :known] = (own[...].astype(F32) + core_in[:, :known].astype(F32)).astype(BF)
        if planes[0].shape[1] > known:
            planes[0][:, known:] = jnp.zeros((half_rows, planes[0].shape[1] - known), BF)
        to_plane(0)
    for p in range(1, pairs):
        send_pair(p)
    loads[2].wait()
    blocks = []
    for s in range(sequences):
        if s % 2 == 0:
            dh_copies[s // 2].wait_recv()
        dh = (dh_own[s].astype(F32) + dh_other[s].astype(F32)).astype(BF)
        dh_sum[s] = dh
        t = jnp.transpose(dh.astype(F32)).astype(BF)
        wide = mm(t[: 3 * RANK], n1[s, :, mine])
        blocks.append(jnp.concatenate([wide[i * RANK : (i + 1) * RANK] for i in range(3)] + [gb[s]], axis=1))
    everything = rank_halves(blocks)
    for b in (0, 1):
        gq[b] = everything[b * half_rows : (b + 1) * half_rows].astype(BF)
    if reduce:
        to_twin[3].start()
    for i in (6, 0, 1):
        loads[i].wait()
    if reduce:
        to_owners(0)
        to_twin[3].wait_recv()
        planes[1][:, :w_qkv] = (gq[core].astype(F32) + core_in[:, known : known + w_qkv].astype(F32)).astype(BF)
        if planes[1].shape[1] > w_qkv:
            planes[1][:, w_qkv:] = jnp.zeros((half_rows, planes[1].shape[1] - w_qkv), BF)
        to_plane(1)
        last_step(0)
        to_owners(1)
        shared_copies = [rows_in(0)]
        last_step(1)
        shared_copies.append(rows_in(1))
        for s in range(2, sequences):
            last_step(s)
        for c in shared_copies:
            c.wait()
        for c in to_twin:
            c.wait_send()
        for g in (0, 1):
            each_chip(lambda k, g=g: plane_copy(g, k, chip).wait_send())
            each_chip(lambda k, g=g: fin_copy(g, k, chip).wait_send())
    else:
        for s in range(sequences):
            last_step(s)
        gout[0][...] = gq[...]
    for c in dh_copies:
        c.wait_send()
    for s in range(sequences):
        part_copy(s).wait_send()


def finish(reduce, count, dq, dkv, pre, h, gains, tables, gain, bc, pick, x, d_mid, n1, weights, ac, grads, shared, collective_id):
    sequences, rows, width = x.shape
    inner, kw = weights[0].shape[1], weights[1].shape[1]
    w_qkv = 3 * (width // 2) + inner + 2 * kw
    half_rows = sequences * RANK // 2
    dma = pltpu.SemaphoreType.DMA
    far = (x, d_mid, n1) + tuple(weights) + (ac,)
    widths = ()
    gshape = (shape((2, half_rows, w_qkv), BF),)
    scratch = [pltpu.VMEM(a.shape, a.dtype) for a in far]
    scratch += [
        pltpu.VMEM((sequences, rows, inner + 2 * kw), BF),
        pltpu.VMEM((sequences, RANK, inner + 2 * kw), F32),
        pltpu.VMEM((sequences, rows, 128), BF),
        pltpu.VMEM((sequences, rows, 128), BF),
        pltpu.VMEM((sequences, rows, 128), BF),
        pltpu.VMEM(x.shape, BF),
        pltpu.VMEM(x.shape, BF),
        pltpu.VMEM((2, half_rows, w_qkv), BF),
        dma((7,)), dma((sequences // 2,)), dma((sequences // 2,)), dma((sequences,)), dma((sequences,)),
    ]
    extra = ()
    if reduce:
        chips = count // 2
        widths = tuple(g.shape[1] for g in grads) + (w_qkv,)
        padded = [-(-n // (256 * chips)) * 256 * chips for n in (sum(widths[:3]), w_qkv)]
        gshape = tuple(shape((RANK // 2, n), F32) for n in padded)
        gshape += tuple(shape((RANK // 2, b - a), F32) for a, b in shared)
        scratch += [pltpu.VMEM((half_rows, n), BF) for n in padded]
        scratch += [pltpu.VMEM((chips, half_rows, n // chips), BF) for n in padded]
        scratch += [pltpu.VMEM((chips, RANK, n // chips // 2), BF) for n in padded] * 2
        scratch += [
            pltpu.VMEM((half_rows, sum(widths[:3])), BF),
            pltpu.VMEM((half_rows, sum(widths)), BF),
            dma((3,)), dma((4,)), dma((4,)),
        ]
        scratch += [dma((2, chips))] * 4 + [dma((4,))]
        extra = tuple(grads)
    return pl.pallas_call(
        functools.partial(finish_kernel, reduce, count, widths, shared),
        out_shape=(shape(x.shape, BF),) + gshape,
        in_specs=[VM] * 10 + [ANYWHERE] * (7 + len(extra)),
        out_specs=(VM,) * (1 + len(gshape)),
        scratch_shapes=scratch,
        compiler_params=pltpu.CompilerParams(
            collective_id=collective_id, has_side_effects=True, vmem_limit_bytes=60 * 2**20
        ),
        name="finish",
    )(dq, dkv, pre, h, gains, *tables, gain, bc, pick, *far, *extra)


def unpack_kernel(hidden_units, tile, inner, kw, first, second, first_x, second_x, *outs):
    ga_query, gb_query, ga_key, gb_key, ga_value, gb_value, ga_out, gb_out, ga_gate, gb_gate, ga_up, gb_up, ga_down, gb_down = outs
    width = ga_query.shape[1]
    w = width // 2
    lower = lax.axis_index("tp") == 0
    for f in range(hidden_units // tile):
        for n, out in enumerate((gb_gate, gb_up, ga_down)):
            out[:, f * tile : (f + 1) * tile] = first[:, (3 * f + n) * tile : (3 * f + n + 1) * tile]
    at = 3 * hidden_units
    ga_out[...] = first[:, at : at + inner]

    def join(out, own, own_at, other, i):
        a = own[:, own_at + i * w : own_at + (i + 1) * w]
        b = other[:, i * w : (i + 1) * w]
        out[:, :w] = jnp.where(lower, a, b)
        out[:, w:] = jnp.where(lower, b, a)

    for i, out in enumerate((ga_gate, ga_up, gb_out, gb_down)):
        join(out, first, at + inner, first_x, i)
    for i, out in enumerate((ga_query, ga_key, ga_value)):
        join(out, second, 0, second_x, i)
    at = 3 * w
    gb_query[...] = second[:, at : at + inner]
    gb_key[...] = second[:, at + inner : at + inner + kw]
    gb_value[...] = second[:, at + inner + kw : at + inner + 2 * kw]


def unpack(first, second, first_x, second_x, width, hidden_units, tile, inner, kw):
    sizes = (width, inner, width, kw, width, kw, inner, width, width, hidden_units, width, hidden_units, hidden_units, width)
    return pl.pallas_call(
        functools.partial(unpack_kernel, hidden_units, tile, inner, kw),
        out_shape=tuple(shape((first.shape[0], n), F32) for n in sizes),
        in_specs=[VM] * 4,
        out_specs=(VM,) * 14,
        name="unpack",
    )(first, second, first_x, second_x)


def rotary_tables(positions):
    half = HEAD_DIM // 2
    frequencies = THETA_BASE ** (-jnp.arange(half, dtype=F32) * 2.0 / HEAD_DIM)
    angles = frequencies[:, None] * positions.astype(F32)[None, :]
    return jnp.cos(angles), jnp.sin(angles)


def swap(values):
    return lax.ppermute(values, "tp", [(0, 1), (1, 0)])


def reduce_scatter_rows(grads, count):
    rows, columns = grads.shape
    index = lax.axis_index("ctx")
    held = grads.reshape(count, rows // count, columns)
    bit = 1
    while bit < count:
        mine = (index // bit) % 2
        pairs = held.reshape(held.shape[0] // 2, 2, held.shape[1], columns)
        kept = lax.dynamic_index_in_dim(pairs, mine, 1, keepdims=False)
        sent = lax.dynamic_index_in_dim(pairs, 1 - mine, 1, keepdims=False).astype(BF)
        held = kept.astype(F32) + lax.ppermute(sent, "ctx", [(i, i ^ bit) for i in range(count)]).astype(F32)
        bit *= 2
    return held[0]


def local(
    tokens, output_cotangent, segment_ids, variant, attn_gain, ffn_gain, q_gain, k_gain,
    query_matrix, key_matrix, value_matrix, output_matrix, gate_matrix, up_matrix, down_matrix,
    query_input_factor, query_output_factor, key_input_factor, key_output_factor,
    value_input_factor, value_output_factor, output_input_factor, output_output_factor,
    gate_input_factor, gate_output_factor, up_input_factor, up_output_factor,
    down_input_factor, down_output_factor,
):
    sequences, rows_here, width = tokens.shape
    count = lax.axis_size("ctx")
    index = lax.axis_index("ctx")
    inner, kw = query_matrix.shape[1], key_matrix.shape[1]
    key_heads = kw // HEAD_DIM
    units = sequences * key_heads
    parts = count // units
    stacked = query_input_factor.shape[0]
    reduce_here = stacked // count == RANK // 2
    tables = rotary_tables(index * rows_here + jnp.arange(rows_here, dtype=jnp.int32))
    weights = (query_matrix, key_matrix, value_matrix)
    ins = (query_input_factor, key_input_factor, value_input_factor)
    outs = (query_output_factor, key_output_factor, value_output_factor)

    output_matrix_other = swap(output_matrix)
    output_input_other = swap(output_input_factor)

    n1, h_one, pre, queries, keys_values, ac, bc, gains, pick = project(
        variant, tokens, attn_gain, weights, ins, outs, q_gain, k_gain, tables
    )
    q_all, kv_all = exchange((queries, keys_values), ("class", "full"), count, parts, 0, "send_qkv")
    o_all, o_wide, lse = attn_fwd(segment_ids, q_all, kv_all, parts, key_heads)
    attn, attn_other = (a.reshape(sequences, inner, rows_here) for a in send_home(o_all, count, parts, 1))
    mid, n2, h_out = middle(
        variant, tokens, ffn_gain, attn, attn_other, output_matrix, output_matrix_other,
        output_input_factor, output_input_other, output_output_factor,
    )

    flat = lambda a: a.reshape(sequences * rows_here, -1)
    by_seq = lambda a: a.reshape(sequences, rows_here, -1)
    fed = [
        feed(
            i, 2, variant, flat(n2), flat(output_cotangent), gate_input_factor, up_input_factor, down_output_factor,
            gate_matrix, up_matrix, down_matrix, gate_output_factor, up_output_factor, down_input_factor,
        )
        for i in (0, 1)
    ]
    backs = [b for f in fed for b in (f[0], swap(f[0]))]
    down, g_ffn = down_part(variant, fed[0][1:], fed[1][1:], down_matrix, down_input_factor)
    d_mid, d_attn, g_mid = turn_back(
        variant, mid, n2, output_cotangent, backs, h_out, attn, ffn_gain, gate_input_factor, up_input_factor,
        output_output_factor, output_input_factor, output_matrix,
    )
    d_attn = d_attn.reshape(queries.shape)
    d_attn, down = lax.optimization_barrier((d_attn, down))
    down_other = swap(down)
    (do_all,) = exchange((d_attn,), ("class",), count, parts, 2, "send_d_attn")
    dq_all, dkv_all = attn_bwd(segment_ids, q_all, kv_all, do_all, o_wide, lse, parts, key_heads)
    block_result, g_down = result(variant, mid, by_seq(down), by_seq(down_other), output_cotangent, down_output_factor)
    dq, dkv = exchange((dq_all, dkv_all), ("class", "full"), count, parts, 3, "send_dqkv")

    w = width // 2
    hidden_units = gate_matrix.shape[1]
    tile = feed_tile(hidden_units)
    at = 3 * hidden_units + inner
    shared = ((at, at + 4 * w), (0, 3 * w))
    ends = finish(
        reduce_here, count, dq.reshape(sequences, inner, rows_here), dkv.reshape(units, parts, 2 * HEAD_DIM, rows_here),
        pre, h_one, gains, tables, attn_gain, bc, pick, tokens, d_mid, n1, weights, ac,
        (g_ffn, g_mid, g_down), shared, 4,
    )
    if reduce_here:
        owned = ends[1:]
    else:
        per = RANK // 2
        pick = (jnp.arange(stacked // RANK, dtype=jnp.int32)[:, None] == variant[None, :]).astype(F32)
        owned, other = [], []
        for grads, (low, high) in zip((jnp.concatenate([g_ffn, g_mid, g_down], axis=1), ends[1]), shared):
            grads = grads.reshape(2, sequences, per, -1).astype(F32)
            dense = jnp.sum(pick[:, None, :, None, None] * grads[None], axis=2)
            owned.append(reduce_scatter_rows(dense.reshape(stacked, -1), count))
            other.append(swap(owned[-1][:, low:high]))
        owned = owned + other
    return (block_result, ends[0]) + tuple(unpack(*owned, width, hidden_units, tile, inner, kw))


def solution(mesh):
    rows, whole, columns = P(None, "ctx", None), P(), P(None, "tp")
    owned, owned_half = P("ctx", None), P("ctx", "tp")
    return jax.shard_map(
        local,
        mesh=mesh,
        in_specs=(rows, rows) + (whole,) * 6
        + (columns, columns, columns, P("tp", None), columns, columns, P("tp", None))
        + (whole, columns) * 3 + (columns, whole) + (whole, columns) * 2 + (columns, whole),
        out_specs=(
            rows, rows, owned, owned_half, owned, owned_half, owned, owned_half,
            owned_half, owned, owned, owned_half, owned, owned_half, owned_half, owned,
        ),
        check_vma=False,
    )
```

time: 510 us -> 369 us (0.72); the launches traced: 501 us -> 369 us
  Pallas kernels: 225 us -> 334 us
  waiting for transfers between devices: 120 us -> 22 us
  local copies, waits for them, and re-layouts: 58.7 us -> 6.27 us
  matrix products: 35 us -> 0 us
  other arithmetic: 33.8 us -> 0.77 us
  starting transfers between devices: 26.2 us -> 5.8 us
    pallas_call x2 -> x10, Pallas kernels: 65.2 us -> 207 us  [the longest x2 57 us: feed(): pl.pallas_call(functools.partial(feed_kernel, index * rows // 128), grid=...]
    ppermute x9 -> x5, waiting for transfers between devices: 95.9 us -> 22 us  [swap(): return lax.ppermute(values, 'tp', [(0, 1), (1, 0)])]
    dot_general x40 -> x0, matrix products: 35 us -> none  [ein(): return jnp.einsum(spec, a, b, preferred_element_type=F32)]
    pallas_call x4 -> x3, Pallas kernels: 127 us -> 97.6 us  [exchange(): pl.pallas_call(functools.partial(exchange_kernel, count, parts, kinds), o...]
    ppermute x8 -> x0, waiting for transfers between devices: 24 us -> none  [reduce_scatter_rows(): lax.ppermute(sent, 'ctx', [(i, i ^ bit) for i in range(count)]).astype(F32)]
    mul x12 -> x0, local copies, waits for them, and re-layouts: 20.3 us -> none  [the longest x8 13.1 us: head_prepare(): return turn(heads * scale * gains[:, None], *tables).astype(BF)]
    ppermute x8 -> x0, starting transfers between devices: 13.9 us -> none  [reduce_scatter_rows(): lax.ppermute(sent, 'ctx', [(i, i ^ bit) for i in range(count)]).astype(F32)]
    convert_element_type x10 -> x0, other arithmetic: 11.4 us -> none  [the longest x2 3.57 us: head_prepare_back(): return back.reshape(values.shape).astype(BF)]
  transfers between devices with their start and end apart: 17 -> 5, of which waited for: 10 -> 2; matrix products, arithmetic and copies ran while one was open for 14% -> 0% of each run, Pallas kernels for 21% -> 52%
where the time goes in v2:
time: 369 us
  Pallas kernels  334 us (91%)
  waiting for transfers between devices  22 us (6%)
  local copies, waits for them, and re-layouts  6.27 us (2%)
  starting transfers between devices  5.8 us (2%)
    pallas_call x3, Pallas kernels, exchange(): pl.pallas_call(functools.partial(exchange_kernel, count, parts, kinds), o...  97.6 us
    pallas_call x2, Pallas kernels, feed(): pl.pallas_call(functools.partial(feed_kernel, index * rows // 128), grid=...  57 us
    pallas_call x1, Pallas kernels, finish(): pl.pallas_call(functools.partial(finish_kernel, reduce, count, widths, sh...  55.3 us
    pallas_call x1, Pallas kernels, send_home(): pl.pallas_call(functools.partial(home_kernel, count, parts), out_shape=(s...  40.9 us
    ppermute x5, waiting for transfers between devices, swap(): return lax.ppermute(values, 'tp', [(0, 1), (1, 0)])  22 us
    pallas_call x1, Pallas kernels, attn_bwd(): pl.pallas_call(functools.partial(attn_bwd_kernel, stride, group, units_pe...  18.5 us
    pallas_call x1, Pallas kernels, down_part(): pl.pallas_call(down_kernel, grid=(units // tile,), out_shape=(shape((rows...  14.9 us
    pallas_call x1, Pallas kernels, turn_back(): pl.pallas_call(turn_back_kernel, out_shape=(shape(mid.shape, F32), shape(...  11.7 us
  transfers between devices with their start and end apart: 5, of which 2 were waited for; matrix products, arithmetic and copies ran while one was open for 0% of the time, Pallas kernels for 52%

profile of v2, /device:TPU:0, one launch (start us, length us, event | category | flops | bytes accessed | tf_op | source)
XLA Modules:
  0.0 369.3 jit_solution(1520099297871827371)
XLA Ops:
  0.6 3.0 collective-permute-start
  3.6 0.1 collective-permute-start.1
  3.7 0.8 multiply_sine_fusion
  4.5 9.4 %project.1 = (bf16[4,128,1536]{2,1,0:T(8,128)(2,1)}, bf16[4,128,128]{2,1,0:T(8,128)(2,1)}, f32[4,1024,128]{2,1,0:T(8,128)}, bf16[16,192,128]{2,1,0:T(8,128)(2,1)...) custom-call(s32[4]{0:T(128)} %variant.13, ...), custom_call_target="tpu_custom_call" | custom-call | flops 2013265920 | bytes 9437184 | tf_op jit(solution)/shard_map/project/pallas_call | solution.py:363
  13.9 31.1 %send_qkv.1 = (bf16[16,192,128]{2,1,0:T(8,128)(2,1)}, bf16[16,128,128]{2,1,0:T(8,128)(2,1)}) custom-call(bf16[16,192,128]{2,1,0:T(8,128)(2,1)} %get-tuple-element.77.refs_0_, bf16[16,128,128]{2,1,0:T(8,128)(2,1)} %get-tuple-element.78.refs_1_), custom_call_target="tpu_custom_call" | custom-call | tf_op jit(solution)/shard_map/send_qkv/pallas_call | solution.py:717
  45.1 10.9 %attention_forward.1 = (bf16[16,192,128]{2,1,0:T(8,128)(2,1)}, f32[16,192,128]{2,1,0:T(8,128)}, f32[8,8,768]{2,1,0:T(8,128)}) custom-call(s32[4,2048]{1,0:T(4,128)} %seg_ref.3, s32[4,2048]{1,0:T(4,128)} %seg_ref.3, bf16[16,192,128]{2,1,0:T(8,128)(2,1)} %get-tuple-element.79.q_ref, bf16[16,128,128]{2,1,0:T(8,128)(2,1)} %get-tuple-element.80.kv_ref), custom_call_target="tpu_custom_call" | custom-call | flops 1610612736 | bytes 1572864 | tf_op jit(solution)/shard_map/attention_forward/pallas_call | solution.py:198
  56.0 40.9 %send_attn.1 = (bf16[16,192,128]{2,1,0:T(8,128)(2,1)}, bf16[16,192,128]{2,1,0:T(8,128)(2,1)}) custom-call(bf16[16,192,128]{2,1,0:T(8,128)(2,1)} %get-tuple-element.81.x), custom_call_target="tpu_custom_call" | custom-call | tf_op jit(solution)/shard_map/send_attn/pallas_call | solution.py:791
  96.9 0.0 collective-permute-done.1.ao_x
  96.9 0.0 copy-start.6
  96.9 0.0 collective-permute-done.wo_x
  96.9 0.0 copy-start.5
  96.9 0.6 copy-done.6
  97.5 0.9 copy-done.5
  98.4 10.3 %middle.1 = (f32[4,128,1536]{2,1,0:T(8,128)}, bf16[4,128,1536]{2,1,0:T(8,128)(2,1)}, bf16[4,128,128]{2,1,0:T(8,128)(2,1)}) custom-call(s32[4]{0:T(128)} %variant.13, bf16[4,128,1536]{2,1,0:T(8,128)(2,1)} %refs_10_.1, f32[1536]{0:T(1024)} %gain_ref.5, bf16[4,768,128]{2,1,0:T(8,128)(2,1)} %bitcast.17, bf16[4,768,128]{2,1,0:T(8,128)(2,1)} %bitcast.20, ...), custom_call_target="tpu_custom_call" | custom-call | flops 2415919104 | bytes 9437184 | tf_op jit(solution)/shard_map/middle/pallas_call | solution.py:407
  108.7 28.3 %feed_forward.2 = (bf16[256,1664]{1,0:T(8,128)(2,1)}, bf16[256,128]{1,0:T(8,128)(2,1)}, bf16[256,3456]{1,0:T(8,128)(2,1)}, bf16[256,3456]{1,0:T(8,128)(2,1)}, bf16[256,3456]{1,0:T(8,128)(2,1)}) custom-call(s32[4]{0:T(128)} %variant.13, bf16[512,1536]{1,0:T(8,128)(2,1)} %bitcast.13, bf16[512,1536]{1,0:T(8,128)(2,1)} %bitcast.9, bf16[128,1536]{1,0:T(8,128)(2,1)} %ag.5, ...), custom_call_target="tpu_custom_call" | custom-call | flops 13589544960 | bytes 31850496 | tf_op jit(solution)/shard_map/feed_forward/pallas_call | solution.py:489
  137.0 0.0 copy-start.2
  137.0 28.7 %feed_forward.3 = (bf16[256,1664]{1,0:T(8,128)(2,1)}, bf16[256,128]{1,0:T(8,128)(2,1)}, bf16[256,3456]{1,0:T(8,128)(2,1)}, bf16[256,3456]{1,0:T(8,128)(2,1)}, bf16[256,3456]{1,0:T(8,128)(2,1)}) custom-call(s32[4]{0:T(128)} %variant.13, bf16[512,1536]{1,0:T(8,128)(2,1)} %bitcast.14, bf16[512,1536]{1,0:T(8,128)(2,1)} %bitcast.10, bf16[128,1536]{1,0:T(8,128)(2,1)} %ag.5, ...), custom_call_target="tpu_custom_call" | custom-call | flops 13589544960 | bytes 31850496 | tf_op jit(solution)/shard_map/feed_forward/pallas_call | solution.py:489
  165.7 0.0 copy-done.2
  165.7 0.6 collective-permute-start.2
  166.3 1.5 collective-permute-start.3
  167.8 14.9 %feed_down.1 = (bf16[512,1664]{1,0:T(8,128)(2,1)}, bf16[64,10368]{1,0:T(8,128)(2,1)}) custom-call(s32[4]{0:T(128)} %variant.13, bf16[256,128]{1,0:T(8,128)(2,1)} %get-tuple-element.90.refs_0_, bf16[256,3456]{1,0:T(8,128)(2,1)} %get-tuple-element.91.refs_1_, bf16[256,3456]{1,0:T(8,128)(2,1)} %get-tuple-element.92.refs_2_, ...), custom_call_target="tpu_custom_call" | custom-call | flops 5435817984 | bytes 10616832 | tf_op jit(solution)/shard_map/feed_down/pallas_call | solution.py:544
  182.7 5.0 %collective-permute-done.2.back_ax = bf16[256,1664]{1,0:T(8,128)(2,1)S(1)} collective-permute-done((bf16[256,1664]{1,0:T(8,128)(2,1)S(1)}, bf16[256,1664]{1,0:T(8,128)(2,1)S(1)}, u32[]{:S(2)}, u32[]{:S(2)}) %collective-permute-start.2) | collective-permute-done | bytes 852000 | tf_op jit(solution)/shard_map/ppermute | solution.py:1133
  187.6 0.0 copy-start.3
  187.6 17.0 %collective-permute-done.3.back_bx = bf16[256,1664]{1,0:T(8,128)(2,1)S(1)} collective-permute-done((bf16[256,1664]{1,0:T(8,128)(2,1)}, bf16[256,1664]{1,0:T(8,128)(2,1)S(1)}, u32[]{:S(2)}, u32[]{:S(2)}) %collective-permute-start.3) | collective-permute-done | bytes 852000 | tf_op jit(solution)/shard_map/ppermute | solution.py:1133
  204.6 0.0 copy-start.4
  204.6 0.9 copy-done.4
  205.5 0.0 copy-done.3
  205.5 0.0 copy-start
  205.5 11.7 %turn_back.1 = (f32[4,128,1536]{2,1,0:T(8,128)}, bf16[4,768,128]{2,1,0:T(8,128)(2,1)}, bf16[64,3072]{1,0:T(8,128)(2,1)}) custom-call(s32[4]{0:T(128)} %variant.13, f32[4,128,1536]{2,1,0:T(8,128)} %get-tuple-element.84.mid_ref, bf16[4,128,1536]{2,1,0:T(8,128)(2,1)} %get-tuple-element.85.n2_ref, bf16[4,128,1536]{2,1,0:T(8,128)(2,1)} %cot_ref.3, ...), custom_call_target="tpu_custom_call" | custom-call | flops 1207959552 | bytes 15728640 | tf_op jit(solution)/shard_map/turn_back/pallas_call | solution.py:604
  217.2 0.0 copy-done
  217.2 0.6 collective-permute-start.4
  217.9 20.4 %send_d_attn.1.do_ref = bf16[16,192,128]{2,1,0:T(8,128)(2,1)} custom-call(bf16[16,192,128]{2,1,0:T(8,128)(2,1)} %bitcast.16), custom_call_target="tpu_custom_call" | custom-call | tf_op jit(solution)/shard_map/send_d_attn/pallas_call | solution.py:717
  238.3 18.5 %attention_backward.1 = (bf16[16,192,128]{2,1,0:T(8,128)(2,1)}, bf16[16,128,128]{2,1,0:T(8,128)(2,1)}) custom-call(s32[4,2048]{1,0:T(4,128)} %seg_ref.3, s32[4,2048]{1,0:T(4,128)} %seg_ref.3, bf16[16,192,128]{2,1,0:T(8,128)(2,1)} %get-tuple-element.79.q_ref, bf16[16,128,128]{2,1,0:T(8,128)(2,1)} %get-tuple-element.80.kv_ref, ...), custom_call_target="tpu_custom_call" | custom-call | flops 4026531840 | bytes 1572864 | tf_op jit(solution)/shard_map/attention_backward/pallas_call | solution.py:223
  256.8 46.1 %send_dqkv.1 = (bf16[16,192,128]{2,1,0:T(8,128)(2,1)}, bf16[16,128,128]{2,1,0:T(8,128)(2,1)}) custom-call(bf16[16,192,128]{2,1,0:T(8,128)(2,1)} %get-tuple-element.104.refs_0_, bf16[16,128,128]{2,1,0:T(8,128)(2,1)} %get-tuple-element.105.refs_1_), custom_call_target="tpu_custom_call" | custom-call | tf_op jit(solution)/shard_map/send_dqkv/pallas_call | solution.py:717
  302.8 0.0 collective-permute-done.4
  302.9 0.0 copy-start.1
  302.9 1.2 copy-done.1
  304.1 5.2 %block_result.1 = (bf16[4,128,1536]{2,1,0:T(8,128)(2,1)}, bf16[64,768]{1,0:T(8,128)(2,1)}) custom-call(s32[4]{0:T(128)} %variant.13, f32[4,128,1536]{2,1,0:T(8,128)} %get-tuple-element.84.mid_ref, bf16[4,128,1664]{2,1,0:T(8,128)(2,1)} %bitcast.11, bf16[4,128,1664]{2,1,0:T(8,128)(2,1)} %bitcast.12, bf16[4,128,1536]{2,1,0:T(8,128)(2,1)} %cot_ref.3, ...), custom_call_target="tpu_custom_call" | custom-call | flops 50331648 | bytes 9437184 | tf_op jit(solution)/shard_map/block_result/pallas_call | solution.py:635
  309.3 55.3 %finish.1 = (bf16[4,128,1536]{2,1,0:T(8,128)(2,1)}, f32[8,14336]{1,0:T(8,128)}, f32[8,4096]{1,0:T(8,128)}, f32[8,3072]{1,0:T(8,128)}, f32[8,2304]{1,0:T(8,128)}) custom-call(bf16[4,768,128]{2,1,0:T(8,128)(2,1)} %bitcast.15, bf16[16,1,128,128]{3,2,1,0:T(8,128)(2,1)} %bitcast.19, f32[4,1024,128]{2,1,0:T(8,128)} %get-tuple-element.108.refs_2_, ...), custom_call_target="tpu_custom_call" | custom-call | tf_op jit(solution)/shard_map/finish/pallas_call | solution.py:1074
  364.6 2.0 unpack.1
  366.7 2.7 copy.46
  (2 shorter events, 0.0 us)
Async XLA Ops:
  0.6 96.2 %collective-permute-start = (bf16[768,1536]{1,0:T(8,128)(2,1)}, bf16[768,1536]{1,0:T(8,128)(2,1)S(1)}, u32[]{:S(2)}, u32[]{:S(2)}) collective-permute-start(bf16[768,1536]{1,0:T(8,128)(2,1)} %wo.3), channel_id=1, source_target_pairs={{0,1},{1,0},{2,3},{3,2},{4,5},{5,4},{6,7},{7,6},{8,9},{9,8},{10,11... | collective-permute-start | bytes 7077896 | tf_op jit(solution)/shard_map/ppermute | solution.py:1133
  3.6 93.2 %collective-permute-start.1 = (bf16[128,768]{1,0:T(8,128)(2,1)}, bf16[128,768]{1,0:T(8,128)(2,1)S(1)}, u32[]{:S(2)}, u32[]{:S(2)}) collective-permute-start(bf16[128,768]{1,0:T(8,128)(2,1)} %ao.3), channel_id=1, source_target_pairs={{0,1},{1,0},{2,3},{3,2},{4,5},{5,4},{6,7},{7,6},{8,9},{9,8},{10,11... | collective-permute-start | bytes 589832 | tf_op jit(solution)/shard_map/ppermute | solution.py:1133
  96.9 0.7 copy-start.6
  96.9 1.5 copy-start.5
  137.0 28.7 %copy-start.2 = (bf16[256,1664]{1,0:T(8,128)(2,1)S(1)}, bf16[256,1664]{1,0:T(8,128)(2,1)}, u32[]{:S(2)}) copy-start(bf16[256,1664]{1,0:T(8,128)(2,1)} %get-tuple-element.86.back_a) | copy-start | bytes 2555908
  165.7 21.9 %collective-permute-start.2 = (bf16[256,1664]{1,0:T(8,128)(2,1)S(1)}, bf16[256,1664]{1,0:T(8,128)(2,1)S(1)}, u32[]{:S(2)}, u32[]{:S(2)}) collective-permute-start(bf16[256,1664]{1,0:T(8,128)(2,1)S(1)} %copy-done.2), channel_id=1, source_target_pairs={{0,1},{1,0},{2,3},{3,2},{4,5},{5,4},{6,7},{7,6},{8,9},{9,8},{10,11... | collective-permute-start | bytes 2555912 | tf_op jit(solution)/shard_map/ppermute | solution.py:1133
  166.3 38.3 %collective-permute-start.3 = (bf16[256,1664]{1,0:T(8,128)(2,1)}, bf16[256,1664]{1,0:T(8,128)(2,1)S(1)}, u32[]{:S(2)}, u32[]{:S(2)}) collective-permute-start(bf16[256,1664]{1,0:T(8,128)(2,1)} %get-tuple-element.87.back_b), channel_id=1, source_target_pairs={{0,1},{1,0},{2,3},{3,2},{4,5},{5,4},{6,7},{7,6},{8,9},{9,8},{10,11... | collective-permute-start | bytes 2555912 | tf_op jit(solution)/shard_map/ppermute | solution.py:1133
  187.6 17.9 %copy-start.3 = (bf16[256,1664]{1,0:T(8,128)(2,1)}, bf16[256,1664]{1,0:T(8,128)(2,1)S(1)}, u32[]{:S(2)}) copy-start(bf16[256,1664]{1,0:T(8,128)(2,1)S(1)} %collective-permute-done.2.back_ax) | copy-start | bytes 2555908
  204.6 0.9 copy-start.4
  205.5 11.7 %copy-start = (bf16[512,1664]{1,0:T(8,128)(2,1)S(1)}, bf16[512,1664]{1,0:T(8,128)(2,1)}, u32[]{:S(2)}) copy-start(bf16[512,1664]{1,0:T(8,128)(2,1)} %get-tuple-element.99) | copy-start | bytes 5111812
  217.2 85.6 %collective-permute-start.4 = (bf16[512,1664]{1,0:T(8,128)(2,1)S(1)}, bf16[512,1664]{1,0:T(8,128)(2,1)S(1)}, u32[]{:S(2)}, u32[]{:S(2)}) collective-permute-start(bf16[512,1664]{1,0:T(8,128)(2,1)S(1)} %copy-done), channel_id=1, source_target_pairs={{0,1},{1,0},{2,3},{3,2},{4,5},{5,4},{6,7},{7,6},{8,9},{9,8},{10,11... | collective-permute-start | bytes 5111816 | tf_op jit(solution)/shard_map/ppermute | solution.py:1133
  302.9 1.2 copy-start.1

commit v3 on v2

v3 whole, which is shorter than its diff:
```python
import functools, jax, jax.numpy as jnp
from jax import lax
from jax.experimental import pallas as pl
from jax.experimental.pallas import tpu as pltpu
from jax.sharding import PartitionSpec as P

HEAD_DIM = 64
LOG2E = 1.4426950408889634
MESH = pl.DeviceIdType.MESH
SMEM = pl.BlockSpec(memory_space=pltpu.SMEM)
VM = pl.BlockSpec(memory_space=pltpu.VMEM)
RANK = 16
EPSILON = 1e-05
THETA_BASE = 1000000.0
BF = jnp.bfloat16
F32 = jnp.float32
NT = (((1,), (1,)), ((), ()))
BIG = pltpu.CompilerParams(vmem_limit_bytes=60 * 2**20)


def cost(rows, width, columns, products, moved):
    return pl.CostEstimate(flops=2 * products * rows * width * columns, bytes_accessed=moved, transcendentals=0)

ANYWHERE = pl.BlockSpec(memory_space=pl.ANY)


def mm(a, b):
    return jnp.dot(a, b, preferred_element_type=F32)


def mm_nt(a, b):
    return lax.dot_general(a, b, NT, preferred_element_type=F32)


def shape(dims, kind):
    return jax.ShapeDtypeStruct(dims, kind)


def remote(source, target, send, recv, device):
    return pltpu.make_async_remote_copy(
        src_ref=source, dst_ref=target, send_sem=send, recv_sem=recv, device_id=device, device_id_type=MESH
    )


def own_rows(ref, variant):
    return ref[pl.ds(pl.multiple_of(variant * RANK, RANK), RANK), :]


def norm_back(u, gain, c):
    scale = lax.rsqrt(jnp.mean(u * u, axis=-1, keepdims=True) + EPSILON)
    y = u * scale
    w = c * gain
    return scale * (w - y * jnp.mean(w * y, axis=-1, keepdims=True))


def turn(values, cosine, sine):
    half = HEAD_DIM // 2
    a, b = values[:, :half], values[:, half:]
    return jnp.concatenate([a * cosine - b * sine, b * cosine + a * sine], axis=1)


def rank_halves(blocks):
    return jnp.concatenate([b[: RANK // 2] for b in blocks] + [b[RANK // 2 :] for b in blocks], axis=0)


def column(ref):
    return jnp.transpose(jnp.broadcast_to(ref[...][None, :], (128, ref.shape[0])))


def project_kernel(
    variant, x_ref, gain_ref, wq, wk, wv, aq, ak, av, bq, bk, bv, qg_ref, kg_ref, cos_ref, sin_ref, *refs,
):
    n1_ref, h_ref, pre_ref, q_ref, kv_ref, ac_ref, bc_ref, gains_ref, pick_ref = refs[6:15]
    n1_s, sems = refs[21:]
    picks = [
        pltpu.make_async_copy(
            refs[n].at[pl.ds(pl.multiple_of(variant[s] * RANK, RANK), RANK), :],
            refs[15 + n].at[pl.ds(s * RANK, RANK), :], sems.at[n, s],
        )
        for n in range(6)
        for s in range(x_ref.shape[0])
    ]
    for c in picks:
        c.start()
    sequences, rows, width = x_ref.shape
    qw, kw = wq.shape[1], wk.shape[1]
    heads_q, heads_k = qw // HEAD_DIM, kw // HEAD_DIM
    cosine, sine = cos_ref[...], sin_ref[...]
    qg, kg = column(qg_ref), column(kg_ref)
    gains_ref[0], gains_ref[1] = qg, kg
    gain = gain_ref[...][None, :]
    for v in range(pick_ref.shape[0]):
        for s in range(sequences):
            pick_ref[v, s] = jnp.full((8, 128), jnp.where(variant[s] == v, 1.0, 0.0), F32)

    def prepare(t, gains):
        heads = t.reshape(t.shape[0] // HEAD_DIM, HEAD_DIM, rows)
        scale = lax.rsqrt(jnp.mean(heads * heads, axis=1, keepdims=True) + EPSILON)
        return turn(heads * scale * gains, cosine, sine).astype(BF)

    def pair(p, _):
        for i in (0, 1):
            x = x_ref[2 * p + i].astype(F32)
            scale = lax.rsqrt(jnp.mean(x * x, axis=-1, keepdims=True) + EPSILON)
            n1 = (x * scale * gain).astype(BF)
            n1_ref[2 * p + i] = n1
            n1_s[i * rows : (i + 1) * rows, :] = n1
        n1 = n1_s[...]
        base = [mm(n1, w[...]) for w in (wq, wk, wv)]
        for i in (0, 1):
            s = 2 * p + i
            v = variant[s]
            half = slice(i * rows, (i + 1) * rows)
            a = jnp.concatenate([own_rows(f, v) for f in (aq, ak, av)], axis=0)
            b = [own_rows(f, v) for f in (bq, bk, bv)]
            ac_ref[s] = a
            bc_ref[s] = jnp.concatenate(b, axis=1)
            h = mm_nt(n1_s[half, :], a).astype(BF)
            h_ref[s] = jnp.concatenate([h, jnp.zeros((rows, 128 - 3 * RANK), BF)], axis=1)
            h2 = h * 2
            q, k, val = (
                jnp.transpose(base[n][half] + mm(h2[:, n * RANK : (n + 1) * RANK], b[n])) for n in range(3)
            )
            pre_ref[s, :qw, :] = q
            pre_ref[s, qw:, :] = k
            group = heads_q // heads_k
            q = prepare(q, qg).reshape(heads_k, group * HEAD_DIM, rows)
            k = prepare(k, kg)
            val = val.astype(BF).reshape(heads_k, HEAD_DIM, rows)
            q_ref[pl.ds(s * heads_k, heads_k)] = q
            kv_ref[pl.ds(s * heads_k, heads_k), :HEAD_DIM, :] = k
            kv_ref[pl.ds(s * heads_k, heads_k), HEAD_DIM:, :] = val
        return 0

    lax.fori_loop(0, sequences // 2, pair, 0)
    for c in picks:
        c.wait()


def project(variant, x, gain, weights, ins, outs, qg, kg, tables, factors):
    sequences, rows, width = x.shape
    qw, kw = weights[0].shape[1], weights[1].shape[1]
    units = sequences * kw // HEAD_DIM
    return pl.pallas_call(
        project_kernel,
        out_shape=(
            shape(x.shape, BF), shape((sequences, rows, 128), BF), shape((sequences, qw + kw, rows), F32),
            shape((units, qw // kw * HEAD_DIM, rows), BF), shape((units, 2 * HEAD_DIM, rows), BF),
            shape((sequences, 3 * RANK, width), BF), shape((sequences, RANK, qw + 2 * kw), BF),
            shape((2, HEAD_DIM, rows), F32), shape((ins[0].shape[0] // RANK, sequences, 8, 128), F32),
        ) + tuple(shape((sequences * RANK, f.shape[1]), BF) for f in factors),
        in_specs=[SMEM] + [VM] * 15 + [ANYWHERE] * 6,
        out_specs=(VM,) * 15,
        scratch_shapes=[pltpu.VMEM((2 * rows, width), BF), pltpu.SemaphoreType.DMA((6, sequences))],
        compiler_params=BIG,
        cost_estimate=cost(sequences * rows, width, qw + 2 * kw, 1, 12 * sequences * rows * width),
        name="project",
    )(variant, x, gain, *weights, *ins, *outs, qg, kg, *tables, *factors)


def middle_kernel(variant, x_ref, gain_ref, attn, attn_x, wo, wo_x, ao, ao_x, bo, mid_ref, n2_ref, h_ref, lhs, lhs_x):
    sequences, rows, width = x_ref.shape

    def pair(p, _):
        for i in (0, 1):
            half = slice(i * rows, (i + 1) * rows)
            lhs[half, :] = jnp.transpose(attn[2 * p + i])
            lhs_x[half, :] = jnp.transpose(attn_x[2 * p + i])
        out = mm(lhs[...], wo[...]) + mm(lhs_x[...], wo_x[...])
        for i in (0, 1):
            s = 2 * p + i
            v = variant[s]
            half = slice(i * rows, (i + 1) * rows)
            h = (mm_nt(lhs[half, :], own_rows(ao, v)) + mm_nt(lhs_x[half, :], own_rows(ao_x, v))).astype(BF)
            h_ref[s] = jnp.concatenate([h, jnp.zeros((rows, 128 - RANK), BF)], axis=1)
            mid = x_ref[s].astype(F32) + (out[half] + mm(h * 2, own_rows(bo, v)))
            mid_ref[s] = mid
            scale = lax.rsqrt(jnp.mean(mid * mid, axis=-1, keepdims=True) + EPSILON)
            n2_ref[s] = (mid * scale * gain_ref[...][None, :]).astype(BF)
        return 0

    lax.fori_loop(0, sequences // 2, pair, 0)


def middle(variant, x, gain, attn, attn_x, wo, wo_x, ao, ao_x, bo):
    sequences, rows, width = x.shape
    inner = attn.shape[1]
    return pl.pallas_call(
        middle_kernel,
        out_shape=(shape(x.shape, F32), shape(x.shape, BF), shape((sequences, rows, 128), BF)),
        in_specs=[SMEM] + [VM] * 9,
        out_specs=(VM,) * 3,
        scratch_shapes=[pltpu.VMEM((2 * rows, inner), BF), pltpu.VMEM((2 * rows, inner), BF)],
        compiler_params=BIG,
        cost_estimate=cost(sequences * rows, width, inner, 2, 12 * sequences * rows * width),
        name="middle",
    )(variant, x, gain, attn, attn_x, wo, wo_x, ao, ao_x, bo)


def feed_kernel(
    chunks, n2_ref, cot_ref, ag, au, bd, wg_ref, wu_ref, wd_ref, bg_ref, bu_ref, ad_ref,
    back_ref, back_x_ref, down_ref, grads_ref,
    hg, hu, dhd, hs, dn2_acc, dhg_acc, dhu_acc, down_acc, h_acc, hidden_s, dgate_s, dup_s, back_s, down_s,
    send_sems, recv_sems, keep_sems,
):
    step = pl.program_id(0)
    rows, width = n2_ref.shape
    tiles, tile = hidden_s.shape[0], hidden_s.shape[2]
    part = rows // chunks
    seqs = rows // 128
    ranks = seqs * RANK
    chunk, f = step // tiles, lax.rem(step, tiles)
    here = pl.ds(pl.multiple_of(chunk * part, part), part)
    across = {"tp": 1 - lax.axis_index("tp")}

    def keep(first, count):
        row = lax.broadcasted_iota(jnp.int32, (count, ranks), 0) // 128 + first // 128
        return row == lax.broadcasted_iota(jnp.int32, (count, ranks), 1) // RANK

    def compact(a, first=0):
        a = jnp.where(keep(first, a.shape[0]), a, 0.0)
        return sum(a[:, i * RANK : (i + 1) * RANK] for i in range(seqs))

    def copies(c):
        there = pl.ds(c * part, part)
        return (
            remote(back_s.at[there, :], back_x_ref.at[there, :], send_sems.at[c], recv_sems.at[c], across),
            pltpu.make_async_copy(back_s.at[there, :], back_ref.at[there, :], keep_sems.at[c]),
        )

    down_copy = pltpu.make_async_copy(down_s, down_ref, keep_sems.at[chunks])

    @pl.when(step == 0)
    def _():
        barrier = pltpu.get_barrier_semaphore()
        pl.semaphore_signal(barrier, inc=1, device_id=across, device_id_type=MESH)
        pl.semaphore_wait(barrier, 1)
        g = jnp.where(keep(0, rows), mm_nt(n2_ref[...], ag[...]), 0.0)
        u = jnp.where(keep(0, rows), mm_nt(n2_ref[...], au[...]), 0.0)
        d = jnp.where(keep(0, rows), mm_nt(cot_ref[...], bd[...]) * 2.0, 0.0)
        hg[...] = (g * 2.0).astype(BF)
        hu[...] = (u * 2.0).astype(BF)
        dhd[...] = d.astype(BF)
        for n, a in enumerate((g * 2.0, u * 2.0, d)):
            turned = jnp.transpose(jnp.concatenate([a, jnp.zeros((rows, 128 - ranks), F32)], axis=1))
            rows_of = [turned[i * RANK : (i + 1) * RANK] for i in range(seqs)]
            hs[n] = rank_halves(rows_of).astype(BF)
        down_acc[...] = jnp.zeros_like(down_acc)
        h_acc[...] = jnp.zeros_like(h_acc)

    @pl.when((step < chunks * tiles) & (f == 0))
    def _():
        dn2_acc[...] = jnp.zeros_like(dn2_acc)
        dhg_acc[...] = jnp.zeros_like(dhg_acc)
        dhu_acc[...] = jnp.zeros_like(dhu_acc)

    @pl.when(step < chunks * tiles)
    def _():
        n2 = n2_ref[here, :]
        bg, bu, ad = bg_ref[...], bu_ref[...], ad_ref[...]
        gate = mm(n2, wg_ref[...]) + mm(hg[here, :], bg)
        up = mm(n2, wu_ref[...]) + mm(hu[here, :], bu)
        sg = 1.0 / (1.0 + jnp.exp(-gate))
        silu = gate * sg
        hidden_s[f, here, :] = (silu * up).astype(BF)
        dh = mm_nt(cot_ref[here, :], wd_ref[...]) + mm(dhd[here, :], ad)
        dg = (dh * up * sg * (1.0 + gate * (1.0 - sg))).astype(BF)
        du = (dh * silu).astype(BF)
        dgate_s[f, here, :] = dg
        dup_s[f, here, :] = du
        dn2_acc[...] += mm_nt(dg, wg_ref[...]) + mm_nt(du, wu_ref[...])
        dhg_acc[...] += mm_nt(dg, bg)
        dhu_acc[...] += mm_nt(du, bu)

    for c in range(chunks):

        @pl.when(step == (c + 1) * tiles - 1)
        def _():
            there = slice(c * part, (c + 1) * part)
            back_s[there, :width] = dn2_acc[...].astype(BF)
            small = [compact(a[...], c * part) * 2 for a in (dhg_acc, dhu_acc)]
            back_s[there, width:] = jnp.concatenate(small + [jnp.zeros((part, 128 - 2 * RANK), F32)], axis=1).astype(BF)
            for copy in copies(c):
                copy.start()

    @pl.when(step >= chunks * tiles)
    def _():
        hidden = hidden_s[f]
        down_acc[...] += mm(hidden, wd_ref[...])
        h_acc[...] += mm_nt(hidden, ad_ref[...])
        for n, kept in enumerate((dgate_s, dup_s, hidden_s)):
            grads_ref[:, n * tile : (n + 1) * tile] = mm(hs[n], kept[f]).astype(BF)

    @pl.when(step == pl.num_programs(0) - 1)
    def _():
        down_s[:, :width] = down_acc[...].astype(BF)
        down_s[:, width:] = jnp.concatenate([compact(h_acc[...]), jnp.zeros((rows, 128 - RANK), F32)], axis=1).astype(BF)
        down_copy.start()
        for c in range(chunks):
            for copy in copies(c):
                copy.wait()
        down_copy.wait()


def feed_tile(units):
    return 1152 if units % 1152 == 0 else units


def feed(chunks, n2, cot, ag, au, bd, wg, wu, wd, bg, bu, ad, collective_id):
    rows, width = n2.shape
    stacked, units = bg.shape
    tile = feed_tile(units)
    tiles, part, ranks = units // tile, rows // chunks, rows // 128 * RANK
    last = chunks * tiles
    once = lambda dims: pl.BlockSpec(dims, lambda i: (0, 0), pipeline_mode=pl.Buffered(1))
    early = lambda height: pl.BlockSpec((height, tile), lambda i: (0, jnp.where(i < last, lax.rem(i, tiles), tiles - 1)))
    down_rows = pl.BlockSpec((tile, width), lambda i: (lax.rem(i, tiles), 0))
    down_cols = pl.BlockSpec((stacked, tile), lambda i: (0, lax.rem(i, tiles)))
    vm, dma = pltpu.VMEM, pltpu.SemaphoreType.DMA
    wide = shape((rows, width + 128), BF)
    return pl.pallas_call(
        functools.partial(feed_kernel, chunks),
        grid=(last + tiles,),
        out_shape=(wide, wide, wide, shape((ranks, 3 * units), BF)),
        in_specs=[once((rows, width)), once((rows, width))] + [once((stacked, width))] * 3
        + [early(width), early(width), down_rows, early(stacked), early(stacked), down_cols],
        out_specs=(ANYWHERE,) * 3 + (pl.BlockSpec((ranks, 3 * tile), lambda i: (0, jnp.maximum(i - last, 0))),),
        scratch_shapes=[vm((rows, ranks), BF)] * 3
        + [vm((3, ranks, rows), BF), vm((part, width), F32), vm((part, ranks), F32), vm((part, ranks), F32)]
        + [vm((rows, width), F32), vm((rows, ranks), F32)] + [vm((tiles, rows, tile), BF)] * 3
        + [vm((rows, width + 128), BF)] * 2 + [dma((chunks,)), dma((chunks,)), dma((chunks + 1,))],
        compiler_params=pltpu.CompilerParams(
            collective_id=collective_id, has_side_effects=True, vmem_limit_bytes=62 * 2**20
        ),
        cost_estimate=cost(rows, width, units, 6, 12 * width * units),
        name="feed_forward",
    )(n2, cot, ag, au, bd, wg, wu, wd, bg, bu, ad)


def turn_back_kernel(
    variant, mid_ref, n2_ref, cot_ref, back_ref, back_x_ref, hout_ref, attn_ref, gain_ref, ag, au, bo, ao, wo,
    dmid_ref, dattn_ref, grads_ref, branch_s, hidden_s,
):
    sequences, rows, width = mid_ref.shape
    half = pl.multiple_of(lax.axis_index("tp") * (width // 2), width // 2)
    mine = pl.ds(half, width // 2)
    gain = gain_ref[...][None, :]
    blocks = []
    for s in range(sequences):
        v = variant[s]
        whole = back_ref[s].astype(F32) + back_x_ref[s].astype(F32)
        dh = whole[:, width : width + 2 * RANK].astype(BF)
        c = whole[:, :width] + mm(dh, jnp.concatenate([own_rows(ag, v), own_rows(au, v)], axis=0))
        d_mid = cot_ref[s].astype(F32) + norm_back(mid_ref[s], gain, c)
        dmid_ref[s] = d_mid
        here = slice(s * rows, (s + 1) * rows)
        branch_s[here, :] = d_mid.astype(BF)
        dho = (mm_nt(branch_s[here, :], own_rows(bo, v)) * 2.0).astype(BF)
        hidden_s[here, :] = mm(dho, own_rows(ao, v))
        wide = jnp.concatenate([dh, dho, hout_ref[s][:, :RANK] * 2, jnp.zeros((rows, 128 - 4 * RANK), BF)], axis=1)
        t = jnp.transpose(wide.astype(F32)).astype(BF)
        blocks.append(
            jnp.concatenate(
                [
                    mm_nt(t[2 * RANK : 3 * RANK], attn_ref[s]),
                    mm(t[:RANK], n2_ref[s, :, mine]),
                    mm(t[RANK : 2 * RANK], n2_ref[s, :, mine]),
                    mm(t[3 * RANK : 4 * RANK], branch_s[here, mine]),
                ],
                axis=1,
            )
        )
    grads_ref[...] = rank_halves(blocks).astype(BF)
    for p in range(sequences // 2):
        d_attn = mm_nt(branch_s[2 * p * rows : 2 * (p + 1) * rows, :], wo[...]) + hidden_s[2 * p * rows : 2 * (p + 1) * rows, :]
        for i in (0, 1):
            dattn_ref[2 * p + i] = jnp.transpose(d_attn[i * rows : (i + 1) * rows]).astype(BF)


def turn_back(variant, mid, n2, cot, back, back_x, hout, attn, gain, ag, au, bo, ao, wo):
    sequences, rows, width = mid.shape
    inner = wo.shape[0]
    return pl.pallas_call(
        turn_back_kernel,
        out_shape=(
            shape(mid.shape, F32), shape((sequences, inner, rows), BF),
            shape((sequences * RANK, inner + 3 * (width // 2)), BF),
        ),
        in_specs=[SMEM] + [VM] * 13,
        out_specs=(VM,) * 3,
        scratch_shapes=[pltpu.VMEM((sequences * rows, width), BF), pltpu.VMEM((sequences * rows, inner), F32)],
        compiler_params=BIG,
        cost_estimate=cost(sequences * rows, width, inner, 1, 20 * sequences * rows * width),
        name="turn_back",
    )(variant, mid, n2, cot, back, back_x, hout, attn, gain, ag, au, bo, ao, wo)


def result_kernel(variant, mid_ref, down_ref, down_x_ref, cot_ref, bd, out_ref, grads_ref):
    sequences, rows, width = mid_ref.shape
    mine = pl.ds(pl.multiple_of(lax.axis_index("tp") * (width // 2), width // 2), width // 2)
    blocks = []
    for s in range(sequences):
        v = variant[s]
        whole = down_ref[s].astype(F32) + down_x_ref[s].astype(F32)
        h = whole[:, width : width + RANK].astype(BF) * 2
        out_ref[s] = (mid_ref[s] + (whole[:, :width] + mm(h, own_rows(bd, v)))).astype(BF)
        t = jnp.transpose(jnp.concatenate([h, jnp.zeros((rows, 128 - RANK), BF)], axis=1).astype(F32)).astype(BF)
        blocks.append(mm(t[:RANK], cot_ref[s, :, mine]))
    grads_ref[...] = rank_halves(blocks).astype(BF)


def result(variant, mid, down, down_x, cot, bd):
    sequences, rows, width = mid.shape
    return pl.pallas_call(
        result_kernel,
        out_shape=(shape(mid.shape, BF), shape((sequences * RANK, width // 2), BF)),
        in_specs=[SMEM] + [VM] * 5,
        out_specs=(VM,) * 2,
        compiler_params=BIG,
        cost_estimate=cost(sequences * rows, width, 16, 2, 12 * sequences * rows * width),
        name="block_result",
    )(variant, mid, down, down_x, cot, bd)


TILE = 512
BLOCKS = TILE // 128
SUB = 512
SCALE = HEAD_DIM**-0.5


def document_starts(seg_ref, seq, seg_rows, starts):
    sequences, length = seg_ref.shape
    blocks = length // 128
    number = lax.broadcasted_iota(jnp.int32, (sequences, length), 0)
    row = jnp.sum(jnp.where(number == seq, seg_ref[...], 0), axis=0, keepdims=True).astype(F32)
    for b in range(blocks):
        seg_rows[b] = row[:, b * 128 : (b + 1) * 128]
        starts[b] = jnp.zeros((1, 128), jnp.int32)

    def keys(j, _):
        k = jnp.transpose(jnp.broadcast_to(seg_rows[j], (128, 128)))

        def queries(i, _):
            earlier = jnp.where(k < jnp.broadcast_to(seg_rows[i], (128, 128)), 1.0, 0.0)
            starts[i] += jnp.sum(earlier, axis=0, keepdims=True).astype(jnp.int32)
            return 0

        return lax.fori_loop(j, blocks, queries, 0)

    lax.fori_loop(0, blocks, keys, 0)


def query_rows(starts, tile, stride, part):
    lanes = lax.broadcasted_iota(jnp.int32, (1, 128), 1)
    blocks = [(BLOCKS * tile + b) * stride + part for b in range(BLOCKS)]
    position = jnp.concatenate([b * 128 + lanes for b in blocks], axis=1)
    return position, jnp.concatenate([starts[b] for b in blocks], axis=1)


def key_range(tile, stride, part):
    return BLOCKS * tile * stride // BLOCKS + part // BLOCKS, ((BLOCKS * tile + BLOCKS - 1) * stride + part) // BLOCKS + 1


def keep_pairs(p, first, start, position, causal):
    key = lax.broadcasted_iota(jnp.int32, p.shape, 0)
    keep = key >= jnp.broadcast_to(start - first, p.shape)
    if causal:
        keep = keep & (key <= jnp.broadcast_to(position - first, p.shape))
    return jnp.where(keep, p, 0.0)


def across_blocks(ref, tile, rows):
    return jnp.concatenate([ref[BLOCKS * tile + b, rows, :] for b in range(BLOCKS)], axis=1)


def load_keys(kv_ref, kb, vt):
    def load(j, _):
        for b in range(BLOCKS):
            kb[j, b * 128 : (b + 1) * 128, :] = jnp.transpose(kv_ref[BLOCKS * j + b, :HEAD_DIM, :])
            vt[j, :HEAD_DIM, b * 128 : (b + 1) * 128] = kv_ref[BLOCKS * j + b, HEAD_DIM:, :]
        vt[j, HEAD_DIM:, :] = jnp.ones((16, TILE), BF)
        return 0

    lax.fori_loop(0, kv_ref.shape[0] // BLOCKS, load, 0)


def head_forward(h, stride, part, q_ref, starts, kb, vt, acc, of_ref, lse_ref, done):
    rows = pl.ds(h * HEAD_DIM, HEAD_DIM)

    def q_step(i, _):
        position, start = query_rows(starts, i, stride, part)
        qt = across_blocks(q_ref, i, rows)
        acc[...] = jnp.zeros_like(acc)

        def k_step(causal, j, _):
            total = acc[...]
            for c in range(TILE // SUB):
                keys = slice(c * SUB, (c + 1) * SUB)
                p = jnp.exp2(mm(kb[j, keys, :], qt) * (LOG2E * SCALE))
                p = keep_pairs(p, j * TILE + c * SUB, start, position, causal)
                total = total + mm(vt[j, :, keys], p.astype(BF))
            acc[...] = total
            return 0

        whole, end = key_range(i, stride, part)
        lax.fori_loop(0, whole, functools.partial(k_step, False), 0)
        lax.fori_loop(whole, end, functools.partial(k_step, True), 0)
        total = acc[HEAD_DIM : HEAD_DIM + 1, :]
        lse_ref[h, i] = jnp.broadcast_to(jnp.log2(total), (8, TILE))
        out = acc[:HEAD_DIM, :] / total
        for b in range(BLOCKS):
            of_ref[BLOCKS * i + b, rows, :] = out[:, b * 128 : (b + 1) * 128]
        done(i, out.astype(BF))
        return 0

    lax.fori_loop(0, q_ref.shape[0] // BLOCKS, q_step, 0)


def pair_backward(h, i, j, causal, stride, part, qt, q3, dot_t, do3, lse_ref, delta, starts, kb, vb, kt, dqt, dk, dv):
    position, start = query_rows(starts, i, stride, part)
    dq = dqt[h, i]
    for c in range(TILE // SUB):
        keys = slice(c * SUB, (c + 1) * SUB)
        p = jnp.exp2(mm(kb[j, keys, :], qt[h, i]) * (LOG2E * SCALE) - lse_ref[h, i, 0:1, :])
        p = keep_pairs(p, j * TILE + c * SUB, start, position, causal)
        dp = mm(vb[j, keys, :], dot_t[h, i])
        ds = (p * (dp - delta[h, i, 0:1, :])).astype(BF)
        dv[j, keys, :] += mm(p.astype(BF), do3[h, i])
        dk[j, keys, :] += mm(ds, q3[h, i])
        dq = dq + mm(kt[j, :, keys], ds)
    dqt[h, i] = dq


def head_rows(h):
    return pl.ds(h * HEAD_DIM, HEAD_DIM)


def loop(low, high, step):
    def body(k, _):
        step(k)
        return 0

    lax.fori_loop(low, high, body, 0)


def class_copy(count, parts, source, target, send, recv):
    def make(index, sender):
        return remote(
            source(index), target(sender), send.at[index], recv.at[sender],
            {"ctx": index * parts + lax.rem(lax.axis_index("ctx"), parts)},
        )

    return make


def attend_kernel(
    count, parts, units_per_seq, seg_ref, q_ref, kv_ref,
    q_all, kv_all, of_ref, lse_ref, starts, home, home_x,
    q_in, kv_in, o_buf, kb, vt, acc, seg_rows,
    kv_send, kv_recv, q_send, q_recv, o_send, o_recv, x_send, x_recv, own_sems, out_sems,
):
    me = lax.axis_index("ctx")
    units = count // parts
    unit, part = me // parts, lax.rem(me, parts)
    group = q_ref.shape[1] // HEAD_DIM
    across = {"tp": 1 - lax.axis_index("tp")}
    barrier = pltpu.get_barrier_semaphore()
    pl.semaphore_signal(barrier, inc=1, device_id=across, device_id_type=MESH)
    loop(
        1, count,
        lambda k: pl.semaphore_signal(barrier, inc=1, device_id={"ctx": lax.rem(me + k, count)}, device_id_type=MESH),
    )
    own = [pltpu.make_async_copy(kv_ref.at[unit], kv_in.at[me], own_sems.at[0])]
    own.append(pltpu.make_async_copy(q_ref.at[unit], q_in.at[unit], own_sems.at[1]))
    for c in own:
        c.start()
    pl.semaphore_wait(barrier, count)

    def kv_copy(device, sender):
        return remote(
            kv_ref.at[device // parts], kv_in.at[sender], kv_send.at[device], kv_recv.at[sender], {"ctx": device}
        )

    q_copy = [
        class_copy(
            count, parts, lambda i, h=h: q_ref.at[i, head_rows(h), :], lambda i, h=h: q_in.at[i, head_rows(h), :],
            q_send.at[h], q_recv.at[h],
        )
        for h in range(group)
    ]
    o_copy = [
        class_copy(
            count, parts, lambda i, h=h: o_buf.at[h, i], lambda i, h=h: home.at[i, head_rows(h), :],
            o_send.at[h], o_recv.at[h],
        )
        for h in range(group)
    ]

    def x_copy(h, i):
        place = (i, head_rows(h), slice(None))
        return remote(home.at[place], home_x.at[place], x_send.at[h, i], x_recv.at[h, i], across)

    def turn_of(k):
        return lax.rem(unit + k, units)

    loop(1, count, lambda k: kv_copy(lax.rem(me + k, count), me).start())
    for h in range(group):
        loop(1, units, lambda k, h=h: q_copy[h](turn_of(k), unit).start())
    document_starts(seg_ref, unit // units_per_seq, seg_rows, starts)
    for c in own:
        c.wait()
    loop(1, count, lambda k: kv_copy(me, lax.rem(me + k, count)).wait_recv())
    load_keys(kv_in, kb, vt)
    saves = [pltpu.make_async_copy(kv_in, kv_all, out_sems.at[0])]
    saves[0].start()

    def keep_own(h):
        return pltpu.make_async_copy(o_buf.at[h, unit], home.at[unit, head_rows(h), :], own_sems.at[2 + h])

    def pass_on(h):
        keep_own(h).wait()
        x_copy(h, unit).start()

        def relay(k):
            other = turn_of(units - k)
            o_copy[h](unit, other).wait_recv()
            x_copy(h, other).start()

        loop(1, units, relay)

    for h in range(group):
        loop(1, units, lambda k, h=h: q_copy[h](unit, turn_of(k)).wait_recv())
        if h == group - 1:
            saves.append(pltpu.make_async_copy(q_in, q_all, out_sems.at[1]))
            saves[1].start()

        def done(i, out, h=h):
            for b in range(BLOCKS):
                block = BLOCKS * i + b
                o_buf[h, block] = out[:, b * 128 : (b + 1) * 128]

                @pl.when(block == unit)
                def _():
                    keep_own(h).start()

                @pl.when(block != unit)
                def _():
                    o_copy[h](block, unit).start()

        head_forward(h, parts, part, q_in, starts, kb, vt, acc, of_ref, lse_ref, done)
        if h > 0:
            pass_on(h - 1)
    pass_on(group - 1)
    for c in saves:
        c.wait()
    loop(1, count, lambda k: kv_copy(lax.rem(me + k, count), me).wait_send())
    for h in range(group):

        def finish_block(k, h=h):
            q_copy[h](turn_of(k), unit).wait_send()
            o_copy[h](turn_of(k), unit).wait_send()

        loop(1, units, finish_block)

        def finish_across(i, h=h):
            x_copy(h, i).wait_send()
            x_copy(h, i).wait_recv()

        loop(0, units, finish_across)


def attend(segs, q, kv, count, parts, units_per_seq, collective_id):
    units, qrows, _ = q.shape
    group, tiles, ktiles = qrows // HEAD_DIM, units // BLOCKS, count // BLOCKS
    dma, vm = pltpu.SemaphoreType.DMA, pltpu.VMEM
    kv_shape = (count,) + kv.shape[1:]
    return pl.pallas_call(
        functools.partial(attend_kernel, count, parts, units_per_seq),
        out_shape=(
            shape(q.shape, BF), shape(kv_shape, BF), shape(q.shape, F32), shape((group, tiles, 8, TILE), F32),
            shape((count, 1, 128), jnp.int32), shape(q.shape, BF), shape(q.shape, BF),
        ),
        in_specs=[VM, ANYWHERE, ANYWHERE],
        out_specs=(ANYWHERE, ANYWHERE, VM, VM, VM, ANYWHERE, ANYWHERE),
        scratch_shapes=[
            vm(q.shape, BF), vm(kv_shape, BF), vm((group, units, HEAD_DIM, 128), BF), vm((ktiles, TILE, HEAD_DIM), BF),
            vm((ktiles, HEAD_DIM + 16, TILE), BF), vm((HEAD_DIM + 16, TILE), F32), vm((count, 1, 128), F32),
            dma((count,)), dma((count,)),
        ]
        + [dma((group, units))] * 6 + [dma((2 + group,)), dma((2,))],
        compiler_params=pltpu.CompilerParams(
            collective_id=collective_id, has_side_effects=True, vmem_limit_bytes=60 * 2**20
        ),
        name="attend",
    )(segs, q, kv)


def attend_back_kernel(
    count, parts, do_ref, q_all, kv_all, of_ref, lse_ref, starts, dq_home, dkv_home,
    do_in, dq_buf, dkv_buf, kb, vb, kt, qt, q3, dot_t, do3, delta, dqt, dk, dv,
    do_send, do_recv, dq_send, dq_recv, dkv_send, dkv_recv, own_sems,
):
    me = lax.axis_index("ctx")
    units = count // parts
    unit, part = me // parts, lax.rem(me, parts)
    group, tiles, ktiles = q_all.shape[1] // HEAD_DIM, units // BLOCKS, count // BLOCKS
    barrier = pltpu.get_barrier_semaphore()
    loop(
        1, count,
        lambda k: pl.semaphore_signal(barrier, inc=1, device_id={"ctx": lax.rem(me + k, count)}, device_id_type=MESH),
    )
    own_do = pltpu.make_async_copy(do_ref.at[unit], do_in.at[unit], own_sems.at[0])
    own_do.start()
    pl.semaphore_wait(barrier, count - 1)

    def turn_of(k):
        return lax.rem(unit + k, units)

    do_copy = [
        class_copy(
            count, parts, lambda i, h=h: do_ref.at[i, head_rows(h), :], lambda i, h=h: do_in.at[i, head_rows(h), :],
            do_send.at[h], do_recv.at[h],
        )
        for h in range(group)
    ]
    dq_copy = [
        class_copy(
            count, parts, lambda i, h=h: dq_buf.at[h, i], lambda i, h=h: dq_home.at[i, head_rows(h), :],
            dq_send.at[h], dq_recv.at[h],
        )
        for h in range(group)
    ]

    def dkv_copy(device, sender):
        return remote(dkv_buf.at[device], dkv_home.at[sender], dkv_send.at[device], dkv_recv.at[sender], {"ctx": device})

    own_dkv = pltpu.make_async_copy(dkv_buf.at[me], dkv_home.at[me], own_sems.at[1])

    def own_dq(h):
        return pltpu.make_async_copy(dq_buf.at[h, unit], dq_home.at[unit, head_rows(h), :], own_sems.at[2 + h])

    for h in range(group):
        loop(1, units, lambda k, h=h: do_copy[h](turn_of(k), unit).start())

    def load_kv(j):
        for b in range(BLOCKS):
            lanes = slice(b * 128, (b + 1) * 128)
            kt[j, :, lanes] = kv_all[BLOCKS * j + b, :HEAD_DIM, :]
            kb[j, lanes, :] = jnp.transpose(kv_all[BLOCKS * j + b, :HEAD_DIM, :])
            vb[j, lanes, :] = jnp.transpose(kv_all[BLOCKS * j + b, HEAD_DIM:, :])

    def load_q(i):
        for h in range(group):
            for b in range(BLOCKS):
                lanes = slice(b * 128, (b + 1) * 128)
                q = q_all[BLOCKS * i + b, h * HEAD_DIM : (h + 1) * HEAD_DIM, :]
                qt[h, i, :, lanes] = q
                q3[h, i, lanes, :] = jnp.transpose(q)
            dqt[h, i] = jnp.zeros((HEAD_DIM, TILE), F32)

    def load_do(h, i):
        rows = slice(h * HEAD_DIM, (h + 1) * HEAD_DIM)
        for b in range(BLOCKS):
            lanes = slice(b * 128, (b + 1) * 128)
            g = do_in[BLOCKS * i + b, rows, :]
            dot_t[h, i, :, lanes] = g
            do3[h, i, lanes, :] = jnp.transpose(g)
            d = jnp.sum(g.astype(F32) * of_ref[BLOCKS * i + b, rows, :], axis=0, keepdims=True)
            delta[h, i, :, lanes] = jnp.broadcast_to(d, (8, 128))

    loop(0, ktiles, load_kv)
    loop(0, tiles, load_q)

    def last_tile(i):
        return key_range(i, parts, part)[1] - 1

    def run(h, j):
        low = jnp.maximum(BLOCKS * j - part + parts - 1, 0) // (BLOCKS * parts)
        full = jnp.minimum((BLOCKS * (j + 1) - part + BLOCKS * parts - 1) // (BLOCKS * parts), tiles)

        def pair(causal, i):
            pair_backward(
                h, i, j, causal, parts, part, qt, q3, dot_t, do3, lse_ref, delta, starts, kb, vb, kt, dqt, dk, dv
            )

        loop(low, full, functools.partial(pair, True))
        loop(full, tiles, functools.partial(pair, False))

    def emit_keys(j):
        for b in range(BLOCKS):
            rows = slice(b * 128, (b + 1) * 128)
            block = BLOCKS * j + b
            dkv_buf[block, :HEAD_DIM, :] = jnp.transpose(dk[j, rows, :] * SCALE).astype(BF)
            dkv_buf[block, HEAD_DIM:, :] = jnp.transpose(dv[j, rows, :]).astype(BF)

            @pl.when(block == me)
            def _():
                own_dkv.start()

            @pl.when(block != me)
            def _():
                dkv_copy(block, me).start()

    def emit_queries(h, j, i):
        @pl.when(last_tile(i) == j)
        def _():
            for b in range(BLOCKS):
                block = BLOCKS * i + b
                dq_buf[h, block] = (dqt[h, i, :, b * 128 : (b + 1) * 128] * SCALE).astype(BF)

                @pl.when(block == unit)
                def _():
                    own_dq(h).start()

                @pl.when(block != unit)
                def _():
                    dq_copy[h](block, unit).start()

    dk[...] = jnp.zeros_like(dk)
    dv[...] = jnp.zeros_like(dv)
    own_do.wait()
    for h in range(group):
        loop(1, units, lambda k, h=h: do_copy[h](unit, turn_of(k)).wait_recv())
        loop(0, tiles, functools.partial(load_do, h))

        def key_step(j, h=h):
            run(h, j)
            if h == group - 1:
                emit_keys(j)
            loop(0, tiles, functools.partial(emit_queries, h, j))

        loop(0, ktiles, key_step)
    for h in range(group):
        own_dq(h).wait()
    own_dkv.wait()

    def finish_full(k):
        other = lax.rem(me + k, count)
        dkv_copy(other, me).wait_send()
        dkv_copy(me, other).wait_recv()

    loop(1, count, finish_full)

    def finish_class(k):
        other = turn_of(k)
        for h in range(group):
            do_copy[h](other, unit).wait_send()
            dq_copy[h](other, unit).wait_send()
            dq_copy[h](unit, other).wait_recv()

    loop(1, units, finish_class)


def attend_back(do, q, kv, of, lse, starts, count, parts, collective_id):
    units, qrows, _ = q.shape
    group, tiles, ktiles = qrows // HEAD_DIM, units // BLOCKS, count // BLOCKS
    dma, vm = pltpu.SemaphoreType.DMA, pltpu.VMEM
    return pl.pallas_call(
        functools.partial(attend_back_kernel, count, parts),
        out_shape=(shape(q.shape, BF), shape(kv.shape, BF)),
        in_specs=[ANYWHERE] + [VM] * 5,
        out_specs=(ANYWHERE, ANYWHERE),
        scratch_shapes=[vm(q.shape, BF), vm((group, units, HEAD_DIM, 128), BF), vm(kv.shape, BF)]
        + [vm((ktiles, TILE, HEAD_DIM), BF)] * 2 + [vm((ktiles, HEAD_DIM, TILE), BF)]
        + [vm((group, tiles, HEAD_DIM, TILE), BF), vm((group, tiles, TILE, HEAD_DIM), BF)] * 2
        + [vm((group, tiles, 8, TILE), F32), vm((group, tiles, HEAD_DIM, TILE), F32)]
        + [vm((ktiles, TILE, HEAD_DIM), F32)] * 2
        + [dma((group, units))] * 4 + [dma((count,))] * 2 + [dma((2 + group,))],
        compiler_params=pltpu.CompilerParams(
            collective_id=collective_id, has_side_effects=True, vmem_limit_bytes=60 * 2**20
        ),
        name="attend_back",
    )(do, q, kv, of, lse, starts)


def finish_kernel(reduce, count, widths, shared, *refs):
    refs = list(refs)
    take = lambda n: [refs.pop(0) for _ in range(n)]
    dq_ref, dkv_ref, pre_ref, h_ref, gains, cos_ref, sin_ref, gain_ref, bc_ref, pick_ref = take(10)
    far = take(7)
    grads = take(3) if reduce else []
    (out_ref,) = take(1)
    gout = take(4) if reduce else take(1)
    x, d_mid, n1, wq, wk, wv, ac = near = take(7)
    d_n, gb, dh_own, dh_other, dh_sum, sbuf, rbuf, gq = take(8)
    near_sems, dh_send, dh_recv, xsend, xrecv = take(5)
    sequences, inner, rows = dq_ref.shape
    width = out_ref.shape[2]
    kw = wk.shape[1]
    half_rows = sequences * RANK // 2
    me = lax.axis_index("ctx")
    across = {"tp": 1 - lax.axis_index("tp")}
    mine = pl.ds(pl.multiple_of(lax.axis_index("tp") * (width // 2), width // 2), width // 2)

    loads = [pltpu.make_async_copy(f, n, near_sems.at[i]) for i, (f, n) in enumerate(zip(far, near))]
    barrier = pltpu.get_barrier_semaphore()
    pl.semaphore_signal(barrier, inc=1, device_id=across, device_id_type=MESH)
    peers = 1
    if reduce:
        planes, plane_ins, fin_outs, fin_ins = take(2), take(2), take(2), take(2)
        own, core_in = take(2)
        own_sems, core_send, core_recv = take(3)
        plane_send, plane_recv, fin_send, fin_recv = take(4)
        (last_sems,) = take(1)
        chips = count // 2
        chip, core = me // 2, lax.rem(me, 2)
        twin = {"ctx": 2 * chip + 1 - core}
        pl.semaphore_signal(barrier, inc=1, device_id=twin, device_id_type=MESH)

        def at_chip(k):
            return lax.rem(chip + k, chips)

        def greet(k, _):
            pl.semaphore_signal(barrier, inc=1, device_id={"ctx": 2 * at_chip(k) + core}, device_id_type=MESH)
            return 0

        lax.fori_loop(1, chips, greet, 0)
        peers += chips

        def part_of(ref, who):
            size = ref.shape[0] // 2
            return ref.at[pl.ds(pl.multiple_of(who * size, 16), size), :]

        known, w_qkv = sum(widths[:3]), widths[3]
        own_loads, to_twin, at = [], [], 0
        for i, ref in enumerate(grads):
            place = slice(at, at + widths[i])
            at += widths[i]
            own_loads.append(pltpu.make_async_copy(part_of(ref, core), own.at[:, place], own_sems.at[i]))
            to_twin.append(
                remote(part_of(ref, 1 - core), core_in.at[:, place], core_send.at[i], core_recv.at[i], twin)
            )
        to_twin.append(remote(gq.at[1 - core], core_in.at[:, known : known + w_qkv], core_send.at[3], core_recv.at[3], twin))
        for c in own_loads:
            c.start()
    for i in (3, 4, 5, 2, 6, 0, 1):
        loads[i].start()
    pl.semaphore_wait(barrier, peers)
    if reduce:
        for c in to_twin[:3]:
            c.start()

    cosine, sine = cos_ref[...], sin_ref[...]
    heads_k = kw // HEAD_DIM
    cuts = (slice(0, inner), slice(inner, inner + kw), slice(inner + kw, inner + 2 * kw))

    def prepare_back(pre, gains, c):
        u = pre.reshape(pre.shape[0] // HEAD_DIM, HEAD_DIM, rows)
        scale = lax.rsqrt(jnp.mean(u * u, axis=1, keepdims=True) + EPSILON)
        y = u * scale
        w = turn(c.reshape(u.shape).astype(F32), cosine, -sine) * gains
        return (scale * (w - y * jnp.mean(w * y, axis=1, keepdims=True))).reshape(pre.shape)

    def first_step(s):
        dkv = dkv_ref[s * heads_k : (s + 1) * heads_k].astype(F32)
        dkv = jnp.sum(dkv, axis=1).astype(BF) if dkv.shape[1] > 1 else dkv[:, 0].astype(BF)
        d_q = prepare_back(pre_ref[s, :inner, :], gains[0], dq_ref[s])
        d_k = prepare_back(pre_ref[s, inner:, :], gains[1], dkv[:, :HEAD_DIM, :].reshape(kw, rows))
        d_v = dkv[:, HEAD_DIM:, :].reshape(kw, rows).astype(F32)
        d = jnp.transpose(jnp.concatenate([d_q, d_k, d_v], axis=0)).astype(BF)
        d_n[s] = d
        dh = [mm_nt(d[:, c], bc_ref[s, :, c]) * 2.0 for c in cuts]
        dh_own[s] = jnp.concatenate(dh + [jnp.zeros((rows, 128 - 3 * RANK), F32)], axis=1).astype(BF)
        t = (jnp.transpose(h_ref[s].astype(F32)) * 2.0).astype(BF)
        gb[s] = jnp.concatenate([mm(t[i * RANK : (i + 1) * RANK], d[:, c]) for i, c in enumerate(cuts)], axis=1)

    def part_copy(s):
        return remote(sbuf.at[s], rbuf.at[s], xsend.at[s], xrecv.at[s], across)

    dh_copies = []

    def send_pair(p):
        pair = pl.ds(2 * p, 2)
        first_step(2 * p)
        first_step(2 * p + 1)
        dh_copies.append(remote(dh_own.at[pair], dh_other.at[pair], dh_send.at[p], dh_recv.at[p], across))
        dh_copies[-1].start()
        if p == 0:
            for i in (3, 4, 5):
                loads[i].wait()
        d = jnp.concatenate([d_n[2 * p], d_n[2 * p + 1]], axis=0)
        part = mm_nt(d[:, cuts[0]], wq[...]) + mm_nt(d[:, cuts[1]], wk[...]) + mm_nt(d[:, cuts[2]], wv[...])
        for i in (0, 1):
            sbuf[2 * p + i] = part[i * rows : (i + 1) * rows].astype(BF)
            part_copy(2 * p + i).start()

    def plane_copy(g, k, slot):
        chunk = planes[g].shape[1] // chips
        return remote(
            planes[g].at[:, pl.ds(pl.multiple_of(k * chunk, 128), chunk)], plane_ins[g].at[slot],
            plane_send.at[g, k], plane_recv.at[g, slot], {"ctx": 2 * k + core},
        )

    def fin_copy(g, k, slot):
        return remote(
            fin_outs[g].at[k], fin_ins[g].at[slot], fin_send.at[g, k], fin_recv.at[g, slot], {"ctx": 2 * k + core}
        )

    def each_chip(step):
        def body(k, _):
            step(at_chip(k))
            return 0

        lax.fori_loop(1, chips, body, 0)

    def to_plane(g):
        chunk = planes[g].shape[1] // chips
        each_chip(lambda k: plane_copy(g, k, chip).start())
        plane_ins[g][chip] = planes[g][:, pl.ds(pl.multiple_of(chip * chunk, 128), chunk)]

    def to_owners(g):
        each_chip(lambda k: plane_copy(g, k, k).wait_recv())
        total = plane_ins[g][0].astype(F32)
        for k in range(1, chips):
            total = total + plane_ins[g][k].astype(F32)
        chunk, per = total.shape[1], RANK // 2
        for k in range(chips):
            row = jnp.zeros((per, chunk), F32)
            for s in range(sequences):
                row = row + total[s * per : (s + 1) * per] * pick_ref[k, s][:, :1]
            fin_outs[g][k] = jnp.concatenate([row[:, : chunk // 2], row[:, chunk // 2 :]], axis=0).astype(BF)
        each_chip(lambda k: fin_copy(g, k, chip).start())
        fin_ins[g][chip] = fin_outs[g][chip]

    def rows_in(g):
        each_chip(lambda k: fin_copy(g, k, k).wait_recv())
        rows_ref, per = gout[g], RANK // 2
        chunk = rows_ref.shape[1] // chips
        for k in range(chips):
            block = fin_ins[g][k].astype(F32)
            rows_ref[:, k * chunk : k * chunk + chunk // 2] = block[:per]
            rows_ref[:, k * chunk + chunk // 2 : (k + 1) * chunk] = block[per:]
        copy = remote(
            rows_ref.at[:, shared[g][0] : shared[g][1]], gout[2 + g], last_sems.at[g], last_sems.at[2 + g], across
        )
        copy.start()
        return copy

    def last_step(s):
        part_copy(s).wait_recv()
        c = sbuf[s].astype(F32) + rbuf[s].astype(F32) + mm(dh_sum[s][:, : 3 * RANK], ac[s])
        out_ref[s] = (d_mid[s] + norm_back(x[s].astype(F32), gain_ref[...][None, :], c)).astype(BF)

    pairs = sequences // 2
    send_pair(0)
    if reduce:
        for c in own_loads:
            c.wait()
        for c in to_twin[:3]:
            c.wait_recv()
        planes[0][:, :known] = (own[...].astype(F32) + core_in[:, :known].astype(F32)).astype(BF)
        if planes[0].shape[1] > known:
            planes[0][:, known:] = jnp.zeros((half_rows, planes[0].shape[1] - known), BF)
        to_plane(0)
    for p in range(1, pairs):
        send_pair(p)
    loads[2].wait()
    blocks = []
    for s in range(sequences):
        if s % 2 == 0:
            dh_copies[s // 2].wait_recv()
        dh = (dh_own[s].astype(F32) + dh_other[s].astype(F32)).astype(BF)
        dh_sum[s] = dh
        t = jnp.transpose(dh.astype(F32)).astype(BF)
        wide = mm(t[: 3 * RANK], n1[s, :, mine])
        blocks.append(jnp.concatenate([wide[i * RANK : (i + 1) * RANK] for i in range(3)] + [gb[s]], axis=1))
    everything = rank_halves(blocks)
    for b in (0, 1):
        gq[b] = everything[b * half_rows : (b + 1) * half_rows].astype(BF)
    if reduce:
        to_twin[3].start()
    for i in (6, 0, 1):
        loads[i].wait()
    if reduce:
        to_owners(0)
        to_twin[3].wait_recv()
        planes[1][:, :w_qkv] = (gq[core].astype(F32) + core_in[:, known : known + w_qkv].astype(F32)).astype(BF)
        if planes[1].shape[1] > w_qkv:
            planes[1][:, w_qkv:] = jnp.zeros((half_rows, planes[1].shape[1] - w_qkv), BF)
        to_plane(1)
        last_step(0)
        to_owners(1)
        shared_copies = [rows_in(0)]
        last_step(1)
        shared_copies.append(rows_in(1))
        for s in range(2, sequences):
            last_step(s)
        for c in shared_copies:
            c.wait()
        for c in to_twin:
            c.wait_send()
        for g in (0, 1):
            each_chip(lambda k, g=g: plane_copy(g, k, chip).wait_send())
            each_chip(lambda k, g=g: fin_copy(g, k, chip).wait_send())
    else:
        for s in range(sequences):
            last_step(s)
        gout[0][...] = gq[...]
    for c in dh_copies:
        c.wait_send()
    for s in range(sequences):
        part_copy(s).wait_send()


def finish(reduce, count, dq, dkv, pre, h, gains, tables, gain, bc, pick, x, d_mid, n1, weights, ac, grads, shared, collective_id):
    sequences, rows, width = x.shape
    inner, kw = weights[0].shape[1], weights[1].shape[1]
    w_qkv = 3 * (width // 2) + inner + 2 * kw
    half_rows = sequences * RANK // 2
    dma = pltpu.SemaphoreType.DMA
    far = (x, d_mid, n1) + tuple(weights) + (ac,)
    widths = ()
    gshape = (shape((2, half_rows, w_qkv), BF),)
    scratch = [pltpu.VMEM(a.shape, a.dtype) for a in far]
    scratch += [
        pltpu.VMEM((sequences, rows, inner + 2 * kw), BF),
        pltpu.VMEM((sequences, RANK, inner + 2 * kw), F32),
        pltpu.VMEM((sequences, rows, 128), BF),
        pltpu.VMEM((sequences, rows, 128), BF),
        pltpu.VMEM((sequences, rows, 128), BF),
        pltpu.VMEM(x.shape, BF),
        pltpu.VMEM(x.shape, BF),
        pltpu.VMEM((2, half_rows, w_qkv), BF),
        dma((7,)), dma((sequences // 2,)), dma((sequences // 2,)), dma((sequences,)), dma((sequences,)),
    ]
    extra = ()
    if reduce:
        chips = count // 2
        widths = tuple(g.shape[1] for g in grads) + (w_qkv,)
        padded = [-(-n // (256 * chips)) * 256 * chips for n in (sum(widths[:3]), w_qkv)]
        gshape = tuple(shape((RANK // 2, n), F32) for n in padded)
        gshape += tuple(shape((RANK // 2, b - a), F32) for a, b in shared)
        scratch += [pltpu.VMEM((half_rows, n), BF) for n in padded]
        scratch += [pltpu.VMEM((chips, half_rows, n // chips), BF) for n in padded]
        scratch += [pltpu.VMEM((chips, RANK, n // chips // 2), BF) for n in padded] * 2
        scratch += [
            pltpu.VMEM((half_rows, sum(widths[:3])), BF),
            pltpu.VMEM((half_rows, sum(widths)), BF),
            dma((3,)), dma((4,)), dma((4,)),
        ]
        scratch += [dma((2, chips))] * 4 + [dma((4,))]
        extra = tuple(grads)
    return pl.pallas_call(
        functools.partial(finish_kernel, reduce, count, widths, shared),
        out_shape=(shape(x.shape, BF),) + gshape,
        in_specs=[VM] * 10 + [ANYWHERE] * (7 + len(extra)),
        out_specs=(VM,) * (1 + len(gshape)),
        scratch_shapes=scratch,
        compiler_params=pltpu.CompilerParams(
            collective_id=collective_id, has_side_effects=True, vmem_limit_bytes=60 * 2**20
        ),
        name="finish",
    )(dq, dkv, pre, h, gains, *tables, gain, bc, pick, *far, *extra)


def unpack_kernel(hidden_units, tile, inner, kw, first, second, first_x, second_x, *outs):
    ga_query, gb_query, ga_key, gb_key, ga_value, gb_value, ga_out, gb_out, ga_gate, gb_gate, ga_up, gb_up, ga_down, gb_down = outs
    width = ga_query.shape[1]
    w = width // 2
    lower = lax.axis_index("tp") == 0
    for f in range(hidden_units // tile):
        for n, out in enumerate((gb_gate, gb_up, ga_down)):
            out[:, f * tile : (f + 1) * tile] = first[:, (3 * f + n) * tile : (3 * f + n + 1) * tile]
    at = 3 * hidden_units
    ga_out[...] = first[:, at : at + inner]

    def join(out, own, own_at, other, i):
        a = own[:, own_at + i * w : own_at + (i + 1) * w]
        b = other[:, i * w : (i + 1) * w]
        out[:, :w] = jnp.where(lower, a, b)
        out[:, w:] = jnp.where(lower, b, a)

    for i, out in enumerate((ga_gate, ga_up, gb_out, gb_down)):
        join(out, first, at + inner, first_x, i)
    for i, out in enumerate((ga_query, ga_key, ga_value)):
        join(out, second, 0, second_x, i)
    at = 3 * w
    gb_query[...] = second[:, at : at + inner]
    gb_key[...] = second[:, at + inner : at + inner + kw]
    gb_value[...] = second[:, at + inner + kw : at + inner + 2 * kw]


def unpack(first, second, first_x, second_x, width, hidden_units, tile, inner, kw):
    sizes = (width, inner, width, kw, width, kw, inner, width, width, hidden_units, width, hidden_units, hidden_units, width)
    return pl.pallas_call(
        functools.partial(unpack_kernel, hidden_units, tile, inner, kw),
        out_shape=tuple(shape((first.shape[0], n), F32) for n in sizes),
        in_specs=[VM] * 4,
        out_specs=(VM,) * 14,
        name="unpack",
    )(first, second, first_x, second_x)


def rotary_tables(positions):
    half = HEAD_DIM // 2
    frequencies = THETA_BASE ** (-jnp.arange(half, dtype=F32) * 2.0 / HEAD_DIM)
    angles = frequencies[:, None] * positions.astype(F32)[None, :]
    return jnp.cos(angles), jnp.sin(angles)


def swap(values):
    return lax.ppermute(values, "tp", [(0, 1), (1, 0)])


def reduce_scatter_rows(grads, count):
    rows, columns = grads.shape
    index = lax.axis_index("ctx")
    held = grads.reshape(count, rows // count, columns)
    bit = 1
    while bit < count:
        mine = (index // bit) % 2
        pairs = held.reshape(held.shape[0] // 2, 2, held.shape[1], columns)
        kept = lax.dynamic_index_in_dim(pairs, mine, 1, keepdims=False)
        sent = lax.dynamic_index_in_dim(pairs, 1 - mine, 1, keepdims=False).astype(BF)
        held = kept.astype(F32) + lax.ppermute(sent, "ctx", [(i, i ^ bit) for i in range(count)]).astype(F32)
        bit *= 2
    return held[0]


def local(
    tokens, output_cotangent, segment_ids, variant, attn_gain, ffn_gain, q_gain, k_gain,
    query_matrix, key_matrix, value_matrix, output_matrix, gate_matrix, up_matrix, down_matrix,
    query_input_factor, query_output_factor, key_input_factor, key_output_factor,
    value_input_factor, value_output_factor, output_input_factor, output_output_factor,
    gate_input_factor, gate_output_factor, up_input_factor, up_output_factor,
    down_input_factor, down_output_factor,
):
    sequences, rows_here, width = tokens.shape
    count = lax.axis_size("ctx")
    index = lax.axis_index("ctx")
    inner, kw = query_matrix.shape[1], key_matrix.shape[1]
    key_heads = kw // HEAD_DIM
    units = sequences * key_heads
    parts = count // units
    stacked = query_input_factor.shape[0]
    reduce_here = stacked // count == RANK // 2
    tables = rotary_tables(index * rows_here + jnp.arange(rows_here, dtype=jnp.int32))
    weights = (query_matrix, key_matrix, value_matrix)
    ins = (query_input_factor, key_input_factor, value_input_factor)
    outs = (query_output_factor, key_output_factor, value_output_factor)

    output_matrix_other = swap(output_matrix)
    output_input_other = swap(output_input_factor)

    n1, h_one, pre, queries, keys_values, ac, bc, gains, pick, *chosen = project(
        variant, tokens, attn_gain, weights, ins, outs, q_gain, k_gain, tables,
        (gate_input_factor, up_input_factor, down_output_factor, gate_output_factor, up_output_factor, down_input_factor),
    )
    *kept, attn, attn_other = attend(segment_ids, queries, keys_values, count, parts, key_heads, 0)
    attn, attn_other = (a.reshape(sequences, inner, rows_here) for a in (attn, attn_other))
    mid, n2, h_out = middle(
        variant, tokens, ffn_gain, attn, attn_other, output_matrix, output_matrix_other,
        output_input_factor, output_input_other, output_output_factor,
    )

    flat = lambda a: a.reshape(sequences * rows_here, -1)
    by_seq = lambda a: a.reshape(sequences, rows_here, -1)
    back, back_other, down, g_ffn = feed(
        2, flat(n2), flat(output_cotangent), *chosen[:3], gate_matrix, up_matrix, down_matrix, *chosen[3:], 3,
    )
    d_mid, d_attn, g_mid = turn_back(
        variant, mid, n2, output_cotangent, by_seq(back), by_seq(back_other), h_out, attn, ffn_gain,
        gate_input_factor, up_input_factor, output_output_factor, output_input_factor, output_matrix,
    )
    d_attn = d_attn.reshape(queries.shape)
    d_attn, down = lax.optimization_barrier((d_attn, down))
    down_other = swap(down)
    dq, dkv = attend_back(d_attn, *kept, count, parts, 1)
    block_result, g_down = result(variant, mid, by_seq(down), by_seq(down_other), output_cotangent, down_output_factor)

    w = width // 2
    hidden_units = gate_matrix.shape[1]
    tile = feed_tile(hidden_units)
    at = 3 * hidden_units + inner
    shared = ((at, at + 4 * w), (0, 3 * w))
    ends = finish(
        reduce_here, count, dq.reshape(sequences, inner, rows_here), dkv.reshape(units, parts, 2 * HEAD_DIM, rows_here),
        pre, h_one, gains, tables, attn_gain, bc, pick, tokens, d_mid, n1, weights, ac,
        (g_ffn, g_mid, g_down), shared, 2,
    )
    if reduce_here:
        owned = ends[1:]
    else:
        per = RANK // 2
        pick = (jnp.arange(stacked // RANK, dtype=jnp.int32)[:, None] == variant[None, :]).astype(F32)
        owned, other = [], []
        for grads, (low, high) in zip((jnp.concatenate([g_ffn, g_mid, g_down], axis=1), ends[1]), shared):
            grads = grads.reshape(2, sequences, per, -1).astype(F32)
            dense = jnp.sum(pick[:, None, :, None, None] * grads[None], axis=2)
            owned.append(reduce_scatter_rows(dense.reshape(stacked, -1), count))
            other.append(swap(owned[-1][:, low:high]))
        owned = owned + other
    return (block_result, ends[0]) + tuple(unpack(*owned, width, hidden_units, tile, inner, kw))


def solution(mesh):
    rows, whole, columns = P(None, "ctx", None), P(), P(None, "tp")
    owned, owned_half = P("ctx", None), P("ctx", "tp")
    return jax.shard_map(
        local,
        mesh=mesh,
        in_specs=(rows, rows) + (whole,) * 6
        + (columns, columns, columns, P("tp", None), columns, columns, P("tp", None))
        + (whole, columns) * 3 + (columns, whole) + (whole, columns) * 2 + (columns, whole),
        out_specs=(
            rows, rows, owned, owned_half, owned, owned_half, owned, owned_half,
            owned_half, owned, owned, owned_half, owned, owned_half, owned_half, owned,
        ),
        check_vma=False,
    )
```

time: 369 us -> 306 us (0.83)
  Pallas kernels: 334 us -> 295 us
  waiting for transfers between devices: 22 us -> 0.01 us
    pallas_call x9 -> x3, Pallas kernels: 240 us -> 191 us  [the longest x1 69.6 us: feed(): pl.pallas_call(functools.partial(feed_kernel, chunks), grid=(last + tiles...]
    ppermute x5 -> x3, waiting for transfers between devices: 22 us -> 0.01 us  [swap(): return lax.ppermute(values, 'tp', [(0, 1), (1, 0)])]
    pallas_call x1, Pallas kernels: 55.3 us -> 63.9 us  [finish(): pl.pallas_call(functools.partial(finish_kernel, reduce, count, widths, sh...]
  transfers between devices with their start and end apart: 5 -> 3, of which waited for: 2 -> 0; matrix products, arithmetic and copies ran while one was open for 0% -> 0% of each run, Pallas kernels for 52% -> 43%
where the time goes in v3:
time: 306 us
  Pallas kernels  295 us (96%)
  local copies, waits for them, and re-layouts  5.31 us (2%)
  starting transfers between devices  4.2 us (1%)
    pallas_call x1, Pallas kernels, feed(): pl.pallas_call(functools.partial(feed_kernel, chunks), grid=(last + tiles...  69.6 us
    pallas_call x1, Pallas kernels, attend(): pl.pallas_call(functools.partial(attend_kernel, count, parts, units_per_s...  65.6 us
    pallas_call x1, Pallas kernels, finish(): pl.pallas_call(functools.partial(finish_kernel, reduce, count, widths, sh...  63.9 us
    pallas_call x1, Pallas kernels, attend_back(): pl.pallas_call(functools.partial(attend_back_kernel, count, parts), out_s...  55.3 us
    pallas_call x1, Pallas kernels, turn_back(): pl.pallas_call(turn_back_kernel, out_shape=(shape(mid.shape, F32), shape(...  11.7 us
    pallas_call x1, Pallas kernels, project(): pl.pallas_call(project_kernel, out_shape=(shape(x.shape, BF), shape((sequ...  10.8 us
    pallas_call x1, Pallas kernels, middle(): pl.pallas_call(middle_kernel, out_shape=(shape(x.shape, F32), shape(x.sha...  10.3 us
  transfers between devices with their start and end apart: 3, of which 0 were waited for; matrix products, arithmetic and copies ran while one was open for 0% of the time, Pallas kernels for 43%

profile of v3, /device:TPU:0, one launch (start us, length us, event | category | flops | bytes accessed | tf_op | source)
XLA Modules:
  0.0 305.6 jit_solution(6130761678164424863)
XLA Ops:
  0.6 3.0 collective-permute-start
  3.6 0.1 collective-permute-start.1
  3.7 0.8 multiply_sine_fusion
  4.5 10.8 %project.1 = (bf16[4,128,1536]{2,1,0:T(8,128)(2,1)}, bf16[4,128,128]{2,1,0:T(8,128)(2,1)}, f32[4,1024,128]{2,1,0:T(8,128)}, bf16[16,192,128]{2,1,0:T(8,128)(2,1)...) custom-call(s32[4]{0:T(128)} %variant.7, ...), custom_call_target="tpu_custom_call" | custom-call | flops 2013265920 | bytes 9437184 | tf_op jit(solution)/shard_map/project/pallas_call | solution.py:144
  15.3 65.6 %attend.1 = (bf16[16,192,128]{2,1,0:T(8,128)(2,1)}, bf16[16,128,128]{2,1,0:T(8,128)(2,1)}, f32[16,192,128]{2,1,0:T(8,128)}, f32[3,4,8,512]{3,2,1,0:T(8,128)}, s3...) custom-call(s32[4,2048]{1,0:T(4,128)} %seg_ref.1, ...), custom_call_target="tpu_custom_call" | custom-call | tf_op jit(solution)/shard_map/attend/pallas_call | solution.py:677
  81.0 0.0 collective-permute-done.1.ao_x
  81.0 0.0 copy-start.3
  81.0 0.0 collective-permute-done.wo_x
  81.0 0.0 copy-start.2
  81.0 0.6 copy-done.3
  81.7 0.8 copy-done.2
  82.5 10.3 %middle.1 = (f32[4,128,1536]{2,1,0:T(8,128)}, bf16[4,128,1536]{2,1,0:T(8,128)(2,1)}, bf16[4,128,128]{2,1,0:T(8,128)(2,1)}) custom-call(s32[4]{0:T(128)} %variant.7, bf16[4,128,1536]{2,1,0:T(8,128)(2,1)} %refs_10_.1, f32[1536]{0:T(1024)} %gain_ref.5, bf16[4,768,128]{2,1,0:T(8,128)(2,1)} %bitcast.19, bf16[4,768,128]{2,1,0:T(8,128)(2,1)} %bitcast.22, ...), custom_call_target="tpu_custom_call" | custom-call | flops 2415919104 | bytes 9437184 | tf_op jit(solution)/shard_map/middle/pallas_call | solution.py:188
  92.8 69.6 %feed_forward.1 = (bf16[512,1664]{1,0:T(8,128)(2,1)}, bf16[512,1664]{1,0:T(8,128)(2,1)}, bf16[512,1664]{1,0:T(8,128)(2,1)}, bf16[64,10368]{1,0:T(8,128)(2,1)}) custom-call(bf16[512,1536]{1,0:T(8,128)(2,1)} %bitcast.16, bf16[512,1536]{1,0:T(8,128)(2,1)} %bitcast.11, bf16[64,1536]{1,0:T(8,128)(2,1)} %get-tuple-element.79.ag, ...), custom_call_target="tpu_custom_call" | custom-call | flops 32614907904 | bytes 63700992 | tf_op jit(solution)/shard_map/feed_forward/pallas_call | solution.py:321
  162.4 0.0 copy-start
  162.4 11.7 %turn_back.1 = (f32[4,128,1536]{2,1,0:T(8,128)}, bf16[4,768,128]{2,1,0:T(8,128)(2,1)}, bf16[64,3072]{1,0:T(8,128)(2,1)}) custom-call(s32[4]{0:T(128)} %variant.7, f32[4,128,1536]{2,1,0:T(8,128)} %get-tuple-element.77.mid_ref, bf16[4,128,1536]{2,1,0:T(8,128)(2,1)} %get-tuple-element.78.n2_ref, bf16[4,128,1536]{2,1,0:T(8,128)(2,1)} %cot_ref.3, ...), custom_call_target="tpu_custom_call" | custom-call | flops 1207959552 | bytes 15728640 | tf_op jit(solution)/shard_map/turn_back/pallas_call | solution.py:383
  174.1 0.0 copy-done
  174.1 1.1 collective-permute-start.2
  175.2 55.3 %attend_back.1 = (bf16[16,192,128]{2,1,0:T(8,128)(2,1)}, bf16[16,128,128]{2,1,0:T(8,128)(2,1)}) custom-call(bf16[16,192,128]{2,1,0:T(8,128)(2,1)} %bitcast.18, bf16[16,192,128]{2,1,0:T(8,128)(2,1)} %get-tuple-element.93.q_all, bf16[16,128,128]{2,1,0:T(8,128)(2,1)} %get-tuple-element.94.kv_all, f32[16,192,128]{2,1,0:T(8,128)} %get-tuple-element.95.of_ref, ...), custom_call_target="tpu_custom_call" | custom-call | tf_op jit(solution)/shard_map/attend_back/pallas_call | solution.py:858
  230.6 0.0 collective-permute-done.2
  230.6 0.0 copy-start.1
  230.6 1.2 copy-done.1
  231.8 5.2 %block_result.1 = (bf16[4,128,1536]{2,1,0:T(8,128)(2,1)}, bf16[64,768]{1,0:T(8,128)(2,1)}) custom-call(s32[4]{0:T(128)} %variant.7, f32[4,128,1536]{2,1,0:T(8,128)} %get-tuple-element.77.mid_ref, bf16[4,128,1664]{2,1,0:T(8,128)(2,1)} %bitcast.12, bf16[4,128,1664]{2,1,0:T(8,128)(2,1)} %bitcast.15, bf16[4,128,1536]{2,1,0:T(8,128)(2,1)} %cot_ref.3, ...), custom_call_target="tpu_custom_call" | custom-call | flops 50331648 | bytes 9437184 | tf_op jit(solution)/shard_map/block_result/pallas_call | solution.py:414
  237.0 63.9 %finish.1 = (bf16[4,128,1536]{2,1,0:T(8,128)(2,1)}, f32[8,14336]{1,0:T(8,128)}, f32[8,4096]{1,0:T(8,128)}, f32[8,3072]{1,0:T(8,128)}, f32[8,2304]{1,0:T(8,128)}) custom-call(bf16[4,768,128]{2,1,0:T(8,128)(2,1)} %bitcast.17, bf16[16,1,128,128]{3,2,1,0:T(8,128)(2,1)} %bitcast.21, f32[4,1024,128]{2,1,0:T(8,128)} %get-tuple-element.100.refs_2_, ...), custom_call_target="tpu_custom_call" | custom-call | tf_op jit(solution)/shard_map/finish/pallas_call | solution.py:1143
  300.9 2.0 unpack.1
  303.0 2.7 copy.46
  (2 shorter events, 0.0 us)
Async XLA Ops:
  0.6 80.4 %collective-permute-start = (bf16[768,1536]{1,0:T(8,128)(2,1)}, bf16[768,1536]{1,0:T(8,128)(2,1)S(1)}, u32[]{:S(2)}, u32[]{:S(2)}) collective-permute-start(bf16[768,1536]{1,0:T(8,128)(2,1)} %wo.3), channel_id=1, source_target_pairs={{0,1},{1,0},{2,3},{3,2},{4,5},{5,4},{6,7},{7,6},{8,9},{9,8},{10,11... | collective-permute-start | bytes 7077896 | tf_op jit(solution)/shard_map/ppermute | solution.py:1202
  3.6 77.3 %collective-permute-start.1 = (bf16[128,768]{1,0:T(8,128)(2,1)}, bf16[128,768]{1,0:T(8,128)(2,1)S(1)}, u32[]{:S(2)}, u32[]{:S(2)}) collective-permute-start(bf16[128,768]{1,0:T(8,128)(2,1)} %ao.3), channel_id=1, source_target_pairs={{0,1},{1,0},{2,3},{3,2},{4,5},{5,4},{6,7},{7,6},{8,9},{9,8},{10,11... | collective-permute-start | bytes 589832 | tf_op jit(solution)/shard_map/ppermute | solution.py:1202
  81.0 0.7 copy-start.3
  81.0 1.5 copy-start.2
  162.4 11.7 %copy-start = (bf16[512,1664]{1,0:T(8,128)(2,1)S(1)}, bf16[512,1664]{1,0:T(8,128)(2,1)}, u32[]{:S(2)}) copy-start(bf16[512,1664]{1,0:T(8,128)(2,1)} %get-tuple-element.90) | copy-start | bytes 5111812
  174.1 56.5 %collective-permute-start.2 = (bf16[512,1664]{1,0:T(8,128)(2,1)S(1)}, bf16[512,1664]{1,0:T(8,128)(2,1)S(1)}, u32[]{:S(2)}, u32[]{:S(2)}) collective-permute-start(bf16[512,1664]{1,0:T(8,128)(2,1)S(1)} %copy-done), channel_id=1, source_target_pairs={{0,1},{1,0},{2,3},{3,2},{4,5},{5,4},{6,7},{7,6},{8,9},{9,8},{10,11... | collective-permute-start | bytes 5111816 | tf_op jit(solution)/shard_map/ppermute | solution.py:1202
  230.6 1.2 copy-start.1
